TPU v7x, 128 devices: a whole 4x4x4 slice. The times are simulated.
128 devices in a mesh: site: 2 (over core), blk: 64 (over y, x, z).
Axes of the slice: x: 4, y: 4, z: 4, core: 2. Of those that a mesh axis runs over, the one named last changes fastest.
Arguments:
- env_in: float32 [3, 128, 512, 512], P(None, 'blk'), may hold values from -6 to 6
- site_tensor: float32 [2, 128, 3, 512, 512], P('site', 'blk'), may hold values from -0.25 to 0.25
- pair_live: int32 [2, 128, 3], P('site', 'blk'), may hold values 0 or 1
- coef_index: int32 [2, 128, 3], P('site', 'blk'), may hold values from 0 to 3
- mpo_coef: float32 [2, 4], P('site'), may hold values from 0.5 to 1.5
Outputs:
- env_out: float32 [2, 3, 128, 512, 512], P('site', None, 'blk')
All inputs are finite; a program needn't handle non-finite values. No bound on the sum of `pair_live` on one device may be relied on, other than what follows from the above.
Results may differ from a plain program's by a relative error of at most 0.00014.
Values sent between devices are 32-bit elements; how exact they have to be, the bound alone decides.
No kernel may reach another device: no remote copies, remote signals or barrier semaphores. Data moves between devices by JAX's collectives and lax.ppermute only.
A program may use at most 128 MiB of HBM per device.

v0:
```python
import functools

import jax
import jax.numpy as jnp
from jax import lax
from jax.experimental import pallas as pl
from jax.experimental.pallas import tpu as pltpu
from jax.sharding import PartitionSpec as P

F32 = jnp.float32
BF16 = jnp.bfloat16
LIMIT = 28 << 20

STORE = 6
CUTS = 2


def split(x):
    high = x.astype(BF16)
    return high, (x - high.astype(F32)).astype(BF16)


def dot_nn(a, b):
    return jnp.dot(a, b, preferred_element_type=F32)


def dot_nt(a, b):
    return lax.dot_general(a, b, (((1,), (1,)), ((), ())), preferred_element_type=F32)


def sandwich(block, high, low):
    block_high, block_low = split(block)
    inner = dot_nt(block_high, high) + dot_nt(block_high, low) + dot_nt(block_low, high)
    inner_high, inner_low = split(inner)
    return dot_nn(high, inner_high) + dot_nn(low, inner_high) + dot_nn(high, inner_low)


def cost():
    return pl.CostEstimate(flops=0, bytes_accessed=1024, transcendentals=0)


def params():
    return pltpu.CompilerParams(vmem_limit_bytes=LIMIT)


def root(live_ref, index_ref, coef_ref, sector, slot, width):
    weight = live_ref[0, sector, slot].astype(F32) * coef_ref[0, index_ref[0, sector, slot]]
    return jnp.sqrt(jnp.full((1, width), weight, F32))


def slot_at(k, c):
    return jnp.where(k == 0, 1, jnp.where(k == 1, 2 - 2 * c, 2 * c))


SCALARS = [pl.BlockSpec(memory_space=pltpu.SMEM)] * 3
HBM_REF = pl.BlockSpec(memory_space=pl.ANY)


def edge(core, env, first, count):
    width = env.shape[-1]
    parts = 4
    rows = width // parts

    def kernel(core_ref, e_ref, o_ref, sems):
        copies = []
        for n in range(count):
            for p in range(parts):
                span = pl.ds(p * rows, rows)
                copies.append(pltpu.make_async_copy(e_ref.at[first + n, core_ref[0], span], o_ref.at[n, span], sems.at[n * parts + p]))
        for copy in copies:
            copy.start()
        for copy in copies:
            copy.wait()

    return pl.pallas_call(
        kernel,
        grid_spec=pltpu.PrefetchScalarGridSpec(
            num_scalar_prefetch=1,
            grid=(1,),
            in_specs=[HBM_REF],
            out_specs=pl.BlockSpec(memory_space=pltpu.VMEM),
            scratch_shapes=[pltpu.SemaphoreType.DMA((count * parts,))],
        ),
        out_shape=jax.ShapeDtypeStruct((count, width, width), F32),
        compiler_params=params(),
        cost_estimate=cost(),
        name=f"edge_{first}",
    )(core, env)


def outgoing(core, scalars, tensors, after):
    width = tensors.shape[-1]

    def kernel(core_ref, live_ref, index_ref, coef_ref, t_ref, after_ref, *o_refs):
        other = 1 - core_ref[0]
        for k, o_ref in enumerate(o_refs):
            slot = slot_at(k, other)
            o_ref[...] = t_ref[0, 0, slot] * root(live_ref, index_ref, coef_ref, other, slot, width)

    return pl.pallas_call(
        kernel,
        grid_spec=pltpu.PrefetchScalarGridSpec(
            num_scalar_prefetch=1,
            grid=(1,),
            in_specs=SCALARS + [pl.BlockSpec((1, 1, 3, width, width), lambda k, c: (0, 1 - c[0], 0, 0, 0)), HBM_REF],
            out_specs=[pl.BlockSpec((width, width), lambda k, c: (0, 0))] * 3,
        ),
        out_shape=[jax.ShapeDtypeStruct((width, width), F32)] * 3,
        compiler_params=params(),
        cost_estimate=cost(),
        name="outgoing",
    )(core, *scalars, tensors, after)


def own_store(core, scalars, tensors, after):
    width = tensors.shape[-1]

    def kernel(core_ref, live_ref, index_ref, coef_ref, t_ref, after_ref, o_ref):
        c = core_ref[0]
        slot = slot_at(pl.program_id(0), c)
        high, low = split((t_ref[0, 0, 0] * root(live_ref, index_ref, coef_ref, c, slot, width)).T)
        o_ref[0, 0] = high
        o_ref[0, 1] = low

    return pl.pallas_call(
        kernel,
        grid_spec=pltpu.PrefetchScalarGridSpec(
            num_scalar_prefetch=1,
            grid=(3,),
            in_specs=SCALARS + [pl.BlockSpec((1, 1, 1, width, width), lambda k, c: (0, c[0], slot_at(k, c[0]), 0, 0)), HBM_REF],
            out_specs=pl.BlockSpec((1, 2, width, width), lambda k, c: (k, 0, 0, 0)),
        ),
        out_shape=jax.ShapeDtypeStruct((STORE, 2, width, width), BF16),
        compiler_params=params(),
        cost_estimate=cost(),
        name="own_store",
    )(core, *scalars, tensors, after)


def full_store(store, received):
    width = store.shape[-1]

    def kernel(*refs):
        o_ref = refs[-1]
        for k in range(3):

            @pl.when(pl.program_id(0) == k)
            def _():
                high, low = split(refs[k][...].T)
                o_ref[0, 0] = high
                o_ref[0, 1] = low

    return pl.pallas_call(
        kernel,
        grid=(3,),
        in_specs=[pl.BlockSpec((width, width), lambda k: (0, 0))] * 3 + [HBM_REF],
        out_specs=pl.BlockSpec((1, 2, width, width), lambda k: (k + 3, 0, 0, 0)),
        out_shape=jax.ShapeDtypeStruct(store.shape, BF16),
        input_output_aliases={3: 0},
        compiler_params=params(),
        cost_estimate=cost(),
        name="full_store",
    )(*received, store)


def near_terms(core, site, own, other, in_env, store, after):
    states, width = own.shape[0], own.shape[-1]

    def kernel(core_ref, a_ref, b_ref, ta_ref, tb_ref, *refs):
        o_ref = refs[-1]
        a, b = (a_ref[0, 0], b_ref[0, 0]) if in_env else (a_ref[0], b_ref[0])
        o_ref[0] = sandwich(a, ta_ref[0, 0], ta_ref[0, 1]) + sandwich(b, tb_ref[0, 0], tb_ref[0, 1])

    def slot(k):
        return lambda n, c: ((3 * c[0] if site == 0 else 3 - 3 * c[0]) + k, 0, 0, 0)

    row = pl.BlockSpec((1, width, width), lambda n, c: (n, 0, 0))
    sources = [row, row]
    if in_env:
        block = (1, 1, width, width)
        sources = [pl.BlockSpec(block, lambda n, c: (n, c[0], 0, 0)), pl.BlockSpec(block, lambda n, c: (n, 1 - c[0], 0, 0))]
    pair = (1, 2, width, width)
    return pl.pallas_call(
        kernel,
        grid_spec=pltpu.PrefetchScalarGridSpec(
            num_scalar_prefetch=1,
            grid=(states,),
            in_specs=sources + [pl.BlockSpec(pair, slot(0)), pl.BlockSpec(pair, slot(1))] + [HBM_REF] * len(after),
            out_specs=row,
        ),
        out_shape=jax.ShapeDtypeStruct((states, width, width), F32),
        compiler_params=params(),
        cost_estimate=cost(),
        name=f"near_terms_{site}",
    )(core, own, other, store, store, *after)


def far_term(core, site, partial, row, halo, halo_row, store, after):
    width = halo.shape[-1]

    def kernel(core_ref, p_ref, h_ref, t_ref, *refs):
        refs[-1][...] = p_ref[...] + sandwich(h_ref[0], t_ref[0, 0], t_ref[0, 1])[None]

    return pl.pallas_call(
        kernel,
        grid_spec=pltpu.PrefetchScalarGridSpec(
            num_scalar_prefetch=1,
            grid=(1,),
            in_specs=[
                pl.BlockSpec((1, width, width), lambda n, c: (row, 0, 0)),
                pl.BlockSpec((1, width, width), lambda n, c: (halo_row, 0, 0)),
                pl.BlockSpec((1, 2, width, width), lambda n, c: ((3 * c[0] if site == 0 else 3 - 3 * c[0]) + 2, 0, 0, 0)),
            ]
            + [HBM_REF] * len(after),
            out_specs=pl.BlockSpec((1, width, width), lambda n, c: (0, 0, 0)),
        ),
        out_shape=jax.ShapeDtypeStruct((1, width, width), F32),
        compiler_params=params(),
        cost_estimate=cost(),
        name=f"far_term_{site}",
    )(core, partial, halo, store, *after)


def write_rows(core, out, shape, moves, sources, name):
    width = shape[-1]
    count = len(sources)

    def kernel(core_ref, *refs):
        o_ref, sems = refs[count + len(old)], refs[-1]
        if not old:
            refs[count + 1][...] = jnp.zeros((8, 128), F32)
        for c in range(2):

            @pl.when(core_ref[0] == c)
            def _():
                copies = [
                    pltpu.make_async_copy(refs[i].at[0], o_ref.at[state, sector], sems.at[m])
                    for m, (i, state, sector) in enumerate(moves[c])
                ]
                for copy in copies:
                    copy.start()
                for copy in copies:
                    copy.wait()

    old = [] if out is None else [out]
    outs = [jax.ShapeDtypeStruct(shape, F32)]
    if not old:
        outs.append(jax.ShapeDtypeStruct((8, 128), F32))
    return pl.pallas_call(
        kernel,
        grid_spec=pltpu.PrefetchScalarGridSpec(
            num_scalar_prefetch=1,
            grid=(1,),
            in_specs=[pl.BlockSpec(memory_space=pltpu.VMEM)] * count + [HBM_REF] * len(old),
            out_specs=[HBM_REF, pl.BlockSpec(memory_space=pltpu.VMEM)][: len(outs)],
            scratch_shapes=[pltpu.SemaphoreType.DMA((6,))],
        ),
        out_shape=outs,
        input_output_aliases={count + 1: 0} if old else {},
        compiler_params=params(),
        cost_estimate=cost(),
        name=name,
    )(core, *sources, *old)


def shards(chips, env_in, site_tensor, pair_live, coef_index, mpo_coef):
    axes = ("site", "blk")
    core = jnp.reshape(lax.axis_index("site"), (1,)).astype(jnp.int32)
    swap = [(s * chips + j, (1 - s) * chips + j) for s in range(2) for j in range(chips)]
    meet = [(chips + j, j + 1) for j in range(chips - 1)] + [(j + 1, chips + j) for j in range(chips - 1)]
    down = [(j, chips + j) for j in range(chips)]

    def send(value, pairs):
        return lax.ppermute(value, axes, pairs)

    scalars = (pair_live, coef_index, mpo_coef)
    pinned = pltpu.with_memory_space_constraint(env_in, pltpu.HBM)
    edge_a = edge(core, pinned, 0, CUTS)
    halo_a = send(edge_a, meet)
    leaving = outgoing(core, scalars, site_tensor, edge_a)
    received = [send(block, swap) for block in leaving]
    store = own_store(core, scalars, site_tensor, leaving[0])
    edge_b = edge(core, pinned, CUTS, 3 - CUTS)
    halo_b = send(edge_b, meet)
    store = full_store(store, received)

    near = near_terms(core, 0, env_in, env_in, True, store, [])
    first, crossed, halos = [], [], []
    for n in range(3):
        halo, row = (halo_a, n) if n < CUTS else (halo_b, n - CUTS)
        first.append(far_term(core, 0, near, n, halo, row, store, first[-1:]))
        halos.append(send(first[n], meet))
        crossed.append(send(first[n], swap))

    second, moved, token, sums = [], [], [], []
    for n in range(3):
        if n == 2:
            early = [(0, 0, 0), (1, 0, 1), (2, 1, 0), (3, 1, 1)], [(4, 0, 1), (5, 1, 1)]
            out, mark = write_rows(core, None, env_in.shape, early, [first[0], crossed[0], first[1], crossed[1], second[0], second[1]], "early_rows")
            token = [mark]
        sums.append(near_terms(core, 1, first[n], crossed[n], False, store, sums[-1:]))
        second.append(far_term(core, 1, sums[n], 0, halos[n], 0, store, token))
        moved.append(send(second[n], down))
    late = [(0, 2, 0), (1, 2, 1)], [(2, 0, 0), (3, 1, 0), (4, 2, 0), (5, 2, 1)]
    (out,) = write_rows(core, out, env_in.shape, late, [first[2], crossed[2], *moved, second[2]], "late_rows")
    return out[None]


def solution(mesh):
    return jax.shard_map(
        functools.partial(shards, mesh.shape["blk"]),
        mesh=mesh,
        in_specs=(
            P(None, "blk", None, None),
            P("site", "blk", None, None, None),
            P("site", "blk", None),
            P("site", "blk", None),
            P("site", None),
        ),
        out_specs=P("site", None, "blk", None, None),
        check_vma=False,
    )
```

profile of v0, /device:TPU:25, one launch (start us, length us, event | category | flops | bytes accessed | tf_op | source)
XLA Modules:
  0.0 92.0 jit_solution(12635131336777396289)
XLA Ops:
  0.0 1.7 %edge_0.1.after_ref = f32[2,512,512]{2,1,0:T(8,128)S(1)} custom-call(s32[1]{0:T(128)} %bitcast.core_ref, f32[3,2,512,512]{3,2,1,0:T(8,128)} %e_ref.3), custom_call_target="tpu_custom_call" | custom-call | bytes 1024 | tf_op jit(solution)/shard_map/edge_0/pallas_call | solution.py:75
  1.8 4.2 %collective-permute-start.4 = (f32[2,512,512]{2,1,0:T(8,128)S(1)}, f32[2,512,512]{2,1,0:T(8,128)S(1)}, u32[]{:S(2)}, u32[]{:S(2)}) collective-permute-start(f32[2,512,512]{2,1,0:T(8,128)S(1)} %edge_0.1.after_ref), channel_id=1, source_target_pairs={{64,1},{65,2},{66,3},{67,4},{68,5},{69,6},{70,7},{71,8},{72,9},{73... | collective-permute-start | bytes 6291464 | tf_op jit(solution)/shard_map/ppermute | solution.py:274
  6.8 4.4 %collective-permute-start = (f32[512,512]{1,0:T(8,128)S(1)}, f32[512,512]{1,0:T(8,128)S(1)}, u32[]{:S(2)}, u32[]{:S(2)}) collective-permute-start(f32[512,512]{1,0:T(8,128)S(1)} %get-tuple-element.10.after_ref), channel_id=1, source_target_pairs={{0,64},{1,65},{2,66},{3,67},{4,68},{5,69},{6,70},{7,71},{8,72},{9,... | collective-permute-start | bytes 3145736 | tf_op jit(solution)/shard_map/ppermute | solution.py:274
  11.8 1.2 %edge_2.1 = f32[1,512,512]{2,1,0:T(8,128)S(1)} custom-call(s32[1]{0:T(128)} %bitcast.core_ref, f32[3,2,512,512]{3,2,1,0:T(8,128)} %e_ref.3), custom_call_target="tpu_custom_call" | custom-call | bytes 1024 | tf_op jit(solution)/shard_map/edge_2/pallas_call | solution.py:75
  13.0 1.9 %collective-permute-start.3 = (f32[1,512,512]{2,1,0:T(8,128)S(1)}, f32[1,512,512]{2,1,0:T(8,128)S(1)}, u32[]{:S(2)}, u32[]{:S(2)}) collective-permute-start(f32[1,512,512]{2,1,0:T(8,128)S(1)} %edge_2.1), channel_id=1, source_target_pairs={{64,1},{65,2},{66,3},{67,4},{68,5},{69,6},{70,7},{71,8},{72,9},{73... | collective-permute-start | bytes 3145736 | tf_op jit(solution)/shard_map/ppermute | solution.py:274
  14.9 1.7 %own_store.1.refs_3_ = bf16[6,2,512,512]{3,2,1,0:T(8,128)(2,1)S(1)} custom-call(s32[1]{0:T(128)} %bitcast.core_ref, s32[1,2,3]{2,1,0:T(2,128)S(1)} %copy-done.1, s32[1,2,3]{2,1,0:T(2,128)S(1)} %copy-done.2, f32[1,4]{1,0:T(1,128)S(1)} %copy-done.3, f32[1,2,3,512,512]{4,3,2,1,0:T(8,128)S(1)} %copy-done, f32[512,512]{1,0:T(8,128)S(1)} %get-tuple-element.10.after_ref), custom_call_target="tpu_custom_call" | custom-call | bytes 1024 | tf_op jit(solution)/shard_map/own_store/pallas_call | solution.py:125
  16.7 1.1 %full_store.1.ta_ref.tb_ref.t_ref = bf16[6,2,512,512]{3,2,1,0:T(8,128)(2,1)S(1)} custom-call(f32[512,512]{1,0:T(8,128)S(1)} %collective-permute-done.refs_0_, f32[512,512]{1,0:T(8,128)S(1)} %collective-permute-done.1.refs_1_, f32[512,512]{1,0:T(8,128)S(1)} %collective-permute-done.2.refs_2_, ...), custom_call_target="tpu_custom_call", output_to_operand_aliasing={{}: (3, {})} | custom-call | bytes 1024 | tf_op jit(solution)/shard_map/full_store/pallas_call | solution.py:153
  18.4 10.9 %near_terms_0.1.p_ref = f32[3,512,512]{2,1,0:T(8,128)S(1)} custom-call(s32[1]{0:T(128)} %bitcast.core_ref, f32[3,2,512,512]{3,2,1,0:T(8,128)S(1)} %bitcast.3, f32[3,2,512,512]{3,2,1,0:T(8,128)S(1)} %bitcast.3, bf16[6,2,512,512]{3,2,1,0:T(8,128)(2,1)S(1)} %full_store.1.ta_ref.tb_ref.t_ref, bf16[6,2,512,512]{3,2,1,0:T(8,128)(2,1)S(1)} %full_store.1.ta_ref.tb_ref.t_ref), custom_call_target="tpu_custom_call" | custom-call | bytes 1024 | tf_op jit(solution)/shard_map/near_terms_0/pallas_call | solution.py:183
  30.0 1.9 %far_term_0.3.refs_0_.a_ref = f32[1,512,512]{2,1,0:T(8,128)S(1)} custom-call(s32[1]{0:T(128)} %bitcast.core_ref, f32[3,512,512]{2,1,0:T(8,128)S(1)} %near_terms_0.1.p_ref, f32[2,512,512]{2,1,0:T(8,128)S(1)} %collective-permute-done.4.h_ref, bf16[6,2,512,512]{3,2,1,0:T(8,128)(2,1)S(1)} %full_store.1.ta_ref.tb_ref.t_ref), custom_call_target="tpu_custom_call" | custom-call | bytes 1024 | tf_op jit(solution)/shard_map/far_term_0/pallas_call | solution.py:204
  31.9 4.2 %collective-permute-start.6 = (f32[1,512,512]{2,1,0:T(8,128)S(1)}, f32[1,512,512]{2,1,0:T(8,128)S(1)}, u32[]{:S(2)}, u32[]{:S(2)}) collective-permute-start(f32[1,512,512]{2,1,0:T(8,128)S(1)} %far_term_0.3.refs_0_.a_ref), channel_id=1, source_target_pairs={{0,64},{1,65},{2,66},{3,67},{4,68},{5,69},{6,70},{7,71},{8,72},{9,... | collective-permute-start | bytes 3145736 | tf_op jit(solution)/shard_map/ppermute | solution.py:274
  36.1 1.9 %far_term_0.4.refs_0_.a_ref.refs_2_ = f32[1,512,512]{2,1,0:T(8,128)S(1)} custom-call(s32[1]{0:T(128)} %bitcast.core_ref, f32[3,512,512]{2,1,0:T(8,128)S(1)} %near_terms_0.1.p_ref, f32[2,512,512]{2,1,0:T(8,128)S(1)} %collective-permute-done.4.h_ref, bf16[6,2,512,512]{3,2,1,0:T(8,128)(2,1)S(1)} %full_store.1.ta_ref.tb_ref.t_ref, ...), custom_call_target="tpu_custom_call" | custom-call | bytes 1024 | tf_op jit(solution)/shard_map/far_term_0/pallas_call | solution.py:204
  38.2 1.9 %collective-permute-start.7 = (f32[1,512,512]{2,1,0:T(8,128)S(1)}, f32[1,512,512]{2,1,0:T(8,128)S(1)}, u32[]{:S(2)}, u32[]{:S(2)}) collective-permute-start(f32[1,512,512]{2,1,0:T(8,128)S(1)} %far_term_0.3.refs_0_.a_ref), channel_id=1, source_target_pairs={{64,1},{65,2},{66,3},{67,4},{68,5},{69,6},{70,7},{71,8},{72,9},{73... | collective-permute-start | bytes 3145736 | tf_op jit(solution)/shard_map/ppermute | solution.py:274
  40.1 3.6 %collective-permute-start.10 = (f32[1,512,512]{2,1,0:T(8,128)S(1)}, f32[1,512,512]{2,1,0:T(8,128)S(1)}, u32[]{:S(2)}, u32[]{:S(2)}) collective-permute-start(f32[1,512,512]{2,1,0:T(8,128)S(1)} %far_term_0.4.refs_0_.a_ref.refs_2_), channel_id=1, source_target_pairs={{64,1},{65,2},{66,3},{67,4},{68,5},{69,6},{70,7},{71,8},{72,9},{73... | collective-permute-start | bytes 3145736 | tf_op jit(solution)/shard_map/ppermute | solution.py:274
  43.7 1.9 %far_term_0.5.a_ref.refs_0_ = f32[1,512,512]{2,1,0:T(8,128)S(1)} custom-call(s32[1]{0:T(128)} %bitcast.core_ref, f32[3,512,512]{2,1,0:T(8,128)S(1)} %near_terms_0.1.p_ref, f32[1,512,512]{2,1,0:T(8,128)S(1)} %collective-permute-done.3.h_ref, bf16[6,2,512,512]{3,2,1,0:T(8,128)(2,1)S(1)} %full_store.1.ta_ref.tb_ref.t_ref, ...), custom_call_target="tpu_custom_call" | custom-call | bytes 1024 | tf_op jit(solution)/shard_map/far_term_0/pallas_call | solution.py:204
  45.7 4.8 %collective-permute-start.5 = (f32[1,512,512]{2,1,0:T(8,128)S(1)}, f32[1,512,512]{2,1,0:T(8,128)S(1)}, u32[]{:S(2)}, u32[]{:S(2)}) collective-permute-start(f32[1,512,512]{2,1,0:T(8,128)S(1)} %far_term_0.5.a_ref.refs_0_), channel_id=1, source_target_pairs={{0,64},{1,65},{2,66},{3,67},{4,68},{5,69},{6,70},{7,71},{8,72},{9,... | collective-permute-start | bytes 3145736 | tf_op jit(solution)/shard_map/ppermute | solution.py:274
  50.4 2.1 %collective-permute-start.12 = (f32[1,512,512]{2,1,0:T(8,128)S(1)}, f32[1,512,512]{2,1,0:T(8,128)S(1)}, u32[]{:S(2)}, u32[]{:S(2)}) collective-permute-start(f32[1,512,512]{2,1,0:T(8,128)S(1)} %far_term_0.5.a_ref.refs_0_), channel_id=1, source_target_pairs={{64,1},{65,2},{66,3},{67,4},{68,5},{69,6},{70,7},{71,8},{72,9},{73... | collective-permute-start | bytes 3145736 | tf_op jit(solution)/shard_map/ppermute | solution.py:274
  52.5 3.6 %near_terms_1.3.p_ref.refs_0_ = f32[1,512,512]{2,1,0:T(8,128)S(1)} custom-call(s32[1]{0:T(128)} %bitcast.core_ref, f32[1,512,512]{2,1,0:T(8,128)S(1)} %far_term_0.3.refs_0_.a_ref, f32[1,512,512]{2,1,0:T(8,128)S(1)} %collective-permute-done.6.b_ref.refs_1_, bf16[6,2,512,512]{3,2,1,0:T(8,128)(2,1)S(1)} %full_store.1.ta_ref.tb_ref.t_ref, ...), custom_call_target="tpu_custom_call" | custom-call | bytes 1024 | tf_op jit(solution)/shard_map/near_terms_1/pallas_call | solution.py:183
  56.2 3.6 %near_terms_1.4.p_ref.refs_0_ = f32[1,512,512]{2,1,0:T(8,128)S(1)} custom-call(s32[1]{0:T(128)} %bitcast.core_ref, f32[1,512,512]{2,1,0:T(8,128)S(1)} %far_term_0.4.refs_0_.a_ref.refs_2_, f32[1,512,512]{2,1,0:T(8,128)S(1)} %collective-permute-done.9.b_ref.refs_3_, bf16[6,2,512,512]{3,2,1,0:T(8,128)(2,1)S(1)} %full_store.1.ta_ref.tb_ref.t_ref, ...), custom_call_target="tpu_custom_call" | custom-call | bytes 1024 | tf_op jit(solution)/shard_map/near_terms_1/pallas_call | solution.py:183
  59.8 1.9 %far_term_1.3.refs_4_ = f32[1,512,512]{2,1,0:T(8,128)S(1)} custom-call(s32[1]{0:T(128)} %bitcast.core_ref, f32[1,512,512]{2,1,0:T(8,128)S(1)} %near_terms_1.3.p_ref.refs_0_, f32[1,512,512]{2,1,0:T(8,128)S(1)} %collective-permute-done.7.h_ref, bf16[6,2,512,512]{3,2,1,0:T(8,128)(2,1)S(1)} %full_store.1.ta_ref.tb_ref.t_ref), custom_call_target="tpu_custom_call" | custom-call | bytes 1024 | tf_op jit(solution)/shard_map/far_term_1/pallas_call | solution.py:204
  61.7 4.1 %collective-permute-done.10.h_ref = f32[1,512,512]{2,1,0:T(8,128)S(1)} collective-permute-done((f32[1,512,512]{2,1,0:T(8,128)S(1)}, f32[1,512,512]{2,1,0:T(8,128)S(1)}, u32[]{:S(2)}, u32[]{:S(2)}) %collective-permute-start.10) | collective-permute-done | bytes 1048608 | tf_op jit(solution)/shard_map/ppermute | solution.py:274
  65.8 1.9 %far_term_1.4.refs_5_ = f32[1,512,512]{2,1,0:T(8,128)S(1)} custom-call(s32[1]{0:T(128)} %bitcast.core_ref, f32[1,512,512]{2,1,0:T(8,128)S(1)} %near_terms_1.4.p_ref.refs_0_, f32[1,512,512]{2,1,0:T(8,128)S(1)} %collective-permute-done.10.h_ref, bf16[6,2,512,512]{3,2,1,0:T(8,128)(2,1)S(1)} %full_store.1.ta_ref.tb_ref.t_ref), custom_call_target="tpu_custom_call" | custom-call | bytes 1024 | tf_op jit(solution)/shard_map/far_term_1/pallas_call | solution.py:204
  67.7 3.6 %near_terms_1.5.p_ref = f32[1,512,512]{2,1,0:T(8,128)S(1)} custom-call(s32[1]{0:T(128)} %bitcast.core_ref, f32[1,512,512]{2,1,0:T(8,128)S(1)} %far_term_0.5.a_ref.refs_0_, f32[1,512,512]{2,1,0:T(8,128)S(1)} %collective-permute-done.5.b_ref.refs_1_, bf16[6,2,512,512]{3,2,1,0:T(8,128)(2,1)S(1)} %full_store.1.ta_ref.tb_ref.t_ref, ...), custom_call_target="tpu_custom_call" | custom-call | bytes 1024 | tf_op jit(solution)/shard_map/near_terms_1/pallas_call | solution.py:183
  71.4 1.4 %early_rows.1 = (f32[3,2,512,512]{3,2,1,0:T(8,128)}, f32[8,128]{1,0:T(8,128)S(1)}) custom-call(s32[1]{0:T(128)} %bitcast.core_ref, f32[1,512,512]{2,1,0:T(8,128)S(1)} %far_term_0.3.refs_0_.a_ref, f32[1,512,512]{2,1,0:T(8,128)S(1)} %collective-permute-done.6.b_ref.refs_1_, f32[1,512,512]{2,1,0:T(8,128)S(1)} %far_term_0.4.refs_0_.a_ref.refs_2_, ...), custom_call_target="tpu_custom_call" | custom-call | bytes 1024 | tf_op jit(solution)/shard_map/early_rows/pallas_call | solution.py:249
  72.7 4.3 %collective-permute-done.12.h_ref = f32[1,512,512]{2,1,0:T(8,128)S(1)} collective-permute-done((f32[1,512,512]{2,1,0:T(8,128)S(1)}, f32[1,512,512]{2,1,0:T(8,128)S(1)}, u32[]{:S(2)}, u32[]{:S(2)}) %collective-permute-start.12) | collective-permute-done | bytes 1048608 | tf_op jit(solution)/shard_map/ppermute | solution.py:274
  77.0 1.9 %far_term_1.5.refs_5_ = f32[1,512,512]{2,1,0:T(8,128)S(1)} custom-call(s32[1]{0:T(128)} %bitcast.core_ref, f32[1,512,512]{2,1,0:T(8,128)S(1)} %near_terms_1.5.p_ref, f32[1,512,512]{2,1,0:T(8,128)S(1)} %collective-permute-done.12.h_ref, bf16[6,2,512,512]{3,2,1,0:T(8,128)(2,1)S(1)} %full_store.1.ta_ref.tb_ref.t_ref, f32[8,128]{1,0:T(8,128)S(1)} %get-tuple-element.13.refs_0_), custom_call_target="tpu_custom_call" | custom-call | bytes 1024 | tf_op jit(solution)/shard_map/far_term_1/pallas_call | solution.py:204
  78.9 1.3 %collective-permute-start.13 = (f32[1,512,512]{2,1,0:T(8,128)S(1)}, f32[1,512,512]{2,1,0:T(8,128)S(1)}, u32[]{:S(2)}, u32[]{:S(2)}) collective-permute-start(f32[1,512,512]{2,1,0:T(8,128)S(1)} %far_term_1.5.refs_5_), channel_id=1, source_target_pairs={{0,64},{1,65},{2,66},{3,67},{4,68},{5,69},{6,70},{7,71},{8,72},{9,... | collective-permute-start | bytes 3145736 | tf_op jit(solution)/shard_map/ppermute | solution.py:274
  80.2 1.3 %collective-permute-start.11 = (f32[1,512,512]{2,1,0:T(8,128)S(1)}, f32[1,512,512]{2,1,0:T(8,128)S(1)}, u32[]{:S(2)}, u32[]{:S(2)}) collective-permute-start(f32[1,512,512]{2,1,0:T(8,128)S(1)} %far_term_1.4.refs_5_), channel_id=1, source_target_pairs={{0,64},{1,65},{2,66},{3,67},{4,68},{5,69},{6,70},{7,71},{8,72},{9,... | collective-permute-start | bytes 3145736 | tf_op jit(solution)/shard_map/ppermute | solution.py:274
  81.5 1.3 %collective-permute-start.8 = (f32[1,512,512]{2,1,0:T(8,128)S(1)}, f32[1,512,512]{2,1,0:T(8,128)S(1)}, u32[]{:S(2)}, u32[]{:S(2)}) collective-permute-start(f32[1,512,512]{2,1,0:T(8,128)S(1)} %far_term_1.3.refs_4_), channel_id=1, source_target_pairs={{0,64},{1,65},{2,66},{3,67},{4,68},{5,69},{6,70},{7,71},{8,72},{9,... | collective-permute-start | bytes 3145736 | tf_op jit(solution)/shard_map/ppermute | solution.py:274
  82.8 3.9 %collective-permute-done.13.refs_4_ = f32[1,512,512]{2,1,0:T(8,128)S(1)} collective-permute-done((f32[1,512,512]{2,1,0:T(8,128)S(1)}, f32[1,512,512]{2,1,0:T(8,128)S(1)}, u32[]{:S(2)}, u32[]{:S(2)}) %collective-permute-start.13) | collective-permute-done | bytes 1048608 | tf_op jit(solution)/shard_map/ppermute | solution.py:274
  86.8 1.5 %collective-permute-done.11.refs_3_ = f32[1,512,512]{2,1,0:T(8,128)S(1)} collective-permute-done((f32[1,512,512]{2,1,0:T(8,128)S(1)}, f32[1,512,512]{2,1,0:T(8,128)S(1)}, u32[]{:S(2)}, u32[]{:S(2)}) %collective-permute-start.11) | collective-permute-done | bytes 1048608 | tf_op jit(solution)/shard_map/ppermute | solution.py:274
  88.3 1.5 %collective-permute-done.8.refs_2_ = f32[1,512,512]{2,1,0:T(8,128)S(1)} collective-permute-done((f32[1,512,512]{2,1,0:T(8,128)S(1)}, f32[1,512,512]{2,1,0:T(8,128)S(1)}, u32[]{:S(2)}, u32[]{:S(2)}) %collective-permute-start.8) | collective-permute-done | bytes 1048608 | tf_op jit(solution)/shard_map/ppermute | solution.py:274
  89.8 2.1 %late_rows.1 = f32[3,2,512,512]{3,2,1,0:T(8,128)} custom-call(s32[1]{0:T(128)} %bitcast.core_ref, f32[1,512,512]{2,1,0:T(8,128)S(1)} %far_term_0.5.a_ref.refs_0_, f32[1,512,512]{2,1,0:T(8,128)S(1)} %collective-permute-done.5.b_ref.refs_1_, f32[1,512,512]{2,1,0:T(8,128)S(1)} %collective-permute-done.8.refs_2_, ...), custom_call_target="tpu_custom_call", output_to_operand_aliasing={{}: (7, {})} | custom-call | bytes 1024 | tf_op jit(solution)/shard_map/late_rows/pallas_call | solution.py:249
  (26 shorter events, 2.7 us)
Async XLA Ops:
  0.0 6.0 %copy-start.1 = (s32[1,2,3]{2,1,0:T(2,128)S(1)}, s32[1,2,3]{2,1,0:T(2,128)}, u32[]{:S(2)}) copy-start(s32[1,2,3]{2,1,0:T(2,128)} %live_ref.3) | copy-start | bytes 76
  0.0 6.0 %copy-start.2 = (s32[1,2,3]{2,1,0:T(2,128)S(1)}, s32[1,2,3]{2,1,0:T(2,128)}, u32[]{:S(2)}) copy-start(s32[1,2,3]{2,1,0:T(2,128)} %index_ref.3) | copy-start | bytes 76
  0.0 6.0 %copy-start.3 = (f32[1,4]{1,0:T(1,128)S(1)}, f32[1,4]{1,0:T(1,128)}, u32[]{:S(2)}) copy-start(f32[1,4]{1,0:T(1,128)} %coef_ref.3) | copy-start | bytes 52
  0.0 6.0 %copy-start = (f32[1,2,3,512,512]{4,3,2,1,0:T(8,128)S(1)}, f32[1,2,3,512,512]{4,3,2,1,0:T(8,128)}, u32[]{:S(2)}) copy-start(f32[1,2,3,512,512]{4,3,2,1,0:T(8,128)} %t_ref.3) | copy-start | bytes 18874372
  1.8 28.2 %collective-permute-start.4 = (f32[2,512,512]{2,1,0:T(8,128)S(1)}, f32[2,512,512]{2,1,0:T(8,128)S(1)}, u32[]{:S(2)}, u32[]{:S(2)}) collective-permute-start(f32[2,512,512]{2,1,0:T(8,128)S(1)} %edge_0.1.after_ref), channel_id=1, source_target_pairs={{64,1},{65,2},{66,3},{67,4},{68,5},{69,6},{70,7},{71,8},{72,9},{73... | collective-permute-start | bytes 6291464 | tf_op jit(solution)/shard_map/ppermute | solution.py:274
  6.8 9.9 %collective-permute-start = (f32[512,512]{1,0:T(8,128)S(1)}, f32[512,512]{1,0:T(8,128)S(1)}, u32[]{:S(2)}, u32[]{:S(2)}) collective-permute-start(f32[512,512]{1,0:T(8,128)S(1)} %get-tuple-element.10.after_ref), channel_id=1, source_target_pairs={{0,64},{1,65},{2,66},{3,67},{4,68},{5,69},{6,70},{7,71},{8,72},{9,... | collective-permute-start | bytes 3145736 | tf_op jit(solution)/shard_map/ppermute | solution.py:274
  11.2 5.5 %collective-permute-start.1 = (f32[512,512]{1,0:T(8,128)S(1)}, f32[512,512]{1,0:T(8,128)S(1)}, u32[]{:S(2)}, u32[]{:S(2)}) collective-permute-start(f32[512,512]{1,0:T(8,128)S(1)} %get-tuple-element.11), channel_id=1, source_target_pairs={{0,64},{1,65},{2,66},{3,67},{4,68},{5,69},{6,70},{7,71},{8,72},{9,... | collective-permute-start | bytes 3145736 | tf_op jit(solution)/shard_map/ppermute | solution.py:274
  11.3 5.4 %collective-permute-start.2 = (f32[512,512]{1,0:T(8,128)S(1)}, f32[512,512]{1,0:T(8,128)S(1)}, u32[]{:S(2)}, u32[]{:S(2)}) collective-permute-start(f32[512,512]{1,0:T(8,128)S(1)} %get-tuple-element.12), channel_id=1, source_target_pairs={{0,64},{1,65},{2,66},{3,67},{4,68},{5,69},{6,70},{7,71},{8,72},{9,... | collective-permute-start | bytes 3145736 | tf_op jit(solution)/shard_map/ppermute | solution.py:274
  13.0 30.7 %collective-permute-start.3 = (f32[1,512,512]{2,1,0:T(8,128)S(1)}, f32[1,512,512]{2,1,0:T(8,128)S(1)}, u32[]{:S(2)}, u32[]{:S(2)}) collective-permute-start(f32[1,512,512]{2,1,0:T(8,128)S(1)} %edge_2.1), channel_id=1, source_target_pairs={{64,1},{65,2},{66,3},{67,4},{68,5},{69,6},{70,7},{71,8},{72,9},{73... | collective-permute-start | bytes 3145736 | tf_op jit(solution)/shard_map/ppermute | solution.py:274
  14.9 2.9 %slice-start = ((s8[6291456]{0:T(1024)(128)(4,1)}), s8[4194304]{0:T(1024)(128)(4,1)S(1)}, s32[]{:S(2)}) async-start(s8[6291456]{0:T(1024)(128)(4,1)} %bitcast.2), calls=%async_computation | async-start | bytes 8388608
  16.7 1.7 %slice-start.1 = ((s8[6291456]{0:T(1024)(128)(4,1)}), s8[2097152]{0:T(1024)(128)(4,1)S(1)}, s32[]{:S(2)}) async-start(s8[6291456]{0:T(1024)(128)(4,1)} %bitcast.2), calls=%async_computation.1 | async-start | bytes 4194304
  31.9 18.5 %collective-permute-start.6 = (f32[1,512,512]{2,1,0:T(8,128)S(1)}, f32[1,512,512]{2,1,0:T(8,128)S(1)}, u32[]{:S(2)}, u32[]{:S(2)}) collective-permute-start(f32[1,512,512]{2,1,0:T(8,128)S(1)} %far_term_0.3.refs_0_.a_ref), channel_id=1, source_target_pairs={{0,64},{1,65},{2,66},{3,67},{4,68},{5,69},{6,70},{7,71},{8,72},{9,... | collective-permute-start | bytes 3145736 | tf_op jit(solution)/shard_map/ppermute | solution.py:274
  38.1 18.1 %collective-permute-start.9 = (f32[1,512,512]{2,1,0:T(8,128)S(1)}, f32[1,512,512]{2,1,0:T(8,128)S(1)}, u32[]{:S(2)}, u32[]{:S(2)}) collective-permute-start(f32[1,512,512]{2,1,0:T(8,128)S(1)} %far_term_0.4.refs_0_.a_ref.refs_2_), channel_id=1, source_target_pairs={{0,64},{1,65},{2,66},{3,67},{4,68},{5,69},{6,70},{7,71},{8,72},{9,... | collective-permute-start | bytes 3145736 | tf_op jit(solution)/shard_map/ppermute | solution.py:274
  38.2 21.7 %collective-permute-start.7 = (f32[1,512,512]{2,1,0:T(8,128)S(1)}, f32[1,512,512]{2,1,0:T(8,128)S(1)}, u32[]{:S(2)}, u32[]{:S(2)}) collective-permute-start(f32[1,512,512]{2,1,0:T(8,128)S(1)} %far_term_0.3.refs_0_.a_ref), channel_id=1, source_target_pairs={{64,1},{65,2},{66,3},{67,4},{68,5},{69,6},{70,7},{71,8},{72,9},{73... | collective-permute-start | bytes 3145736 | tf_op jit(solution)/shard_map/ppermute | solution.py:274
  40.1 25.7 %collective-permute-start.10 = (f32[1,512,512]{2,1,0:T(8,128)S(1)}, f32[1,512,512]{2,1,0:T(8,128)S(1)}, u32[]{:S(2)}, u32[]{:S(2)}) collective-permute-start(f32[1,512,512]{2,1,0:T(8,128)S(1)} %far_term_0.4.refs_0_.a_ref.refs_2_), channel_id=1, source_target_pairs={{64,1},{65,2},{66,3},{67,4},{68,5},{69,6},{70,7},{71,8},{72,9},{73... | collective-permute-start | bytes 3145736 | tf_op jit(solution)/shard_map/ppermute | solution.py:274
  45.7 22.1 %collective-permute-start.5 = (f32[1,512,512]{2,1,0:T(8,128)S(1)}, f32[1,512,512]{2,1,0:T(8,128)S(1)}, u32[]{:S(2)}, u32[]{:S(2)}) collective-permute-start(f32[1,512,512]{2,1,0:T(8,128)S(1)} %far_term_0.5.a_ref.refs_0_), channel_id=1, source_target_pairs={{0,64},{1,65},{2,66},{3,67},{4,68},{5,69},{6,70},{7,71},{8,72},{9,... | collective-permute-start | bytes 3145736 | tf_op jit(solution)/shard_map/ppermute | solution.py:274
  50.4 26.6 %collective-permute-start.12 = (f32[1,512,512]{2,1,0:T(8,128)S(1)}, f32[1,512,512]{2,1,0:T(8,128)S(1)}, u32[]{:S(2)}, u32[]{:S(2)}) collective-permute-start(f32[1,512,512]{2,1,0:T(8,128)S(1)} %far_term_0.5.a_ref.refs_0_), channel_id=1, source_target_pairs={{64,1},{65,2},{66,3},{67,4},{68,5},{69,6},{70,7},{71,8},{72,9},{73... | collective-permute-start | bytes 3145736 | tf_op jit(solution)/shard_map/ppermute | solution.py:274
  78.9 7.8 %collective-permute-start.13 = (f32[1,512,512]{2,1,0:T(8,128)S(1)}, f32[1,512,512]{2,1,0:T(8,128)S(1)}, u32[]{:S(2)}, u32[]{:S(2)}) collective-permute-start(f32[1,512,512]{2,1,0:T(8,128)S(1)} %far_term_1.5.refs_5_), channel_id=1, source_target_pairs={{0,64},{1,65},{2,66},{3,67},{4,68},{5,69},{6,70},{7,71},{8,72},{9,... | collective-permute-start | bytes 3145736 | tf_op jit(solution)/shard_map/ppermute | solution.py:274
  80.2 8.0 %collective-permute-start.11 = (f32[1,512,512]{2,1,0:T(8,128)S(1)}, f32[1,512,512]{2,1,0:T(8,128)S(1)}, u32[]{:S(2)}, u32[]{:S(2)}) collective-permute-start(f32[1,512,512]{2,1,0:T(8,128)S(1)} %far_term_1.4.refs_5_), channel_id=1, source_target_pairs={{0,64},{1,65},{2,66},{3,67},{4,68},{5,69},{6,70},{7,71},{8,72},{9,... | collective-permute-start | bytes 3145736 | tf_op jit(solution)/shard_map/ppermute | solution.py:274
  81.5 8.2 %collective-permute-start.8 = (f32[1,512,512]{2,1,0:T(8,128)S(1)}, f32[1,512,512]{2,1,0:T(8,128)S(1)}, u32[]{:S(2)}, u32[]{:S(2)}) collective-permute-start(f32[1,512,512]{2,1,0:T(8,128)S(1)} %far_term_1.3.refs_4_), channel_id=1, source_target_pairs={{0,64},{1,65},{2,66},{3,67},{4,68},{5,69},{6,70},{7,71},{8,72},{9,... | collective-permute-start | bytes 3145736 | tf_op jit(solution)/shard_map/ppermute | solution.py:274
where the time goes:
time: 92.7 us; the launch traced here: 92 us
  Pallas kernels  43.2 us (47%)
  starting transfers between devices  31.7 us (34%)
  waiting for transfers between devices  16 us (17%)
    ppermute x14, starting transfers between devices, send(): return lax.ppermute(value, axes, pairs)  31.7 us
    pallas_call x4, Pallas kernels, near_terms(): pl.pallas_call(kernel, grid_spec=pltpu.PrefetchScalarGridSpec(num_scalar_...  21.7 us
    ppermute x14, waiting for transfers between devices, send(): return lax.ppermute(value, axes, pairs)  16 us
    pallas_call x6, Pallas kernels, far_term(): pl.pallas_call(kernel, grid_spec=pltpu.PrefetchScalarGridSpec(num_scalar_...  11.5 us
    pallas_call x2, Pallas kernels, write_rows(): pl.pallas_call(kernel, grid_spec=pltpu.PrefetchScalarGridSpec(num_scalar_...  3.44 us
    pallas_call x2, Pallas kernels, edge(): pl.pallas_call(kernel, grid_spec=pltpu.PrefetchScalarGridSpec(num_scalar_...  2.94 us
  transfers between devices with their start and end apart: 14, of which 6 were waited for; matrix products, arithmetic and copies ran while one was open for 0% of the time, Pallas kernels for 41%

commit v1 on v0

--- a/solution.py
+++ b/solution.py
@@ -13,6 +13,7 @@
 
 STORE = 6
 CUTS = 2
+PARTS = 2
 
 
 def split(x):
@@ -35,8 +36,8 @@
     return dot_nn(high, inner_high) + dot_nn(low, inner_high) + dot_nn(high, inner_low)
 
 
-def cost():
-    return pl.CostEstimate(flops=0, bytes_accessed=1024, transcendentals=0)
+def cost(weight=0.0):
+    return pl.CostEstimate(flops=int(weight * 1.15e9), bytes_accessed=1024, transcendentals=0)
 
 
 def params():
@@ -56,17 +57,17 @@
 HBM_REF = pl.BlockSpec(memory_space=pl.ANY)
 
 
-def edge(core, env, first, count):
+def edge(core, env):
     width = env.shape[-1]
     parts = 4
     rows = width // parts
 
     def kernel(core_ref, e_ref, o_ref, sems):
         copies = []
-        for n in range(count):
+        for n in range(CUTS):
             for p in range(parts):
                 span = pl.ds(p * rows, rows)
-                copies.append(pltpu.make_async_copy(e_ref.at[first + n, core_ref[0], span], o_ref.at[n, span], sems.at[n * parts + p]))
+                copies.append(pltpu.make_async_copy(e_ref.at[n, core_ref[0], span], o_ref.at[n, span], sems.at[n * parts + p]))
         for copy in copies:
             copy.start()
         for copy in copies:
@@ -79,12 +80,12 @@
             grid=(1,),
             in_specs=[HBM_REF],
             out_specs=pl.BlockSpec(memory_space=pltpu.VMEM),
-            scratch_shapes=[pltpu.SemaphoreType.DMA((count * parts,))],
-        ),
-        out_shape=jax.ShapeDtypeStruct((count, width, width), F32),
-        compiler_params=params(),
-        cost_estimate=cost(),
-        name=f"edge_{first}",
+            scratch_shapes=[pltpu.SemaphoreType.DMA((CUTS * parts,))],
+        ),
+        out_shape=jax.ShapeDtypeStruct((CUTS, width, width), F32),
+        compiler_params=params(),
+        cost_estimate=cost(),
+        name="edge",
     )(core, env)
 
 
@@ -112,29 +113,47 @@
     )(core, *scalars, tensors, after)
 
 
-def own_store(core, scalars, tensors, after):
+def own_store(core, scalars, tensors, env, after):
     width = tensors.shape[-1]
 
-    def kernel(core_ref, live_ref, index_ref, coef_ref, t_ref, after_ref, o_ref):
+    def kernel(core_ref, live_ref, index_ref, coef_ref, t_ref, e_ref, after_ref, o_ref, edge_ref, sems):
         c = core_ref[0]
         slot = slot_at(pl.program_id(0), c)
+        parts = 4
+        copies = []
+        for p in range(parts):
+            span = pl.ds(p * (width // parts), width // parts)
+            for n in range(3 - CUTS):
+                copies.append(pltpu.make_async_copy(e_ref.at[CUTS + n, c, span], edge_ref.at[n, span], sems.at[n * parts + p]))
+
+        @pl.when(pl.program_id(0) == 0)
+        def _():
+            for copy in copies:
+                copy.start()
+
         high, low = split((t_ref[0, 0, 0] * root(live_ref, index_ref, coef_ref, c, slot, width)).T)
         o_ref[0, 0] = high
         o_ref[0, 1] = low
 
+        @pl.when(pl.program_id(0) == 2)
+        def _():
+            for copy in copies:
+                copy.wait()
+
     return pl.pallas_call(
         kernel,
         grid_spec=pltpu.PrefetchScalarGridSpec(
             num_scalar_prefetch=1,
             grid=(3,),
-            in_specs=SCALARS + [pl.BlockSpec((1, 1, 1, width, width), lambda k, c: (0, c[0], slot_at(k, c[0]), 0, 0)), HBM_REF],
-            out_specs=pl.BlockSpec((1, 2, width, width), lambda k, c: (k, 0, 0, 0)),
-        ),
-        out_shape=jax.ShapeDtypeStruct((STORE, 2, width, width), BF16),
+            in_specs=SCALARS + [pl.BlockSpec((1, 1, 1, width, width), lambda k, c: (0, c[0], slot_at(k, c[0]), 0, 0)), HBM_REF, HBM_REF],
+            out_specs=[pl.BlockSpec((1, 2, width, width), lambda k, c: (k, 0, 0, 0)), pl.BlockSpec(memory_space=pltpu.VMEM)],
+            scratch_shapes=[pltpu.SemaphoreType.DMA((4 * (3 - CUTS),))],
+        ),
+        out_shape=[jax.ShapeDtypeStruct((STORE, 2, width, width), BF16), jax.ShapeDtypeStruct((3 - CUTS, width, width), F32)],
         compiler_params=params(),
         cost_estimate=cost(),
         name="own_store",
-    )(core, *scalars, tensors, after)
+    )(core, *scalars, tensors, env, after)
 
 
 def full_store(store, received):
@@ -195,54 +214,68 @@
     )(core, own, other, store, store, *after)
 
 
-def far_term(core, site, partial, row, halo, halo_row, store, after):
-    width = halo.shape[-1]
+def far_terms(core, site, partial, first, halo, store, parts, weight, after):
+    states, width = halo.shape[0], halo.shape[-1]
+    rows = width // parts
 
     def kernel(core_ref, p_ref, h_ref, t_ref, *refs):
-        refs[-1][...] = p_ref[...] + sandwich(h_ref[0], t_ref[0, 0], t_ref[0, 1])[None]
-
-    return pl.pallas_call(
-        kernel,
-        grid_spec=pltpu.PrefetchScalarGridSpec(
-            num_scalar_prefetch=1,
-            grid=(1,),
+        total = p_ref[0] + sandwich(h_ref[0], t_ref[0, 0], t_ref[0, 1])
+        for p in range(parts):
+            refs[len(after) + p][0] = total[p * rows : (p + 1) * rows]
+
+    return pl.pallas_call(
+        kernel,
+        grid_spec=pltpu.PrefetchScalarGridSpec(
+            num_scalar_prefetch=1,
+            grid=(states,),
             in_specs=[
-                pl.BlockSpec((1, width, width), lambda n, c: (row, 0, 0)),
-                pl.BlockSpec((1, width, width), lambda n, c: (halo_row, 0, 0)),
+                pl.BlockSpec((1, width, width), lambda n, c: (n + first, 0, 0)),
+                pl.BlockSpec((1, width, width), lambda n, c: (n, 0, 0)),
                 pl.BlockSpec((1, 2, width, width), lambda n, c: ((3 * c[0] if site == 0 else 3 - 3 * c[0]) + 2, 0, 0, 0)),
             ]
             + [HBM_REF] * len(after),
-            out_specs=pl.BlockSpec((1, width, width), lambda n, c: (0, 0, 0)),
-        ),
-        out_shape=jax.ShapeDtypeStruct((1, width, width), F32),
-        compiler_params=params(),
-        cost_estimate=cost(),
-        name=f"far_term_{site}",
+            out_specs=[pl.BlockSpec((1, rows, width), lambda n, c: (n, 0, 0))] * parts,
+        ),
+        out_shape=[jax.ShapeDtypeStruct((states, rows, width), F32)] * parts,
+        compiler_params=params(),
+        cost_estimate=cost(weight),
+        name=f"far_terms_{site}",
     )(core, partial, halo, store, *after)
 
 
-def write_rows(core, out, shape, moves, sources, name):
+def write_rows(core, out, shape, moves, name):
     width = shape[-1]
+    sources = [block for c in range(2) for blocks, _, _ in moves[c] for block in blocks]
     count = len(sources)
+    old = [] if out is None else [out]
 
     def kernel(core_ref, *refs):
         o_ref, sems = refs[count + len(old)], refs[-1]
         if not old:
             refs[count + 1][...] = jnp.zeros((8, 128), F32)
+        at = 0
+        plans = []
+        for c in range(2):
+            plan = []
+            for blocks, state, sector in moves[c]:
+                rows = width // len(blocks)
+                for p in range(len(blocks)):
+                    plan += [(at, n, state + n, sector, p * rows, rows) for n in range(blocks[p].shape[0])]
+                    at += 1
+            plans.append(plan)
         for c in range(2):
 
             @pl.when(core_ref[0] == c)
             def _():
                 copies = [
-                    pltpu.make_async_copy(refs[i].at[0], o_ref.at[state, sector], sems.at[m])
-                    for m, (i, state, sector) in enumerate(moves[c])
+                    pltpu.make_async_copy(refs[i].at[n], o_ref.at[state, sector, pl.ds(begin, rows)], sems.at[m])
+                    for m, (i, n, state, sector, begin, rows) in enumerate(plans[c])
                 ]
                 for copy in copies:
                     copy.start()
                 for copy in copies:
                     copy.wait()
 
-    old = [] if out is None else [out]
     outs = [jax.ShapeDtypeStruct(shape, F32)]
     if not old:
         outs.append(jax.ShapeDtypeStruct((8, 128), F32))
@@ -253,7 +286,7 @@
             grid=(1,),
             in_specs=[pl.BlockSpec(memory_space=pltpu.VMEM)] * count + [HBM_REF] * len(old),
             out_specs=[HBM_REF, pl.BlockSpec(memory_space=pltpu.VMEM)][: len(outs)],
-            scratch_shapes=[pltpu.SemaphoreType.DMA((6,))],
+            scratch_shapes=[pltpu.SemaphoreType.DMA((16,))],
         ),
         out_shape=outs,
         input_output_aliases={count + 1: 0} if old else {},
@@ -268,41 +301,37 @@
     core = jnp.reshape(lax.axis_index("site"), (1,)).astype(jnp.int32)
     swap = [(s * chips + j, (1 - s) * chips + j) for s in range(2) for j in range(chips)]
     meet = [(chips + j, j + 1) for j in range(chips - 1)] + [(j + 1, chips + j) for j in range(chips - 1)]
-    down = [(j, chips + j) for j in range(chips)]
 
     def send(value, pairs):
         return lax.ppermute(value, axes, pairs)
 
     scalars = (pair_live, coef_index, mpo_coef)
     pinned = pltpu.with_memory_space_constraint(env_in, pltpu.HBM)
-    edge_a = edge(core, pinned, 0, CUTS)
+    edge_a = edge(core, pinned)
     halo_a = send(edge_a, meet)
     leaving = outgoing(core, scalars, site_tensor, edge_a)
     received = [send(block, swap) for block in leaving]
-    store = own_store(core, scalars, site_tensor, leaving[0])
-    edge_b = edge(core, pinned, CUTS, 3 - CUTS)
+    store, edge_b = own_store(core, scalars, site_tensor, pinned, leaving[0])
     halo_b = send(edge_b, meet)
     store = full_store(store, received)
 
     near = near_terms(core, 0, env_in, env_in, True, store, [])
-    first, crossed, halos = [], [], []
-    for n in range(3):
-        halo, row = (halo_a, n) if n < CUTS else (halo_b, n - CUTS)
-        first.append(far_term(core, 0, near, n, halo, row, store, first[-1:]))
-        halos.append(send(first[n], meet))
-        crossed.append(send(first[n], swap))
-
-    second, moved, token, sums = [], [], [], []
-    for n in range(3):
-        if n == 2:
-            early = [(0, 0, 0), (1, 0, 1), (2, 1, 0), (3, 1, 1)], [(4, 0, 1), (5, 1, 1)]
-            out, mark = write_rows(core, None, env_in.shape, early, [first[0], crossed[0], first[1], crossed[1], second[0], second[1]], "early_rows")
-            token = [mark]
-        sums.append(near_terms(core, 1, first[n], crossed[n], False, store, sums[-1:]))
-        second.append(far_term(core, 1, sums[n], 0, halos[n], 0, store, token))
-        moved.append(send(second[n], down))
-    late = [(0, 2, 0), (1, 2, 1)], [(2, 0, 0), (3, 1, 0), (4, 2, 0), (5, 2, 1)]
-    (out,) = write_rows(core, out, env_in.shape, late, [first[2], crossed[2], *moved, second[2]], "late_rows")
+    first_a, = far_terms(core, 0, near, 0, halo_a, store, 1, 0, [])
+    second_halo_a, crossed_a = send(first_a, meet), send(first_a, swap)
+    first_b, = far_terms(core, 0, near, CUTS, halo_b, store, 1, 16, [first_a])
+    second_halo_b, crossed_b = send(first_b, meet), send(first_b, swap)
+
+    near_a = near_terms(core, 1, first_a, crossed_a, False, store, [])
+    near_b = near_terms(core, 1, first_b, crossed_b, False, store, [near_a])
+    second_a = far_terms(core, 1, near_a, 0, second_halo_a, store, 2 * PARTS, 0, [near_b])
+    moved_a = [send(block, swap) for block in second_a]
+    early = [([first_a], 0, 0), ([crossed_a], 0, 1)], [(moved_a, 0, 0), (second_a, 0, 1)]
+    out, mark = write_rows(core, None, env_in.shape, early, "early_rows")
+    second_b = far_terms(core, 1, near_b, 0, second_halo_b, store, PARTS, 0, [mark])
+    moved_b = [send(block, swap) for block in second_b]
+    middle = [([first_b], CUTS, 0), ([crossed_b], CUTS, 1)], [(second_b, CUTS, 1)]
+    (out,) = write_rows(core, out, env_in.shape, middle, "middle_rows")
+    (out,) = write_rows(core, out, env_in.shape, ([], [(moved_b, CUTS, 0)]), "late_rows")
     return out[None]
 
 

time: 92.7 us -> 86.6 us (0.934)
  waiting for transfers between devices: 16 us -> 12 us
  starting transfers between devices: 31.7 us -> 30.2 us
    ppermute x14 -> x15, waiting for transfers between devices: 16 us -> 12 us  [send(): return lax.ppermute(value, axes, pairs)]
    ppermute x14 -> x15, starting transfers between devices: 31.7 us -> 30.2 us  [send(): return lax.ppermute(value, axes, pairs)]
    pallas_call x2 -> x1, Pallas kernels: 2.94 us -> 1.72 us  [edge(): pl.pallas_call(kernel, grid_spec=pltpu.PrefetchScalarGridSpec(num_scalar_...]
    pallas_call x2 -> x3, Pallas kernels: 3.44 us -> 4.34 us  [write_rows(): pl.pallas_call(kernel, grid_spec=pltpu.PrefetchScalarGridSpec(num_scalar_...]
    pallas_call x6 -> x4, Pallas kernels: 11.5 us -> 11.5 us  [far_terms(): pl.pallas_call(kernel, grid_spec=pltpu.PrefetchScalarGridSpec(num_scalar_...]
    pallas_call x4 -> x3, Pallas kernels: 21.7 us -> 21.8 us  [near_terms(): pl.pallas_call(kernel, grid_spec=pltpu.PrefetchScalarGridSpec(num_scalar_...]
  transfers between devices with their start and end apart: 14 -> 15, of which waited for: 6 -> 10; matrix products, arithmetic and copies ran while one was open for 0% -> 0% of each run, Pallas kernels for 41% -> 45%
where the time goes in v1:
time: 86.6 us; the launch traced here: 86.5 us
  Pallas kernels  43.3 us (50%)
  starting transfers between devices  30.2 us (35%)
  waiting for transfers between devices  12 us (14%)
    ppermute x15, starting transfers between devices, send(): return lax.ppermute(value, axes, pairs)  30.2 us
    pallas_call x3, Pallas kernels, near_terms(): pl.pallas_call(kernel, grid_spec=pltpu.PrefetchScalarGridSpec(num_scalar_...  21.8 us
    ppermute x15, waiting for transfers between devices, send(): return lax.ppermute(value, axes, pairs)  12 us
    pallas_call x4, Pallas kernels, far_terms(): pl.pallas_call(kernel, grid_spec=pltpu.PrefetchScalarGridSpec(num_scalar_...  11.5 us
    pallas_call x3, Pallas kernels, write_rows(): pl.pallas_call(kernel, grid_spec=pltpu.PrefetchScalarGridSpec(num_scalar_...  4.34 us
    pallas_call x1, Pallas kernels, own_store(): pl.pallas_call(kernel, grid_spec=pltpu.PrefetchScalarGridSpec(num_scalar_...  2.09 us
  transfers between devices with their start and end apart: 15, of which 10 were waited for; matrix products, arithmetic and copies ran while one was open for 0% of the time, Pallas kernels for 45%

profile of v1, /device:TPU:25, one launch (start us, length us, event | category | flops | bytes accessed | tf_op | source)
XLA Modules:
  0.0 86.5 jit_solution(199150580379411736)
XLA Ops:
  0.0 1.7 %edge.1.after_ref = f32[2,512,512]{2,1,0:T(8,128)S(1)} custom-call(s32[1]{0:T(128)} %bitcast.core_ref, f32[3,2,512,512]{3,2,1,0:T(8,128)} %b_ref.1), custom_call_target="tpu_custom_call" | custom-call | bytes 1024 | tf_op jit(solution)/shard_map/edge/pallas_call | solution.py:76
  1.8 4.2 %collective-permute-start.4 = (f32[2,512,512]{2,1,0:T(8,128)S(1)}, f32[2,512,512]{2,1,0:T(8,128)S(1)}, u32[]{:S(2)}, u32[]{:S(2)}) collective-permute-start(f32[2,512,512]{2,1,0:T(8,128)S(1)} %edge.1.after_ref), channel_id=1, source_target_pairs={{64,1},{65,2},{66,3},{67,4},{68,5},{69,6},{70,7},{71,8},{72,9},{73... | collective-permute-start | bytes 6291464 | tf_op jit(solution)/shard_map/ppermute | solution.py:306
  6.0 0.8 outgoing.1
  6.8 4.4 %collective-permute-start = (f32[512,512]{1,0:T(8,128)S(1)}, f32[512,512]{1,0:T(8,128)S(1)}, u32[]{:S(2)}, u32[]{:S(2)}) collective-permute-start(f32[512,512]{1,0:T(8,128)S(1)} %get-tuple-element.18.after_ref), channel_id=1, source_target_pairs={{0,64},{1,65},{2,66},{3,67},{4,68},{5,69},{6,70},{7,71},{8,72},{9,... | collective-permute-start | bytes 3145736 | tf_op jit(solution)/shard_map/ppermute | solution.py:306
  11.8 2.1 %own_store.1 = (bf16[6,2,512,512]{3,2,1,0:T(8,128)(2,1)S(1)}, f32[1,512,512]{2,1,0:T(8,128)S(1)}) custom-call(s32[1]{0:T(128)} %bitcast.core_ref, s32[1,2,3]{2,1,0:T(2,128)S(1)} %copy-done.1, s32[1,2,3]{2,1,0:T(2,128)S(1)} %copy-done.2, f32[1,4]{1,0:T(1,128)S(1)} %copy-done.3, f32[1,2,3,512,512]{4,3,2,1,0:T(8,128)S(1)} %copy-done, f32[3,2,512,512]{3,2,1,0:T(8,128)} %b_ref.1, ...), custom_call_target="tpu_custom_call" | custom-call | bytes 1024 | tf_op jit(solution)/shard_map/own_store/pallas_call | solution.py:143
  13.9 1.9 %collective-permute-start.3 = (f32[1,512,512]{2,1,0:T(8,128)S(1)}, f32[1,512,512]{2,1,0:T(8,128)S(1)}, u32[]{:S(2)}, u32[]{:S(2)}) collective-permute-start(f32[1,512,512]{2,1,0:T(8,128)S(1)} %get-tuple-element.22), channel_id=1, source_target_pairs={{64,1},{65,2},{66,3},{67,4},{68,5},{69,6},{70,7},{71,8},{72,9},{73... | collective-permute-start | bytes 3145736 | tf_op jit(solution)/shard_map/ppermute | solution.py:306
  15.8 0.7 collective-permute-done.2.refs_2_
  16.5 1.1 %full_store.1.ta_ref.tb_ref.t_ref = bf16[6,2,512,512]{3,2,1,0:T(8,128)(2,1)S(1)} custom-call(f32[512,512]{1,0:T(8,128)S(1)} %collective-permute-done.refs_0_, f32[512,512]{1,0:T(8,128)S(1)} %collective-permute-done.1.refs_1_, f32[512,512]{1,0:T(8,128)S(1)} %collective-permute-done.2.refs_2_, ...), custom_call_target="tpu_custom_call", output_to_operand_aliasing={{}: (3, {})} | custom-call | bytes 1024 | tf_op jit(solution)/shard_map/full_store/pallas_call | solution.py:172
  18.1 10.9 %near_terms_0.1.p_ref = f32[3,512,512]{2,1,0:T(8,128)S(1)} custom-call(s32[1]{0:T(128)} %bitcast.core_ref, f32[3,2,512,512]{3,2,1,0:T(8,128)S(1)} %bitcast.3, f32[3,2,512,512]{3,2,1,0:T(8,128)S(1)} %bitcast.3, bf16[6,2,512,512]{3,2,1,0:T(8,128)(2,1)S(1)} %full_store.1.ta_ref.tb_ref.t_ref, bf16[6,2,512,512]{3,2,1,0:T(8,128)(2,1)S(1)} %full_store.1.ta_ref.tb_ref.t_ref), custom_call_target="tpu_custom_call" | custom-call | bytes 1024 | tf_op jit(solution)/shard_map/near_terms_0/pallas_call | solution.py:202
  29.0 1.0 %collective-permute-done.4.h_ref = f32[2,512,512]{2,1,0:T(8,128)S(1)} collective-permute-done((f32[2,512,512]{2,1,0:T(8,128)S(1)}, f32[2,512,512]{2,1,0:T(8,128)S(1)}, u32[]{:S(2)}, u32[]{:S(2)}) %collective-permute-start.4) | collective-permute-done | bytes 2097184 | tf_op jit(solution)/shard_map/ppermute | solution.py:306
  30.0 3.9 %far_terms_0.2.refs_0_.a_ref = f32[2,512,512]{2,1,0:T(8,128)S(1)} custom-call(s32[1]{0:T(128)} %bitcast.core_ref, f32[3,512,512]{2,1,0:T(8,128)S(1)} %near_terms_0.1.p_ref, f32[2,512,512]{2,1,0:T(8,128)S(1)} %collective-permute-done.4.h_ref, bf16[6,2,512,512]{3,2,1,0:T(8,128)(2,1)S(1)} %full_store.1.ta_ref.tb_ref.t_ref), custom_call_target="tpu_custom_call" | custom-call | bytes 1024 | tf_op jit(solution)/shard_map/far_terms_0/pallas_call | solution.py:226
  33.9 4.2 %collective-permute-start.6 = (f32[2,512,512]{2,1,0:T(8,128)S(1)}, f32[2,512,512]{2,1,0:T(8,128)S(1)}, u32[]{:S(2)}, u32[]{:S(2)}) collective-permute-start(f32[2,512,512]{2,1,0:T(8,128)S(1)} %far_terms_0.2.refs_0_.a_ref), channel_id=1, source_target_pairs={{0,64},{1,65},{2,66},{3,67},{4,68},{5,69},{6,70},{7,71},{8,72},{9,... | collective-permute-start | bytes 6291464 | tf_op jit(solution)/shard_map/ppermute | solution.py:306
  38.1 1.9 %collective-permute-start.8 = (f32[2,512,512]{2,1,0:T(8,128)S(1)}, f32[2,512,512]{2,1,0:T(8,128)S(1)}, u32[]{:S(2)}, u32[]{:S(2)}) collective-permute-start(f32[2,512,512]{2,1,0:T(8,128)S(1)} %far_terms_0.2.refs_0_.a_ref), channel_id=1, source_target_pairs={{64,1},{65,2},{66,3},{67,4},{68,5},{69,6},{70,7},{71,8},{72,9},{73... | collective-permute-start | bytes 6291464 | tf_op jit(solution)/shard_map/ppermute | solution.py:306
  40.0 1.2 %collective-permute-done.3.h_ref = f32[1,512,512]{2,1,0:T(8,128)S(1)} collective-permute-done((f32[1,512,512]{2,1,0:T(8,128)S(1)}, f32[1,512,512]{2,1,0:T(8,128)S(1)}, u32[]{:S(2)}, u32[]{:S(2)}) %collective-permute-start.3) | collective-permute-done | bytes 1048608 | tf_op jit(solution)/shard_map/ppermute | solution.py:306
  41.2 1.9 %far_terms_0.3.a_ref.refs_0_ = f32[1,512,512]{2,1,0:T(8,128)S(1)} custom-call(s32[1]{0:T(128)} %bitcast.core_ref, f32[3,512,512]{2,1,0:T(8,128)S(1)} %near_terms_0.1.p_ref, f32[1,512,512]{2,1,0:T(8,128)S(1)} %collective-permute-done.3.h_ref, bf16[6,2,512,512]{3,2,1,0:T(8,128)(2,1)S(1)} %full_store.1.ta_ref.tb_ref.t_ref, ...), custom_call_target="tpu_custom_call" | custom-call | flops 18400000000 | bytes 1024 | tf_op jit(solution)/shard_map/far_terms_0/pallas_call | solution.py:226
  43.2 4.7 %collective-permute-start.5 = (f32[1,512,512]{2,1,0:T(8,128)S(1)}, f32[1,512,512]{2,1,0:T(8,128)S(1)}, u32[]{:S(2)}, u32[]{:S(2)}) collective-permute-start(f32[1,512,512]{2,1,0:T(8,128)S(1)} %far_terms_0.3.a_ref.refs_0_), channel_id=1, source_target_pairs={{0,64},{1,65},{2,66},{3,67},{4,68},{5,69},{6,70},{7,71},{8,72},{9,... | collective-permute-start | bytes 3145736 | tf_op jit(solution)/shard_map/ppermute | solution.py:306
  47.9 2.1 %collective-permute-start.7 = (f32[1,512,512]{2,1,0:T(8,128)S(1)}, f32[1,512,512]{2,1,0:T(8,128)S(1)}, u32[]{:S(2)}, u32[]{:S(2)}) collective-permute-start(f32[1,512,512]{2,1,0:T(8,128)S(1)} %far_terms_0.3.a_ref.refs_0_), channel_id=1, source_target_pairs={{64,1},{65,2},{66,3},{67,4},{68,5},{69,6},{70,7},{71,8},{72,9},{73... | collective-permute-start | bytes 3145736 | tf_op jit(solution)/shard_map/ppermute | solution.py:306
  50.0 7.3 %near_terms_1.2.refs_0_.p_ref = f32[2,512,512]{2,1,0:T(8,128)S(1)} custom-call(s32[1]{0:T(128)} %bitcast.core_ref, f32[2,512,512]{2,1,0:T(8,128)S(1)} %far_terms_0.2.refs_0_.a_ref, f32[2,512,512]{2,1,0:T(8,128)S(1)} %collective-permute-done.6.b_ref.refs_1_, bf16[6,2,512,512]{3,2,1,0:T(8,128)(2,1)S(1)} %full_store.1.ta_ref.tb_ref.t_ref, ...), custom_call_target="tpu_custom_call" | custom-call | bytes 1024 | tf_op jit(solution)/shard_map/near_terms_1/pallas_call | solution.py:202
  57.3 3.6 %near_terms_1.3.refs_0_.p_ref = f32[1,512,512]{2,1,0:T(8,128)S(1)} custom-call(s32[1]{0:T(128)} %bitcast.core_ref, f32[1,512,512]{2,1,0:T(8,128)S(1)} %far_terms_0.3.a_ref.refs_0_, f32[1,512,512]{2,1,0:T(8,128)S(1)} %collective-permute-done.5.b_ref.refs_1_, bf16[6,2,512,512]{3,2,1,0:T(8,128)(2,1)S(1)} %full_store.1.ta_ref.tb_ref.t_ref, ...), custom_call_target="tpu_custom_call" | custom-call | bytes 1024 | tf_op jit(solution)/shard_map/near_terms_1/pallas_call | solution.py:202
  60.9 4.8 %collective-permute-done.8.h_ref = f32[2,512,512]{2,1,0:T(8,128)S(1)} collective-permute-done((f32[2,512,512]{2,1,0:T(8,128)S(1)}, f32[2,512,512]{2,1,0:T(8,128)S(1)}, u32[]{:S(2)}, u32[]{:S(2)}) %collective-permute-start.8) | collective-permute-done | bytes 2097184 | tf_op jit(solution)/shard_map/ppermute | solution.py:306
  65.7 3.8 %far_terms_1.2 = (f32[2,128,512]{2,1,0:T(8,128)S(1)}, f32[2,128,512]{2,1,0:T(8,128)S(1)}, f32[2,128,512]{2,1,0:T(8,128)S(1)}, f32[2,128,512]{2,1,0:T(8,128)S(1)}) custom-call(s32[1]{0:T(128)} %bitcast.core_ref, f32[2,512,512]{2,1,0:T(8,128)S(1)} %near_terms_1.2.refs_0_.p_ref, f32[2,512,512]{2,1,0:T(8,128)S(1)} %collective-permute-done.8.h_ref, ...), custom_call_target="tpu_custom_call" | custom-call | bytes 1024 | tf_op jit(solution)/shard_map/far_terms_1/pallas_call | solution.py:226
  69.6 4.0 %collective-permute-start.10 = (f32[2,128,512]{2,1,0:T(8,128)S(1)}, f32[2,128,512]{2,1,0:T(8,128)S(1)}, u32[]{:S(2)}, u32[]{:S(2)}) collective-permute-start(f32[2,128,512]{2,1,0:T(8,128)S(1)} %get-tuple-element.24.refs_7_), channel_id=1, source_target_pairs={{0,64},{1,65},{2,66},{3,67},{4,68},{5,69},{6,70},{7,71},{8,72},{9,... | collective-permute-start | bytes 1572872 | tf_op jit(solution)/shard_map/ppermute | solution.py:306
  74.2 0.9 %collective-permute-done.10.refs_3_ = f32[2,128,512]{2,1,0:T(8,128)S(1)} collective-permute-done((f32[2,128,512]{2,1,0:T(8,128)S(1)}, f32[2,128,512]{2,1,0:T(8,128)S(1)}, u32[]{:S(2)}, u32[]{:S(2)}) %collective-permute-start.10) | collective-permute-done | bytes 524320 | tf_op jit(solution)/shard_map/ppermute | solution.py:306
  75.1 0.7 collective-permute-done.11.refs_4_
  75.9 0.7 collective-permute-done.12.refs_5_
  76.6 0.7 collective-permute-done.9.refs_2_
  77.4 2.1 %early_rows.1 = (f32[3,2,512,512]{3,2,1,0:T(8,128)}, f32[8,128]{1,0:T(8,128)S(1)}) custom-call(s32[1]{0:T(128)} %bitcast.core_ref, f32[2,512,512]{2,1,0:T(8,128)S(1)} %far_terms_0.2.refs_0_.a_ref, f32[2,512,512]{2,1,0:T(8,128)S(1)} %collective-permute-done.6.b_ref.refs_1_, f32[2,128,512]{2,1,0:T(8,128)S(1)} %collective-permute-done.9.refs_2_, ...), custom_call_target="tpu_custom_call" | custom-call | bytes 1024 | tf_op jit(solution)/shard_map/early_rows/pallas_call | solution.py:282
  79.5 1.9 %far_terms_1.3 = (f32[1,256,512]{2,1,0:T(8,128)S(1)}, f32[1,256,512]{2,1,0:T(8,128)S(1)}) custom-call(s32[1]{0:T(128)} %bitcast.core_ref, f32[1,512,512]{2,1,0:T(8,128)S(1)} %near_terms_1.3.refs_0_.p_ref, f32[1,512,512]{2,1,0:T(8,128)S(1)} %collective-permute-done.7.h_ref, bf16[6,2,512,512]{3,2,1,0:T(8,128)(2,1)S(1)} %full_store.1.ta_ref.tb_ref.t_ref, ...), custom_call_target="tpu_custom_call" | custom-call | bytes 1024 | tf_op jit(solution)/shard_map/far_terms_1/pallas_call | solution.py:226
  81.5 1.4 %collective-permute-start.13 = (f32[1,256,512]{2,1,0:T(8,128)S(1)}, f32[1,256,512]{2,1,0:T(8,128)S(1)}, u32[]{:S(2)}, u32[]{:S(2)}) collective-permute-start(f32[1,256,512]{2,1,0:T(8,128)S(1)} %get-tuple-element.28.refs_2_), channel_id=1, source_target_pairs={{0,64},{1,65},{2,66},{3,67},{4,68},{5,69},{6,70},{7,71},{8,72},{9,... | collective-permute-start | bytes 1572872 | tf_op jit(solution)/shard_map/ppermute | solution.py:306
  83.0 1.1 %middle_rows.1.refs_2_ = f32[3,2,512,512]{3,2,1,0:T(8,128)} custom-call(s32[1]{0:T(128)} %bitcast.core_ref, f32[1,512,512]{2,1,0:T(8,128)S(1)} %far_terms_0.3.a_ref.refs_0_, f32[1,512,512]{2,1,0:T(8,128)S(1)} %collective-permute-done.5.b_ref.refs_1_, f32[1,256,512]{2,1,0:T(8,128)S(1)} %get-tuple-element.28.refs_2_, ...), custom_call_target="tpu_custom_call", output_to_operand_aliasing={{}: (5, {})} | custom-call | bytes 1024 | tf_op jit(solution)/shard_map/middle_rows/pallas_call | solution.py:282
  84.4 0.7 collective-permute-done.14.refs_1_
  85.2 1.1 %late_rows.1 = f32[3,2,512,512]{3,2,1,0:T(8,128)} custom-call(s32[1]{0:T(128)} %bitcast.core_ref, f32[1,256,512]{2,1,0:T(8,128)S(1)} %collective-permute-done.13.refs_0_, f32[1,256,512]{2,1,0:T(8,128)S(1)} %collective-permute-done.14.refs_1_, f32[3,2,512,512]{3,2,1,0:T(8,128)} %middle_rows.1.refs_2_), custom_call_target="tpu_custom_call", output_to_operand_aliasing={{}: (3, {})} | custom-call | bytes 1024 | tf_op jit(solution)/shard_map/late_rows/pallas_call | solution.py:282
  (25 shorter events, 2.1 us)
Async XLA Ops:
  0.0 6.0 %copy-start.1 = (s32[1,2,3]{2,1,0:T(2,128)S(1)}, s32[1,2,3]{2,1,0:T(2,128)}, u32[]{:S(2)}) copy-start(s32[1,2,3]{2,1,0:T(2,128)} %live_ref.3) | copy-start | bytes 76
  0.0 6.0 %copy-start.2 = (s32[1,2,3]{2,1,0:T(2,128)S(1)}, s32[1,2,3]{2,1,0:T(2,128)}, u32[]{:S(2)}) copy-start(s32[1,2,3]{2,1,0:T(2,128)} %index_ref.3) | copy-start | bytes 76
  0.0 6.0 %copy-start.3 = (f32[1,4]{1,0:T(1,128)S(1)}, f32[1,4]{1,0:T(1,128)}, u32[]{:S(2)}) copy-start(f32[1,4]{1,0:T(1,128)} %coef_ref.3) | copy-start | bytes 52
  0.0 6.0 %copy-start = (f32[1,2,3,512,512]{4,3,2,1,0:T(8,128)S(1)}, f32[1,2,3,512,512]{4,3,2,1,0:T(8,128)}, u32[]{:S(2)}) copy-start(f32[1,2,3,512,512]{4,3,2,1,0:T(8,128)} %t_ref.3) | copy-start | bytes 18874372
  1.8 28.2 %collective-permute-start.4 = (f32[2,512,512]{2,1,0:T(8,128)S(1)}, f32[2,512,512]{2,1,0:T(8,128)S(1)}, u32[]{:S(2)}, u32[]{:S(2)}) collective-permute-start(f32[2,512,512]{2,1,0:T(8,128)S(1)} %edge.1.after_ref), channel_id=1, source_target_pairs={{64,1},{65,2},{66,3},{67,4},{68,5},{69,6},{70,7},{71,8},{72,9},{73... | collective-permute-start | bytes 6291464 | tf_op jit(solution)/shard_map/ppermute | solution.py:306
  6.8 9.0 %collective-permute-start = (f32[512,512]{1,0:T(8,128)S(1)}, f32[512,512]{1,0:T(8,128)S(1)}, u32[]{:S(2)}, u32[]{:S(2)}) collective-permute-start(f32[512,512]{1,0:T(8,128)S(1)} %get-tuple-element.18.after_ref), channel_id=1, source_target_pairs={{0,64},{1,65},{2,66},{3,67},{4,68},{5,69},{6,70},{7,71},{8,72},{9,... | collective-permute-start | bytes 3145736 | tf_op jit(solution)/shard_map/ppermute | solution.py:306
  11.2 4.6 %collective-permute-start.1 = (f32[512,512]{1,0:T(8,128)S(1)}, f32[512,512]{1,0:T(8,128)S(1)}, u32[]{:S(2)}, u32[]{:S(2)}) collective-permute-start(f32[512,512]{1,0:T(8,128)S(1)} %get-tuple-element.19), channel_id=1, source_target_pairs={{0,64},{1,65},{2,66},{3,67},{4,68},{5,69},{6,70},{7,71},{8,72},{9,... | collective-permute-start | bytes 3145736 | tf_op jit(solution)/shard_map/ppermute | solution.py:306
  11.3 5.2 %collective-permute-start.2 = (f32[512,512]{1,0:T(8,128)S(1)}, f32[512,512]{1,0:T(8,128)S(1)}, u32[]{:S(2)}, u32[]{:S(2)}) collective-permute-start(f32[512,512]{1,0:T(8,128)S(1)} %get-tuple-element.20), channel_id=1, source_target_pairs={{0,64},{1,65},{2,66},{3,67},{4,68},{5,69},{6,70},{7,71},{8,72},{9,... | collective-permute-start | bytes 3145736 | tf_op jit(solution)/shard_map/ppermute | solution.py:306
  11.8 5.9 %slice-start = ((s8[6291456]{0:T(1024)(128)(4,1)}), s8[4194304]{0:T(1024)(128)(4,1)S(1)}, s32[]{:S(2)}) async-start(s8[6291456]{0:T(1024)(128)(4,1)} %bitcast.2), calls=%async_computation | async-start | bytes 8388608
  13.9 27.4 %collective-permute-start.3 = (f32[1,512,512]{2,1,0:T(8,128)S(1)}, f32[1,512,512]{2,1,0:T(8,128)S(1)}, u32[]{:S(2)}, u32[]{:S(2)}) collective-permute-start(f32[1,512,512]{2,1,0:T(8,128)S(1)} %get-tuple-element.22), channel_id=1, source_target_pairs={{64,1},{65,2},{66,3},{67,4},{68,5},{69,6},{70,7},{71,8},{72,9},{73... | collective-permute-start | bytes 3145736 | tf_op jit(solution)/shard_map/ppermute | solution.py:306
  16.5 1.6 %slice-start.1 = ((s8[6291456]{0:T(1024)(128)(4,1)}), s8[2097152]{0:T(1024)(128)(4,1)S(1)}, s32[]{:S(2)}) async-start(s8[6291456]{0:T(1024)(128)(4,1)} %bitcast.2), calls=%async_computation.1 | async-start | bytes 4194304
  33.9 16.1 %collective-permute-start.6 = (f32[2,512,512]{2,1,0:T(8,128)S(1)}, f32[2,512,512]{2,1,0:T(8,128)S(1)}, u32[]{:S(2)}, u32[]{:S(2)}) collective-permute-start(f32[2,512,512]{2,1,0:T(8,128)S(1)} %far_terms_0.2.refs_0_.a_ref), channel_id=1, source_target_pairs={{0,64},{1,65},{2,66},{3,67},{4,68},{5,69},{6,70},{7,71},{8,72},{9,... | collective-permute-start | bytes 6291464 | tf_op jit(solution)/shard_map/ppermute | solution.py:306
  38.1 27.6 %collective-permute-start.8 = (f32[2,512,512]{2,1,0:T(8,128)S(1)}, f32[2,512,512]{2,1,0:T(8,128)S(1)}, u32[]{:S(2)}, u32[]{:S(2)}) collective-permute-start(f32[2,512,512]{2,1,0:T(8,128)S(1)} %far_terms_0.2.refs_0_.a_ref), channel_id=1, source_target_pairs={{64,1},{65,2},{66,3},{67,4},{68,5},{69,6},{70,7},{71,8},{72,9},{73... | collective-permute-start | bytes 6291464 | tf_op jit(solution)/shard_map/ppermute | solution.py:306
  43.2 14.1 %collective-permute-start.5 = (f32[1,512,512]{2,1,0:T(8,128)S(1)}, f32[1,512,512]{2,1,0:T(8,128)S(1)}, u32[]{:S(2)}, u32[]{:S(2)}) collective-permute-start(f32[1,512,512]{2,1,0:T(8,128)S(1)} %far_terms_0.3.a_ref.refs_0_), channel_id=1, source_target_pairs={{0,64},{1,65},{2,66},{3,67},{4,68},{5,69},{6,70},{7,71},{8,72},{9,... | collective-permute-start | bytes 3145736 | tf_op jit(solution)/shard_map/ppermute | solution.py:306
  47.9 31.7 %collective-permute-start.7 = (f32[1,512,512]{2,1,0:T(8,128)S(1)}, f32[1,512,512]{2,1,0:T(8,128)S(1)}, u32[]{:S(2)}, u32[]{:S(2)}) collective-permute-start(f32[1,512,512]{2,1,0:T(8,128)S(1)} %far_terms_0.3.a_ref.refs_0_), channel_id=1, source_target_pairs={{64,1},{65,2},{66,3},{67,4},{68,5},{69,6},{70,7},{71,8},{72,9},{73... | collective-permute-start | bytes 3145736 | tf_op jit(solution)/shard_map/ppermute | solution.py:306
  69.6 5.6 %collective-permute-start.10 = (f32[2,128,512]{2,1,0:T(8,128)S(1)}, f32[2,128,512]{2,1,0:T(8,128)S(1)}, u32[]{:S(2)}, u32[]{:S(2)}) collective-permute-start(f32[2,128,512]{2,1,0:T(8,128)S(1)} %get-tuple-element.24.refs_7_), channel_id=1, source_target_pairs={{0,64},{1,65},{2,66},{3,67},{4,68},{5,69},{6,70},{7,71},{8,72},{9,... | collective-permute-start | bytes 1572872 | tf_op jit(solution)/shard_map/ppermute | solution.py:306
  73.6 2.3 %collective-permute-start.11 = (f32[2,128,512]{2,1,0:T(8,128)S(1)}, f32[2,128,512]{2,1,0:T(8,128)S(1)}, u32[]{:S(2)}, u32[]{:S(2)}) collective-permute-start(f32[2,128,512]{2,1,0:T(8,128)S(1)} %get-tuple-element.25.refs_8_), channel_id=1, source_target_pairs={{0,64},{1,65},{2,66},{3,67},{4,68},{5,69},{6,70},{7,71},{8,72},{9,... | collective-permute-start | bytes 1572872 | tf_op jit(solution)/shard_map/ppermute | solution.py:306
  73.7 2.9 %collective-permute-start.12 = (f32[2,128,512]{2,1,0:T(8,128)S(1)}, f32[2,128,512]{2,1,0:T(8,128)S(1)}, u32[]{:S(2)}, u32[]{:S(2)}) collective-permute-start(f32[2,128,512]{2,1,0:T(8,128)S(1)} %get-tuple-element.26.refs_9_), channel_id=1, source_target_pairs={{0,64},{1,65},{2,66},{3,67},{4,68},{5,69},{6,70},{7,71},{8,72},{9,... | collective-permute-start | bytes 1572872 | tf_op jit(solution)/shard_map/ppermute | solution.py:306
  74.1 3.3 %collective-permute-start.9 = (f32[2,128,512]{2,1,0:T(8,128)S(1)}, f32[2,128,512]{2,1,0:T(8,128)S(1)}, u32[]{:S(2)}, u32[]{:S(2)}) collective-permute-start(f32[2,128,512]{2,1,0:T(8,128)S(1)} %get-tuple-element.23.refs_6_), channel_id=1, source_target_pairs={{0,64},{1,65},{2,66},{3,67},{4,68},{5,69},{6,70},{7,71},{8,72},{9,... | collective-permute-start | bytes 1572872 | tf_op jit(solution)/shard_map/ppermute | solution.py:306
  81.5 3.0 %collective-permute-start.13 = (f32[1,256,512]{2,1,0:T(8,128)S(1)}, f32[1,256,512]{2,1,0:T(8,128)S(1)}, u32[]{:S(2)}, u32[]{:S(2)}) collective-permute-start(f32[1,256,512]{2,1,0:T(8,128)S(1)} %get-tuple-element.28.refs_2_), channel_id=1, source_target_pairs={{0,64},{1,65},{2,66},{3,67},{4,68},{5,69},{6,70},{7,71},{8,72},{9,... | collective-permute-start | bytes 1572872 | tf_op jit(solution)/shard_map/ppermute | solution.py:306
  82.9 2.3 %collective-permute-start.14 = (f32[1,256,512]{2,1,0:T(8,128)S(1)}, f32[1,256,512]{2,1,0:T(8,128)S(1)}, u32[]{:S(2)}, u32[]{:S(2)}) collective-permute-start(f32[1,256,512]{2,1,0:T(8,128)S(1)} %get-tuple-element.29.refs_3_), channel_id=1, source_target_pairs={{0,64},{1,65},{2,66},{3,67},{4,68},{5,69},{6,70},{7,71},{8,72},{9,... | collective-permute-start | bytes 1572872 | tf_op jit(solution)/shard_map/ppermute | solution.py:306

commit v2 on v1

--- a/solution.py
+++ b/solution.py
@@ -11,9 +11,10 @@
 BF16 = jnp.bfloat16
 LIMIT = 28 << 20
 
-STORE = 6
+STORE = 7
 CUTS = 2
-PARTS = 2
+PARTS = 1
+HALVES = 2
 
 
 def split(x):
@@ -29,11 +30,17 @@
     return lax.dot_general(a, b, (((1,), (1,)), ((), ())), preferred_element_type=F32)
 
 
+def inner_halves(block, high, low):
+    block_high, block_low = split(block)
+    return split(dot_nt(block_high, high) + dot_nt(block_high, low) + dot_nt(block_low, high))
+
+
+def outer(high, low, inner_high, inner_low):
+    return dot_nn(high, inner_high) + dot_nn(low, inner_high) + dot_nn(high, inner_low)
+
+
 def sandwich(block, high, low):
-    block_high, block_low = split(block)
-    inner = dot_nt(block_high, high) + dot_nt(block_high, low) + dot_nt(block_low, high)
-    inner_high, inner_low = split(inner)
-    return dot_nn(high, inner_high) + dot_nn(low, inner_high) + dot_nn(high, inner_low)
+    return outer(high, low, *inner_halves(block, high, low))
 
 
 def cost(weight=0.0):
@@ -118,7 +125,8 @@
 
     def kernel(core_ref, live_ref, index_ref, coef_ref, t_ref, e_ref, after_ref, o_ref, edge_ref, sems):
         c = core_ref[0]
-        slot = slot_at(pl.program_id(0), c)
+        k = pl.program_id(0)
+        slot = jnp.where(k < 3, slot_at(k, c), 0)
         parts = 4
         copies = []
         for p in range(parts):
@@ -126,16 +134,16 @@
             for n in range(3 - CUTS):
                 copies.append(pltpu.make_async_copy(e_ref.at[CUTS + n, c, span], edge_ref.at[n, span], sems.at[n * parts + p]))
 
-        @pl.when(pl.program_id(0) == 0)
+        @pl.when(k == 0)
         def _():
             for copy in copies:
                 copy.start()
 
-        high, low = split((t_ref[0, 0, 0] * root(live_ref, index_ref, coef_ref, c, slot, width)).T)
+        high, low = split((t_ref[0, 0, 0] * root(live_ref, index_ref, coef_ref, jnp.where(k < 3, c, 1 - c), slot, width)).T)
         o_ref[0, 0] = high
         o_ref[0, 1] = low
 
-        @pl.when(pl.program_id(0) == 2)
+        @pl.when(k == 3)
         def _():
             for copy in copies:
                 copy.wait()
@@ -144,9 +152,9 @@
         kernel,
         grid_spec=pltpu.PrefetchScalarGridSpec(
             num_scalar_prefetch=1,
-            grid=(3,),
-            in_specs=SCALARS + [pl.BlockSpec((1, 1, 1, width, width), lambda k, c: (0, c[0], slot_at(k, c[0]), 0, 0)), HBM_REF, HBM_REF],
-            out_specs=[pl.BlockSpec((1, 2, width, width), lambda k, c: (k, 0, 0, 0)), pl.BlockSpec(memory_space=pltpu.VMEM)],
+            grid=(4,),
+            in_specs=SCALARS + [pl.BlockSpec((1, 1, 1, width, width), lambda k, c: (0, jnp.where(k < 3, c[0], 1 - c[0]), jnp.where(k < 3, slot_at(k, c[0]), 0), 0, 0)), HBM_REF, HBM_REF],
+            out_specs=[pl.BlockSpec((1, 2, width, width), lambda k, c: (jnp.where(k < 3, k, 6), 0, 0, 0)), pl.BlockSpec(memory_space=pltpu.VMEM)],
             scratch_shapes=[pltpu.SemaphoreType.DMA((4 * (3 - CUTS),))],
         ),
         out_shape=[jax.ShapeDtypeStruct((STORE, 2, width, width), BF16), jax.ShapeDtypeStruct((3 - CUTS, width, width), F32)],
@@ -182,13 +190,15 @@
     )(*received, store)
 
 
-def near_terms(core, site, own, other, in_env, store, after):
+def near_terms(core, site, own, other, in_env, store, parts, after):
     states, width = own.shape[0], own.shape[-1]
+    rows = width // parts
 
     def kernel(core_ref, a_ref, b_ref, ta_ref, tb_ref, *refs):
-        o_ref = refs[-1]
         a, b = (a_ref[0, 0], b_ref[0, 0]) if in_env else (a_ref[0], b_ref[0])
-        o_ref[0] = sandwich(a, ta_ref[0, 0], ta_ref[0, 1]) + sandwich(b, tb_ref[0, 0], tb_ref[0, 1])
+        total = sandwich(a, ta_ref[0, 0], ta_ref[0, 1]) + sandwich(b, tb_ref[0, 0], tb_ref[0, 1])
+        for p in range(parts):
+            refs[len(after) + p][0] = total[p * rows : (p + 1) * rows]
 
     def slot(k):
         return lambda n, c: ((3 * c[0] if site == 0 else 3 - 3 * c[0]) + k, 0, 0, 0)
@@ -205,9 +215,9 @@
             num_scalar_prefetch=1,
             grid=(states,),
             in_specs=sources + [pl.BlockSpec(pair, slot(0)), pl.BlockSpec(pair, slot(1))] + [HBM_REF] * len(after),
-            out_specs=row,
-        ),
-        out_shape=jax.ShapeDtypeStruct((states, width, width), F32),
+            out_specs=[pl.BlockSpec((1, rows, width), lambda n, c: (n, 0, 0))] * parts,
+        ),
+        out_shape=[jax.ShapeDtypeStruct((states, rows, width), F32)] * parts,
         compiler_params=params(),
         cost_estimate=cost(),
         name=f"near_terms_{site}",
@@ -296,11 +306,69 @@
     )(core, *sources, *old)
 
 
+def last_rows(core, out, moved, partials, sums, from_left, from_right, store):
+    width = from_left.shape[-1]
+    rows = width // HALVES
+    first = out.shape[0] - from_left.shape[0]
+    given = [*moved, *partials, *sums]
+    early = moved[0].shape[1]
+
+    def kernel(core_ref, *refs):
+        blocks, near = refs[: len(moved)], refs[len(moved) : len(given)]
+        left, right, t_left, t_right, _, o_ref, buf, sems, early_sems = refs[len(given) :]
+
+        @pl.when(core_ref[0] == 1)
+        def _():
+            copies = []
+            for p, block in enumerate(blocks):
+                for n in range(first):
+                    copies.append(pltpu.make_async_copy(block.at[n], o_ref.at[n, 0, pl.ds(p * early, early)], early_sems.at[p, n]))
+                    copies[-1].start()
+            for sector, (halo, t) in enumerate(((left, t_left), (right, t_right))):
+                high, low = t[0, 0], t[0, 1]
+                inner_high, inner_low = inner_halves(halo[0], high, low)
+                for h in range(HALVES):
+                    span = slice(h * rows, (h + 1) * rows)
+                    part, inside = h * PARTS // HALVES, h * rows % (width // PARTS)
+                    base = near[sector * PARTS + part][0, inside : inside + rows]
+                    buf[sector, span] = base + outer(high[span], low[span], inner_high, inner_low)
+                    copies.append(pltpu.make_async_copy(buf.at[sector, span], o_ref.at[first, sector, span], sems.at[sector, h]))
+                    copies[-1].start()
+            for copy in copies:
+                copy.wait()
+
+    whole = pl.BlockSpec(memory_space=pltpu.VMEM)
+    pair = (1, 2, width, width)
+    return pl.pallas_call(
+        kernel,
+        grid_spec=pltpu.PrefetchScalarGridSpec(
+            num_scalar_prefetch=1,
+            grid=(1,),
+            in_specs=[whole] * (len(given) + 2)
+            + [pl.BlockSpec(pair, lambda n, c: (6, 0, 0, 0)), pl.BlockSpec(pair, lambda n, c: (2, 0, 0, 0)), HBM_REF],
+            out_specs=HBM_REF,
+            scratch_shapes=[
+                pltpu.VMEM((2, width, width), F32),
+                pltpu.SemaphoreType.DMA((2, HALVES)),
+                pltpu.SemaphoreType.DMA((len(moved), first)),
+            ],
+        ),
+        out_shape=jax.ShapeDtypeStruct(out.shape, F32),
+        input_output_aliases={len(given) + 5: 0},
+        compiler_params=params(),
+        cost_estimate=cost(),
+        name="last_rows",
+    )(core, *given, from_left, from_right, store, store, out)
+
+
 def shards(chips, env_in, site_tensor, pair_live, coef_index, mpo_coef):
     axes = ("site", "blk")
     core = jnp.reshape(lax.axis_index("site"), (1,)).astype(jnp.int32)
     swap = [(s * chips + j, (1 - s) * chips + j) for s in range(2) for j in range(chips)]
     meet = [(chips + j, j + 1) for j in range(chips - 1)] + [(j + 1, chips + j) for j in range(chips - 1)]
+
+    to_right = [(chips + j, chips + j + 1) for j in range(chips - 1)]
+    to_left = [(j + 1, chips + j) for j in range(chips - 1)]
 
     def send(value, pairs):
         return lax.ppermute(value, axes, pairs)
@@ -315,23 +383,20 @@
     halo_b = send(edge_b, meet)
     store = full_store(store, received)
 
-    near = near_terms(core, 0, env_in, env_in, True, store, [])
-    first_a, = far_terms(core, 0, near, 0, halo_a, store, 1, 0, [])
+    (near,) = near_terms(core, 0, env_in, env_in, True, store, 1, [])
+    (first_a,) = far_terms(core, 0, near, 0, halo_a, store, 1, 0, [])
     second_halo_a, crossed_a = send(first_a, meet), send(first_a, swap)
-    first_b, = far_terms(core, 0, near, CUTS, halo_b, store, 1, 16, [first_a])
-    second_halo_b, crossed_b = send(first_b, meet), send(first_b, swap)
-
-    near_a = near_terms(core, 1, first_a, crossed_a, False, store, [])
-    near_b = near_terms(core, 1, first_b, crossed_b, False, store, [near_a])
-    second_a = far_terms(core, 1, near_a, 0, second_halo_a, store, 2 * PARTS, 0, [near_b])
+    (first_b,) = far_terms(core, 0, near, CUTS, halo_b, store, 1, 16, [first_a])
+    from_left, from_right, crossed_b = send(first_b, to_right), send(first_b, to_left), send(first_b, swap)
+
+    (near_a,) = near_terms(core, 1, first_a, crossed_a, False, store, 1, [])
+    sums = near_terms(core, 1, first_b, crossed_b, False, store, PARTS, [near_a])
+    partials = [send(block, swap) for block in sums]
+    second_a = far_terms(core, 1, near_a, 0, second_halo_a, store, 2, 0, sums[:1])
     moved_a = [send(block, swap) for block in second_a]
-    early = [([first_a], 0, 0), ([crossed_a], 0, 1)], [(moved_a, 0, 0), (second_a, 0, 1)]
-    out, mark = write_rows(core, None, env_in.shape, early, "early_rows")
-    second_b = far_terms(core, 1, near_b, 0, second_halo_b, store, PARTS, 0, [mark])
-    moved_b = [send(block, swap) for block in second_b]
-    middle = [([first_b], CUTS, 0), ([crossed_b], CUTS, 1)], [(second_b, CUTS, 1)]
-    (out,) = write_rows(core, out, env_in.shape, middle, "middle_rows")
-    (out,) = write_rows(core, out, env_in.shape, ([], [(moved_b, CUTS, 0)]), "late_rows")
+    early = [([first_a], 0, 0), ([crossed_a], 0, 1), ([first_b], CUTS, 0), ([crossed_b], CUTS, 1)], [(second_a, 0, 1)]
+    out, _ = write_rows(core, None, env_in.shape, early, "early_rows")
+    out = last_rows(core, out, moved_a, partials, sums, from_left, from_right, store)
     return out[None]
 
 

time: 86.6 us -> 85 us (0.982)
  waiting for transfers between devices: 12 us -> 7.21 us
  starting transfers between devices: 30.2 us -> 33 us
    ppermute x15 -> x13, waiting for transfers between devices: 12 us -> 7.21 us  [send(): return lax.ppermute(value, axes, pairs)]
    pallas_call x0 -> x1, Pallas kernels: none -> 4.53 us  [last_rows(): pl.pallas_call(kernel, grid_spec=pltpu.PrefetchScalarGridSpec(num_scalar_...]
    ppermute x15 -> x13, starting transfers between devices: 30.2 us -> 33 us  [send(): return lax.ppermute(value, axes, pairs)]
    pallas_call x3 -> x1, Pallas kernels: 4.34 us -> 2.04 us  [write_rows(): pl.pallas_call(kernel, grid_spec=pltpu.PrefetchScalarGridSpec(num_scalar_...]
    pallas_call x4 -> x3, Pallas kernels: 11.5 us -> 9.6 us  [far_terms(): pl.pallas_call(kernel, grid_spec=pltpu.PrefetchScalarGridSpec(num_scalar_...]
  transfers between devices with their start and end apart: 15 -> 13, of which waited for: 10 -> 4; matrix products, arithmetic and copies ran while one was open for 0% -> 0% of each run, Pallas kernels for 45% -> 44%
where the time goes in v2:
time: 85 us; the launch traced here: 84.8 us
  Pallas kernels  43.7 us (51%)
  starting transfers between devices  33 us (39%)
  waiting for transfers between devices  7.21 us (8%)
    ppermute x13, starting transfers between devices, send(): return lax.ppermute(value, axes, pairs)  33 us
    pallas_call x3, Pallas kernels, near_terms(): pl.pallas_call(kernel, grid_spec=pltpu.PrefetchScalarGridSpec(num_scalar_...  21.8 us
    pallas_call x3, Pallas kernels, far_terms(): pl.pallas_call(kernel, grid_spec=pltpu.PrefetchScalarGridSpec(num_scalar_...  9.6 us
    ppermute x13, waiting for transfers between devices, send(): return lax.ppermute(value, axes, pairs)  7.21 us
    pallas_call x1, Pallas kernels, last_rows(): pl.pallas_call(kernel, grid_spec=pltpu.PrefetchScalarGridSpec(num_scalar_...  4.53 us
    pallas_call x1, Pallas kernels, own_store(): pl.pallas_call(kernel, grid_spec=pltpu.PrefetchScalarGridSpec(num_scalar_...  2.16 us
    pallas_call x1, Pallas kernels, write_rows(): pl.pallas_call(kernel, grid_spec=pltpu.PrefetchScalarGridSpec(num_scalar_...  2.04 us
    pallas_call x1, Pallas kernels, edge(): pl.pallas_call(kernel, grid_spec=pltpu.PrefetchScalarGridSpec(num_scalar_...  1.72 us
  transfers between devices with their start and end apart: 13, of which 4 were waited for; matrix products, arithmetic and copies ran while one was open for 0% of the time, Pallas kernels for 44%

profile of v2, /device:TPU:25, one launch (start us, length us, event | category | flops | bytes accessed | tf_op | source)
XLA Modules:
  0.0 84.8 jit_solution(6311426643804375409)
XLA Ops:
  0.0 1.7 %edge.1.after_ref = f32[2,512,512]{2,1,0:T(8,128)S(1)} custom-call(s32[1]{0:T(128)} %bitcast.core_ref, f32[3,2,512,512]{3,2,1,0:T(8,128)} %b_ref.1), custom_call_target="tpu_custom_call" | custom-call | bytes 1024 | tf_op jit(solution)/shard_map/edge/pallas_call | solution.py:83
  1.8 4.2 %collective-permute-start.3 = (f32[2,512,512]{2,1,0:T(8,128)S(1)}, f32[2,512,512]{2,1,0:T(8,128)S(1)}, u32[]{:S(2)}, u32[]{:S(2)}) collective-permute-start(f32[2,512,512]{2,1,0:T(8,128)S(1)} %edge.1.after_ref), channel_id=1, source_target_pairs={{64,1},{65,2},{66,3},{67,4},{68,5},{69,6},{70,7},{71,8},{72,9},{73... | collective-permute-start | bytes 6291464 | tf_op jit(solution)/shard_map/ppermute | solution.py:374
  6.0 0.8 outgoing.1
  6.8 4.4 %collective-permute-start.1 = (f32[512,512]{1,0:T(8,128)S(1)}, f32[512,512]{1,0:T(8,128)S(1)}, u32[]{:S(2)}, u32[]{:S(2)}) collective-permute-start(f32[512,512]{1,0:T(8,128)S(1)} %get-tuple-element.14), channel_id=1, source_target_pairs={{0,64},{1,65},{2,66},{3,67},{4,68},{5,69},{6,70},{7,71},{8,72},{9,... | collective-permute-start | bytes 3145736 | tf_op jit(solution)/shard_map/ppermute | solution.py:374
  11.2 0.1 collective-permute-start.2
  11.3 0.4 collective-permute-start
  11.8 2.2 %own_store.1 = (bf16[7,2,512,512]{3,2,1,0:T(8,128)(2,1)S(1)}, f32[1,512,512]{2,1,0:T(8,128)S(1)}) custom-call(s32[1]{0:T(128)} %bitcast.core_ref, s32[1,2,3]{2,1,0:T(2,128)S(1)} %copy-done.1, s32[1,2,3]{2,1,0:T(2,128)S(1)} %copy-done.2, f32[1,4]{1,0:T(1,128)S(1)} %copy-done.3, f32[1,2,3,512,512]{4,3,2,1,0:T(8,128)S(1)} %copy-done, f32[3,2,512,512]{3,2,1,0:T(8,128)} %b_ref.1, ...), custom_call_target="tpu_custom_call" | custom-call | bytes 1024 | tf_op jit(solution)/shard_map/own_store/pallas_call | solution.py:151
  13.9 1.9 %collective-permute-start.6 = (f32[1,512,512]{2,1,0:T(8,128)S(1)}, f32[1,512,512]{2,1,0:T(8,128)S(1)}, u32[]{:S(2)}, u32[]{:S(2)}) collective-permute-start(f32[1,512,512]{2,1,0:T(8,128)S(1)} %get-tuple-element.17), channel_id=1, source_target_pairs={{64,1},{65,2},{66,3},{67,4},{68,5},{69,6},{70,7},{71,8},{72,9},{73... | collective-permute-start | bytes 3145736 | tf_op jit(solution)/shard_map/ppermute | solution.py:374
  15.9 0.0 collective-permute-done.1.refs_1_
  15.9 0.7 collective-permute-done.refs_0_
  16.5 1.1 %full_store.1.ta_ref.tb_ref.t_ref.refs_6_.refs_7_ = bf16[7,2,512,512]{3,2,1,0:T(8,128)(2,1)S(1)} custom-call(f32[512,512]{1,0:T(8,128)S(1)} %collective-permute-done.refs_0_, f32[512,512]{1,0:T(8,128)S(1)} %collective-permute-done.1.refs_1_, f32[512,512]{1,0:T(8,128)S(1)} %collective-permute-done.2.refs_2_, ...), custom_call_target="tpu_custom_call", output_to_operand_aliasing={{}: (3, {})} | custom-call | bytes 1024 | tf_op jit(solution)/shard_map/full_store/pallas_call | solution.py:180
  17.6 0.5 slice-done.1
  18.1 10.9 %near_terms_0.1.p_ref = f32[3,512,512]{2,1,0:T(8,128)S(1)} custom-call(s32[1]{0:T(128)} %bitcast.core_ref, f32[3,2,512,512]{3,2,1,0:T(8,128)S(1)} %bitcast.3, f32[3,2,512,512]{3,2,1,0:T(8,128)S(1)} %bitcast.3, bf16[7,2,512,512]{3,2,1,0:T(8,128)(2,1)S(1)} %full_store.1.ta_ref.tb_ref.t_ref.refs_6_.refs_7_, ...), custom_call_target="tpu_custom_call" | custom-call | bytes 1024 | tf_op jit(solution)/shard_map/near_terms_0/pallas_call | solution.py:212
  29.0 1.0 %collective-permute-done.3.h_ref = f32[2,512,512]{2,1,0:T(8,128)S(1)} collective-permute-done((f32[2,512,512]{2,1,0:T(8,128)S(1)}, f32[2,512,512]{2,1,0:T(8,128)S(1)}, u32[]{:S(2)}, u32[]{:S(2)}) %collective-permute-start.3) | collective-permute-done | bytes 2097184 | tf_op jit(solution)/shard_map/ppermute | solution.py:374
  30.0 3.8 %far_terms_0.2.a_ref.refs_0_ = f32[2,512,512]{2,1,0:T(8,128)S(1)} custom-call(s32[1]{0:T(128)} %bitcast.core_ref, f32[3,512,512]{2,1,0:T(8,128)S(1)} %near_terms_0.1.p_ref, f32[2,512,512]{2,1,0:T(8,128)S(1)} %collective-permute-done.3.h_ref, bf16[7,2,512,512]{3,2,1,0:T(8,128)(2,1)S(1)} %full_store.1.ta_ref.tb_ref.t_ref.refs_6_.refs_7_), custom_call_target="tpu_custom_call" | custom-call | bytes 1024 | tf_op jit(solution)/shard_map/far_terms_0/pallas_call | solution.py:236
  33.8 3.4 %collective-permute-start.5 = (f32[2,512,512]{2,1,0:T(8,128)S(1)}, f32[2,512,512]{2,1,0:T(8,128)S(1)}, u32[]{:S(2)}, u32[]{:S(2)}) collective-permute-start(f32[2,512,512]{2,1,0:T(8,128)S(1)} %far_terms_0.2.a_ref.refs_0_), channel_id=1, source_target_pairs={{64,1},{65,2},{66,3},{67,4},{68,5},{69,6},{70,7},{71,8},{72,9},{73... | collective-permute-start | bytes 6291464 | tf_op jit(solution)/shard_map/ppermute | solution.py:374
  37.2 8.6 %collective-permute-start.4 = (f32[2,512,512]{2,1,0:T(8,128)S(1)}, f32[2,512,512]{2,1,0:T(8,128)S(1)}, u32[]{:S(2)}, u32[]{:S(2)}) collective-permute-start(f32[2,512,512]{2,1,0:T(8,128)S(1)} %far_terms_0.2.a_ref.refs_0_), channel_id=1, source_target_pairs={{0,64},{1,65},{2,66},{3,67},{4,68},{5,69},{6,70},{7,71},{8,72},{9,... | collective-permute-start | bytes 6291464 | tf_op jit(solution)/shard_map/ppermute | solution.py:374
  45.8 0.0 collective-permute-done.6.h_ref
  45.8 1.9 %far_terms_0.3.a_ref.refs_2_ = f32[1,512,512]{2,1,0:T(8,128)S(1)} custom-call(s32[1]{0:T(128)} %bitcast.core_ref, f32[3,512,512]{2,1,0:T(8,128)S(1)} %near_terms_0.1.p_ref, f32[1,512,512]{2,1,0:T(8,128)S(1)} %collective-permute-done.6.h_ref, bf16[7,2,512,512]{3,2,1,0:T(8,128)(2,1)S(1)} %full_store.1.ta_ref.tb_ref.t_ref.refs_6_.refs_7_, ...), custom_call_target="tpu_custom_call" | custom-call | flops 18400000000 | bytes 1024 | tf_op jit(solution)/shard_map/far_terms_0/pallas_call | solution.py:236
  47.8 0.1 collective-permute-start.7
  47.9 1.3 %collective-permute-start.12 = (f32[1,512,512]{2,1,0:T(8,128)S(1)}, f32[1,512,512]{2,1,0:T(8,128)S(1)}, u32[]{:S(2)}, u32[]{:S(2)}) collective-permute-start(f32[1,512,512]{2,1,0:T(8,128)S(1)} %far_terms_0.3.a_ref.refs_2_), channel_id=1, source_target_pairs={{1,64},{2,65},{3,66},{4,67},{5,68},{6,69},{7,70},{8,71},{9,72},{10... | collective-permute-start | bytes 3145736 | tf_op jit(solution)/shard_map/ppermute | solution.py:374
  49.1 2.1 %collective-permute-start.11 = (f32[1,512,512]{2,1,0:T(8,128)S(1)}, f32[1,512,512]{2,1,0:T(8,128)S(1)}, u32[]{:S(2)}, u32[]{:S(2)}) collective-permute-start(f32[1,512,512]{2,1,0:T(8,128)S(1)} %far_terms_0.3.a_ref.refs_2_), channel_id=1, source_target_pairs={{64,65},{65,66},{66,67},{67,68},{68,69},{69,70},{70,71},{71,72},{7... | collective-permute-start | bytes 3145736 | tf_op jit(solution)/shard_map/ppermute | solution.py:374
  51.3 7.3 %near_terms_1.2.refs_0_.p_ref = f32[2,512,512]{2,1,0:T(8,128)S(1)} custom-call(s32[1]{0:T(128)} %bitcast.core_ref, f32[2,512,512]{2,1,0:T(8,128)S(1)} %far_terms_0.2.a_ref.refs_0_, f32[2,512,512]{2,1,0:T(8,128)S(1)} %collective-permute-done.4.b_ref.refs_1_, bf16[7,2,512,512]{3,2,1,0:T(8,128)(2,1)S(1)} %full_store.1.ta_ref.tb_ref.t_ref.refs_6_.refs_7_, ...), custom_call_target="tpu_custom_call" | custom-call | bytes 1024 | tf_op jit(solution)/shard_map/near_terms_1/pallas_call | solution.py:212
  58.6 3.6 %near_terms_1.3.refs_0_.refs_3_ = f32[1,512,512]{2,1,0:T(8,128)S(1)} custom-call(s32[1]{0:T(128)} %bitcast.core_ref, f32[1,512,512]{2,1,0:T(8,128)S(1)} %far_terms_0.3.a_ref.refs_2_, f32[1,512,512]{2,1,0:T(8,128)S(1)} %collective-permute-done.7.b_ref.refs_3_, bf16[7,2,512,512]{3,2,1,0:T(8,128)(2,1)S(1)} %full_store.1.ta_ref.tb_ref.t_ref.refs_6_.refs_7_, ...), custom_call_target="tpu_custom_call" | custom-call | bytes 1024 | tf_op jit(solution)/shard_map/near_terms_1/pallas_call | solution.py:212
  62.2 1.5 %collective-permute-done.5.h_ref = f32[2,512,512]{2,1,0:T(8,128)S(1)} collective-permute-done((f32[2,512,512]{2,1,0:T(8,128)S(1)}, f32[2,512,512]{2,1,0:T(8,128)S(1)}, u32[]{:S(2)}, u32[]{:S(2)}) %collective-permute-start.5) | collective-permute-done | bytes 2097184 | tf_op jit(solution)/shard_map/ppermute | solution.py:374
  63.7 3.8 %far_terms_1.1 = (f32[2,256,512]{2,1,0:T(8,128)S(1)}, f32[2,256,512]{2,1,0:T(8,128)S(1)}) custom-call(s32[1]{0:T(128)} %bitcast.core_ref, f32[2,512,512]{2,1,0:T(8,128)S(1)} %near_terms_1.2.refs_0_.p_ref, f32[2,512,512]{2,1,0:T(8,128)S(1)} %collective-permute-done.5.h_ref, bf16[7,2,512,512]{3,2,1,0:T(8,128)(2,1)S(1)} %full_store.1.ta_ref.tb_ref.t_ref.refs_6_.refs_7_, ...), custom_call_target="tpu_custom_call" | custom-call | bytes 1024 | tf_op jit(solution)/shard_map/far_terms_1/pallas_call | solution.py:236
  67.6 5.9 %collective-permute-start.8 = (f32[2,256,512]{2,1,0:T(8,128)S(1)}, f32[2,256,512]{2,1,0:T(8,128)S(1)}, u32[]{:S(2)}, u32[]{:S(2)}) collective-permute-start(f32[2,256,512]{2,1,0:T(8,128)S(1)} %get-tuple-element.18.refs_4_), channel_id=1, source_target_pairs={{0,64},{1,65},{2,66},{3,67},{4,68},{5,69},{6,70},{7,71},{8,72},{9,... | collective-permute-start | bytes 3145736 | tf_op jit(solution)/shard_map/ppermute | solution.py:374
  73.5 0.1 collective-permute-start.9
  73.6 0.4 collective-permute-start.10
  74.0 2.0 %early_rows.1 = (f32[3,2,512,512]{3,2,1,0:T(8,128)}, f32[8,128]{1,0:T(8,128)}) custom-call(s32[1]{0:T(128)} %bitcast.core_ref, f32[2,512,512]{2,1,0:T(8,128)S(1)} %far_terms_0.2.a_ref.refs_0_, f32[2,512,512]{2,1,0:T(8,128)S(1)} %collective-permute-done.4.b_ref.refs_1_, f32[1,512,512]{2,1,0:T(8,128)S(1)} %far_terms_0.3.a_ref.refs_2_, ...), custom_call_target="tpu_custom_call" | custom-call | bytes 1024 | tf_op jit(solution)/shard_map/early_rows/pallas_call | solution.py:292
  76.1 4.0 %collective-permute-done.11.refs_4_ = f32[1,512,512]{2,1,0:T(8,128)S(1)} collective-permute-done((f32[1,512,512]{2,1,0:T(8,128)S(1)}, f32[1,512,512]{2,1,0:T(8,128)S(1)}, u32[]{:S(2)}, u32[]{:S(2)}) %collective-permute-start.11) | collective-permute-done | bytes 1048608 | tf_op jit(solution)/shard_map/ppermute | solution.py:374
  80.1 4.5 %last_rows.1 = f32[3,2,512,512]{3,2,1,0:T(8,128)} custom-call(s32[1]{0:T(128)} %bitcast.core_ref, f32[2,256,512]{2,1,0:T(8,128)S(1)} %collective-permute-done.8.refs_0_, f32[2,256,512]{2,1,0:T(8,128)S(1)} %collective-permute-done.9.refs_1_, f32[1,512,512]{2,1,0:T(8,128)S(1)} %collective-permute-done.10.refs_2_, ...), custom_call_target="tpu_custom_call", output_to_operand_aliasing={{}: (9, {})} | custom-call | bytes 1024 | tf_op jit(solution)/shard_map/last_rows/pallas_call | solution.py:342
  (19 shorter events, 0.0 us)
Async XLA Ops:
  0.0 6.0 %copy-start = (f32[1,2,3,512,512]{4,3,2,1,0:T(8,128)S(1)}, f32[1,2,3,512,512]{4,3,2,1,0:T(8,128)}, u32[]{:S(2)}) copy-start(f32[1,2,3,512,512]{4,3,2,1,0:T(8,128)} %t_ref.3) | copy-start | bytes 18874372
  0.0 6.0 %copy-start.1 = (s32[1,2,3]{2,1,0:T(2,128)S(1)}, s32[1,2,3]{2,1,0:T(2,128)}, u32[]{:S(2)}) copy-start(s32[1,2,3]{2,1,0:T(2,128)} %live_ref.3) | copy-start | bytes 76
  0.0 6.0 %copy-start.2 = (s32[1,2,3]{2,1,0:T(2,128)S(1)}, s32[1,2,3]{2,1,0:T(2,128)}, u32[]{:S(2)}) copy-start(s32[1,2,3]{2,1,0:T(2,128)} %index_ref.3) | copy-start | bytes 76
  0.0 6.0 %copy-start.3 = (f32[1,4]{1,0:T(1,128)S(1)}, f32[1,4]{1,0:T(1,128)}, u32[]{:S(2)}) copy-start(f32[1,4]{1,0:T(1,128)} %coef_ref.3) | copy-start | bytes 52
  1.8 28.2 %collective-permute-start.3 = (f32[2,512,512]{2,1,0:T(8,128)S(1)}, f32[2,512,512]{2,1,0:T(8,128)S(1)}, u32[]{:S(2)}, u32[]{:S(2)}) collective-permute-start(f32[2,512,512]{2,1,0:T(8,128)S(1)} %edge.1.after_ref), channel_id=1, source_target_pairs={{64,1},{65,2},{66,3},{67,4},{68,5},{69,6},{70,7},{71,8},{72,9},{73... | collective-permute-start | bytes 6291464 | tf_op jit(solution)/shard_map/ppermute | solution.py:374
  6.8 9.0 %collective-permute-start.1 = (f32[512,512]{1,0:T(8,128)S(1)}, f32[512,512]{1,0:T(8,128)S(1)}, u32[]{:S(2)}, u32[]{:S(2)}) collective-permute-start(f32[512,512]{1,0:T(8,128)S(1)} %get-tuple-element.14), channel_id=1, source_target_pairs={{0,64},{1,65},{2,66},{3,67},{4,68},{5,69},{6,70},{7,71},{8,72},{9,... | collective-permute-start | bytes 3145736 | tf_op jit(solution)/shard_map/ppermute | solution.py:374
  11.2 4.6 %collective-permute-start.2 = (f32[512,512]{1,0:T(8,128)S(1)}, f32[512,512]{1,0:T(8,128)S(1)}, u32[]{:S(2)}, u32[]{:S(2)}) collective-permute-start(f32[512,512]{1,0:T(8,128)S(1)} %get-tuple-element.15), channel_id=1, source_target_pairs={{0,64},{1,65},{2,66},{3,67},{4,68},{5,69},{6,70},{7,71},{8,72},{9,... | collective-permute-start | bytes 3145736 | tf_op jit(solution)/shard_map/ppermute | solution.py:374
  11.3 5.2 %collective-permute-start = (f32[512,512]{1,0:T(8,128)S(1)}, f32[512,512]{1,0:T(8,128)S(1)}, u32[]{:S(2)}, u32[]{:S(2)}) collective-permute-start(f32[512,512]{1,0:T(8,128)S(1)} %get-tuple-element.13.after_ref), channel_id=1, source_target_pairs={{0,64},{1,65},{2,66},{3,67},{4,68},{5,69},{6,70},{7,71},{8,72},{9,... | collective-permute-start | bytes 3145736 | tf_op jit(solution)/shard_map/ppermute | solution.py:374
  11.8 5.9 %slice-start = ((s8[6291456]{0:T(1024)(128)(4,1)}), s8[4194304]{0:T(1024)(128)(4,1)S(1)}, s32[]{:S(2)}) async-start(s8[6291456]{0:T(1024)(128)(4,1)} %bitcast.2), calls=%async_computation | async-start | bytes 8388608
  13.9 31.9 %collective-permute-start.6 = (f32[1,512,512]{2,1,0:T(8,128)S(1)}, f32[1,512,512]{2,1,0:T(8,128)S(1)}, u32[]{:S(2)}, u32[]{:S(2)}) collective-permute-start(f32[1,512,512]{2,1,0:T(8,128)S(1)} %get-tuple-element.17), channel_id=1, source_target_pairs={{64,1},{65,2},{66,3},{67,4},{68,5},{69,6},{70,7},{71,8},{72,9},{73... | collective-permute-start | bytes 3145736 | tf_op jit(solution)/shard_map/ppermute | solution.py:374
  16.5 1.6 %slice-start.1 = ((s8[6291456]{0:T(1024)(128)(4,1)}), s8[2097152]{0:T(1024)(128)(4,1)S(1)}, s32[]{:S(2)}) async-start(s8[6291456]{0:T(1024)(128)(4,1)} %bitcast.2), calls=%async_computation.1 | async-start | bytes 4194304
  33.8 29.9 %collective-permute-start.5 = (f32[2,512,512]{2,1,0:T(8,128)S(1)}, f32[2,512,512]{2,1,0:T(8,128)S(1)}, u32[]{:S(2)}, u32[]{:S(2)}) collective-permute-start(f32[2,512,512]{2,1,0:T(8,128)S(1)} %far_terms_0.2.a_ref.refs_0_), channel_id=1, source_target_pairs={{64,1},{65,2},{66,3},{67,4},{68,5},{69,6},{70,7},{71,8},{72,9},{73... | collective-permute-start | bytes 6291464 | tf_op jit(solution)/shard_map/ppermute | solution.py:374
  37.2 14.0 %collective-permute-start.4 = (f32[2,512,512]{2,1,0:T(8,128)S(1)}, f32[2,512,512]{2,1,0:T(8,128)S(1)}, u32[]{:S(2)}, u32[]{:S(2)}) collective-permute-start(f32[2,512,512]{2,1,0:T(8,128)S(1)} %far_terms_0.2.a_ref.refs_0_), channel_id=1, source_target_pairs={{0,64},{1,65},{2,66},{3,67},{4,68},{5,69},{6,70},{7,71},{8,72},{9,... | collective-permute-start | bytes 6291464 | tf_op jit(solution)/shard_map/ppermute | solution.py:374
  47.8 10.8 %collective-permute-start.7 = (f32[1,512,512]{2,1,0:T(8,128)S(1)}, f32[1,512,512]{2,1,0:T(8,128)S(1)}, u32[]{:S(2)}, u32[]{:S(2)}) collective-permute-start(f32[1,512,512]{2,1,0:T(8,128)S(1)} %far_terms_0.3.a_ref.refs_2_), channel_id=1, source_target_pairs={{0,64},{1,65},{2,66},{3,67},{4,68},{5,69},{6,70},{7,71},{8,72},{9,... | collective-permute-start | bytes 3145736 | tf_op jit(solution)/shard_map/ppermute | solution.py:374
  47.9 28.2 %collective-permute-start.12 = (f32[1,512,512]{2,1,0:T(8,128)S(1)}, f32[1,512,512]{2,1,0:T(8,128)S(1)}, u32[]{:S(2)}, u32[]{:S(2)}) collective-permute-start(f32[1,512,512]{2,1,0:T(8,128)S(1)} %far_terms_0.3.a_ref.refs_2_), channel_id=1, source_target_pairs={{1,64},{2,65},{3,66},{4,67},{5,68},{6,69},{7,70},{8,71},{9,72},{10... | collective-permute-start | bytes 3145736 | tf_op jit(solution)/shard_map/ppermute | solution.py:374
  49.1 31.0 %collective-permute-start.11 = (f32[1,512,512]{2,1,0:T(8,128)S(1)}, f32[1,512,512]{2,1,0:T(8,128)S(1)}, u32[]{:S(2)}, u32[]{:S(2)}) collective-permute-start(f32[1,512,512]{2,1,0:T(8,128)S(1)} %far_terms_0.3.a_ref.refs_2_), channel_id=1, source_target_pairs={{64,65},{65,66},{66,67},{67,68},{68,69},{69,70},{70,71},{71,72},{7... | collective-permute-start | bytes 3145736 | tf_op jit(solution)/shard_map/ppermute | solution.py:374
  67.6 12.5 %collective-permute-start.8 = (f32[2,256,512]{2,1,0:T(8,128)S(1)}, f32[2,256,512]{2,1,0:T(8,128)S(1)}, u32[]{:S(2)}, u32[]{:S(2)}) collective-permute-start(f32[2,256,512]{2,1,0:T(8,128)S(1)} %get-tuple-element.18.refs_4_), channel_id=1, source_target_pairs={{0,64},{1,65},{2,66},{3,67},{4,68},{5,69},{6,70},{7,71},{8,72},{9,... | collective-permute-start | bytes 3145736 | tf_op jit(solution)/shard_map/ppermute | solution.py:374
  73.5 6.6 %collective-permute-start.9 = (f32[2,256,512]{2,1,0:T(8,128)S(1)}, f32[2,256,512]{2,1,0:T(8,128)S(1)}, u32[]{:S(2)}, u32[]{:S(2)}) collective-permute-start(f32[2,256,512]{2,1,0:T(8,128)S(1)} %get-tuple-element.19.refs_5_), channel_id=1, source_target_pairs={{0,64},{1,65},{2,66},{3,67},{4,68},{5,69},{6,70},{7,71},{8,72},{9,... | collective-permute-start | bytes 3145736 | tf_op jit(solution)/shard_map/ppermute | solution.py:374
  73.6 6.5 %collective-permute-start.10 = (f32[1,512,512]{2,1,0:T(8,128)S(1)}, f32[1,512,512]{2,1,0:T(8,128)S(1)}, u32[]{:S(2)}, u32[]{:S(2)}) collective-permute-start(f32[1,512,512]{2,1,0:T(8,128)S(1)} %near_terms_1.3.refs_0_.refs_3_), channel_id=1, source_target_pairs={{0,64},{1,65},{2,66},{3,67},{4,68},{5,69},{6,70},{7,71},{8,72},{9,... | collective-permute-start | bytes 3145736 | tf_op jit(solution)/shard_map/ppermute | solution.py:374

commit v3 on v2

--- a/solution.py
+++ b/solution.py
@@ -13,6 +13,7 @@
 
 STORE = 7
 CUTS = 2
+SWAPS = 4
 PARTS = 1
 HALVES = 2
 
@@ -71,7 +72,7 @@
 
     def kernel(core_ref, e_ref, o_ref, sems):
         copies = []
-        for n in range(CUTS):
+        for n in range(1):
             for p in range(parts):
                 span = pl.ds(p * rows, rows)
                 copies.append(pltpu.make_async_copy(e_ref.at[n, core_ref[0], span], o_ref.at[n, span], sems.at[n * parts + p]))
@@ -87,9 +88,9 @@
             grid=(1,),
             in_specs=[HBM_REF],
             out_specs=pl.BlockSpec(memory_space=pltpu.VMEM),
-            scratch_shapes=[pltpu.SemaphoreType.DMA((CUTS * parts,))],
-        ),
-        out_shape=jax.ShapeDtypeStruct((CUTS, width, width), F32),
+            scratch_shapes=[pltpu.SemaphoreType.DMA((parts,))],
+        ),
+        out_shape=jax.ShapeDtypeStruct((1, width, width), F32),
         compiler_params=params(),
         cost_estimate=cost(),
         name="edge",
@@ -98,12 +99,15 @@
 
 def outgoing(core, scalars, tensors, after):
     width = tensors.shape[-1]
+    rows = width // SWAPS
 
     def kernel(core_ref, live_ref, index_ref, coef_ref, t_ref, after_ref, *o_refs):
         other = 1 - core_ref[0]
-        for k, o_ref in enumerate(o_refs):
+        for k in range(3):
             slot = slot_at(k, other)
-            o_ref[...] = t_ref[0, 0, slot] * root(live_ref, index_ref, coef_ref, other, slot, width)
+            scaled = t_ref[0, 0, slot] * root(live_ref, index_ref, coef_ref, other, slot, width)
+            for p, o_ref in enumerate(o_refs):
+                o_ref[k] = scaled[p * rows : (p + 1) * rows]
 
     return pl.pallas_call(
         kernel,
@@ -111,9 +115,9 @@
             num_scalar_prefetch=1,
             grid=(1,),
             in_specs=SCALARS + [pl.BlockSpec((1, 1, 3, width, width), lambda k, c: (0, 1 - c[0], 0, 0, 0)), HBM_REF],
-            out_specs=[pl.BlockSpec((width, width), lambda k, c: (0, 0))] * 3,
-        ),
-        out_shape=[jax.ShapeDtypeStruct((width, width), F32)] * 3,
+            out_specs=[pl.BlockSpec((3, rows, width), lambda k, c: (0, 0, 0))] * SWAPS,
+        ),
+        out_shape=[jax.ShapeDtypeStruct((3, rows, width), F32)] * SWAPS,
         compiler_params=params(),
         cost_estimate=cost(),
         name="outgoing",
@@ -131,8 +135,7 @@
         copies = []
         for p in range(parts):
             span = pl.ds(p * (width // parts), width // parts)
-            for n in range(3 - CUTS):
-                copies.append(pltpu.make_async_copy(e_ref.at[CUTS + n, c, span], edge_ref.at[n, span], sems.at[n * parts + p]))
+            copies.append(pltpu.make_async_copy(e_ref.at[1, c, span], edge_ref.at[0, span], sems.at[p]))
 
         @pl.when(k == 0)
         def _():
@@ -155,43 +158,60 @@
             grid=(4,),
             in_specs=SCALARS + [pl.BlockSpec((1, 1, 1, width, width), lambda k, c: (0, jnp.where(k < 3, c[0], 1 - c[0]), jnp.where(k < 3, slot_at(k, c[0]), 0), 0, 0)), HBM_REF, HBM_REF],
             out_specs=[pl.BlockSpec((1, 2, width, width), lambda k, c: (jnp.where(k < 3, k, 6), 0, 0, 0)), pl.BlockSpec(memory_space=pltpu.VMEM)],
-            scratch_shapes=[pltpu.SemaphoreType.DMA((4 * (3 - CUTS),))],
-        ),
-        out_shape=[jax.ShapeDtypeStruct((STORE, 2, width, width), BF16), jax.ShapeDtypeStruct((3 - CUTS, width, width), F32)],
+            scratch_shapes=[pltpu.SemaphoreType.DMA((4,))],
+        ),
+        out_shape=[jax.ShapeDtypeStruct((STORE, 2, width, width), BF16), jax.ShapeDtypeStruct((1, width, width), F32)],
         compiler_params=params(),
         cost_estimate=cost(),
         name="own_store",
     )(core, *scalars, tensors, env, after)
 
 
-def full_store(store, received):
+def full_store(core, store, received, env):
     width = store.shape[-1]
-
-    def kernel(*refs):
-        o_ref = refs[-1]
-        for k in range(3):
-
-            @pl.when(pl.program_id(0) == k)
-            def _():
-                high, low = split(refs[k][...].T)
-                o_ref[0, 0] = high
-                o_ref[0, 1] = low
-
-    return pl.pallas_call(
-        kernel,
-        grid=(3,),
-        in_specs=[pl.BlockSpec((width, width), lambda k: (0, 0))] * 3 + [HBM_REF],
-        out_specs=pl.BlockSpec((1, 2, width, width), lambda k: (k + 3, 0, 0, 0)),
-        out_shape=jax.ShapeDtypeStruct(store.shape, BF16),
-        input_output_aliases={3: 0},
+    rows = width // SWAPS
+
+    def kernel(core_ref, *refs):
+        blocks, (_, e_ref, o_ref, edge_ref, sems) = refs[:SWAPS], refs[SWAPS:]
+        k = pl.program_id(0)
+        copies = []
+        for p in range(SWAPS):
+            span = pl.ds(p * rows, rows)
+            copies.append(pltpu.make_async_copy(e_ref.at[2, core_ref[0], span], edge_ref.at[0, span], sems.at[p]))
+
+        @pl.when(k == 0)
+        def _():
+            for copy in copies:
+                copy.start()
+
+        high, low = split(jnp.concatenate([block[0] for block in blocks], 0).T)
+        o_ref[0, 0] = high
+        o_ref[0, 1] = low
+
+        @pl.when(k == 2)
+        def _():
+            for copy in copies:
+                copy.wait()
+
+    return pl.pallas_call(
+        kernel,
+        grid_spec=pltpu.PrefetchScalarGridSpec(
+            num_scalar_prefetch=1,
+            grid=(3,),
+            in_specs=[pl.BlockSpec((1, rows, width), lambda k, c: (k, 0, 0))] * SWAPS + [HBM_REF, HBM_REF],
+            out_specs=[pl.BlockSpec((1, 2, width, width), lambda k, c: (k + 3, 0, 0, 0)), pl.BlockSpec(memory_space=pltpu.VMEM)],
+            scratch_shapes=[pltpu.SemaphoreType.DMA((SWAPS,))],
+        ),
+        out_shape=[jax.ShapeDtypeStruct(store.shape, BF16), jax.ShapeDtypeStruct((1, width, width), F32)],
+        input_output_aliases={SWAPS + 1: 0},
         compiler_params=params(),
         cost_estimate=cost(),
         name="full_store",
-    )(*received, store)
-
-
-def near_terms(core, site, own, other, in_env, store, parts, after):
-    states, width = own.shape[0], own.shape[-1]
+    )(core, *received, store, env)
+
+
+def near_terms(core, site, own, other, in_env, store, parts, after, first=0, states=None):
+    states, width = states or own.shape[0], own.shape[-1]
     rows = width // parts
 
     def kernel(core_ref, a_ref, b_ref, ta_ref, tb_ref, *refs):
@@ -207,7 +227,7 @@
     sources = [row, row]
     if in_env:
         block = (1, 1, width, width)
-        sources = [pl.BlockSpec(block, lambda n, c: (n, c[0], 0, 0)), pl.BlockSpec(block, lambda n, c: (n, 1 - c[0], 0, 0))]
+        sources = [pl.BlockSpec(block, lambda n, c: (n + first, c[0], 0, 0)), pl.BlockSpec(block, lambda n, c: (n + first, 1 - c[0], 0, 0))]
     pair = (1, 2, width, width)
     return pl.pallas_call(
         kernel,
@@ -251,6 +271,34 @@
         cost_estimate=cost(weight),
         name=f"far_terms_{site}",
     )(core, partial, halo, store, *after)
+
+
+def far_pair(core, partial, done, halo, store, weight):
+    width = halo.shape[-1]
+
+    def kernel(core_ref, p_ref, d_ref, h_ref, t_ref, o_ref):
+        o_ref[0] = d_ref[0]
+        o_ref[1] = p_ref[0] + sandwich(h_ref[0], t_ref[0, 0], t_ref[0, 1])
+
+    row = pl.BlockSpec((1, width, width), lambda n, c: (0, 0, 0))
+    return pl.pallas_call(
+        kernel,
+        grid_spec=pltpu.PrefetchScalarGridSpec(
+            num_scalar_prefetch=1,
+            grid=(1,),
+            in_specs=[
+                pl.BlockSpec((1, width, width), lambda n, c: (1, 0, 0)),
+                row,
+                row,
+                pl.BlockSpec((1, 2, width, width), lambda n, c: (3 * c[0] + 2, 0, 0, 0)),
+            ],
+            out_specs=pl.BlockSpec((2, width, width), lambda n, c: (0, 0, 0)),
+        ),
+        out_shape=jax.ShapeDtypeStruct((2, width, width), F32),
+        compiler_params=params(),
+        cost_estimate=cost(weight),
+        name="far_pair",
+    )(core, partial, done, halo, store)
 
 
 def write_rows(core, out, shape, moves, name):
@@ -375,18 +423,21 @@
 
     scalars = (pair_live, coef_index, mpo_coef)
     pinned = pltpu.with_memory_space_constraint(env_in, pltpu.HBM)
-    edge_a = edge(core, pinned)
-    halo_a = send(edge_a, meet)
-    leaving = outgoing(core, scalars, site_tensor, edge_a)
+    edge_0 = edge(core, pinned)
+    halo_0 = send(edge_0, meet)
+    leaving = outgoing(core, scalars, site_tensor, edge_0)
     received = [send(block, swap) for block in leaving]
-    store, edge_b = own_store(core, scalars, site_tensor, pinned, leaving[0])
-    halo_b = send(edge_b, meet)
-    store = full_store(store, received)
-
-    (near,) = near_terms(core, 0, env_in, env_in, True, store, 1, [])
-    (first_a,) = far_terms(core, 0, near, 0, halo_a, store, 1, 0, [])
+    store, edge_1 = own_store(core, scalars, site_tensor, pinned, leaving[0])
+    halo_1 = send(edge_1, meet)
+    store, edge_2 = full_store(core, store, received, pinned)
+    halo_2 = send(edge_2, meet)
+
+    (near_01,) = near_terms(core, 0, env_in, env_in, True, store, 1, [], 0, CUTS)
+    (first_0,) = far_terms(core, 0, near_01, 0, halo_0, store, 1, 16, [])
+    first_a = far_pair(core, near_01, first_0, halo_1, store, 0)
     second_halo_a, crossed_a = send(first_a, meet), send(first_a, swap)
-    (first_b,) = far_terms(core, 0, near, CUTS, halo_b, store, 1, 16, [first_a])
+    (near_2,) = near_terms(core, 0, env_in, env_in, True, store, 1, [first_a], CUTS, 3 - CUTS)
+    (first_b,) = far_terms(core, 0, near_2, 0, halo_2, store, 1, 0, [first_a])
     from_left, from_right, crossed_b = send(first_b, to_right), send(first_b, to_left), send(first_b, swap)
 
     (near_a,) = near_terms(core, 1, first_a, crossed_a, False, store, 1, [])

time: 85 us -> 84 us (0.988)
  waiting for transfers between devices: 7.21 us -> 5.48 us
    pallas_call x1 -> x2, Pallas kernels: 1.07 us -> 3.38 us  [the longest x1 2.01 us: far_pair(): pl.pallas_call(kernel, grid_spec=pltpu.PrefetchScalarGridSpec(num_scalar_...]
    pallas_call x3, Pallas kernels: 9.6 us -> 7.69 us  [far_terms(): pl.pallas_call(kernel, grid_spec=pltpu.PrefetchScalarGridSpec(num_scalar_...]
    ppermute x13 -> x15, waiting for transfers between devices: 7.21 us -> 5.48 us  [send(): return lax.ppermute(value, axes, pairs)]
    ppermute x13 -> x15, starting transfers between devices: 33 us -> 33.8 us  [send(): return lax.ppermute(value, axes, pairs)]
    pallas_call x3 -> x4, Pallas kernels: 21.8 us -> 21.8 us  [near_terms(): pl.pallas_call(kernel, grid_spec=pltpu.PrefetchScalarGridSpec(num_scalar_...]
  transfers between devices with their start and end apart: 13 -> 15, of which waited for: 4 -> 5; matrix products, arithmetic and copies ran while one was open for 0% -> 0% of each run, Pallas kernels for 44% -> 45%
where the time goes in v3:
time: 84 us; the launch traced here: 83.8 us
  Pallas kernels  44 us (52%)
  starting transfers between devices  33.8 us (40%)
  waiting for transfers between devices  5.48 us (7%)
    ppermute x15, starting transfers between devices, send(): return lax.ppermute(value, axes, pairs)  33.8 us
    pallas_call x4, Pallas kernels, near_terms(): pl.pallas_call(kernel, grid_spec=pltpu.PrefetchScalarGridSpec(num_scalar_...  21.8 us
    pallas_call x3, Pallas kernels, far_terms(): pl.pallas_call(kernel, grid_spec=pltpu.PrefetchScalarGridSpec(num_scalar_...  7.69 us
    ppermute x15, waiting for transfers between devices, send(): return lax.ppermute(value, axes, pairs)  5.48 us
    pallas_call x1, Pallas kernels, last_rows(): pl.pallas_call(kernel, grid_spec=pltpu.PrefetchScalarGridSpec(num_scalar_...  4.74 us
    pallas_call x1, Pallas kernels, own_store(): pl.pallas_call(kernel, grid_spec=pltpu.PrefetchScalarGridSpec(num_scalar_...  2.16 us
    pallas_call x1, Pallas kernels, write_rows(): pl.pallas_call(kernel, grid_spec=pltpu.PrefetchScalarGridSpec(num_scalar_...  2.03 us
    pallas_call x1, Pallas kernels, far_pair(): pl.pallas_call(kernel, grid_spec=pltpu.PrefetchScalarGridSpec(num_scalar_...  2.01 us
  transfers between devices with their start and end apart: 15, of which 5 were waited for; matrix products, arithmetic and copies ran while one was open for 0% of the time, Pallas kernels for 45%

profile of v3, /device:TPU:25, one launch (start us, length us, event | category | flops | bytes accessed | tf_op | source)
XLA Modules:
  0.0 83.8 jit_solution(10328728921707701412)
XLA Ops:
  0.0 1.4 %edge.1.after_ref = f32[1,512,512]{2,1,0:T(8,128)S(1)} custom-call(s32[1]{0:T(128)} %bitcast.core_ref, f32[3,2,512,512]{3,2,1,0:T(8,128)} %b_ref.3), custom_call_target="tpu_custom_call" | custom-call | bytes 1024 | tf_op jit(solution)/shard_map/edge/pallas_call | solution.py:84
  1.4 4.2 %collective-permute-start.4 = (f32[1,512,512]{2,1,0:T(8,128)S(1)}, f32[1,512,512]{2,1,0:T(8,128)S(1)}, u32[]{:S(2)}, u32[]{:S(2)}) collective-permute-start(f32[1,512,512]{2,1,0:T(8,128)S(1)} %edge.1.after_ref), channel_id=1, source_target_pairs={{64,1},{65,2},{66,3},{67,4},{68,5},{69,6},{70,7},{71,8},{72,9},{73... | collective-permute-start | bytes 3145736 | tf_op jit(solution)/shard_map/ppermute | solution.py:422
  5.7 0.8 outgoing.1
  6.5 4.4 %collective-permute-start.1 = (f32[3,128,512]{2,1,0:T(8,128)S(1)}, f32[3,128,512]{2,1,0:T(8,128)S(1)}, u32[]{:S(2)}, u32[]{:S(2)}) collective-permute-start(f32[3,128,512]{2,1,0:T(8,128)S(1)} %get-tuple-element.17), channel_id=1, source_target_pairs={{0,64},{1,65},{2,66},{3,67},{4,68},{5,69},{6,70},{7,71},{8,72},{9,... | collective-permute-start | bytes 2359304 | tf_op jit(solution)/shard_map/ppermute | solution.py:422
  11.0 0.4 collective-permute-start.3
  11.4 0.1 collective-permute-start
  11.5 2.2 %own_store.1 = (bf16[7,2,512,512]{3,2,1,0:T(8,128)(2,1)S(1)}, f32[1,512,512]{2,1,0:T(8,128)S(1)}) custom-call(s32[1]{0:T(128)} %bitcast.core_ref, s32[1,2,3]{2,1,0:T(2,128)S(1)} %copy-done.1, s32[1,2,3]{2,1,0:T(2,128)S(1)} %copy-done.2, f32[1,4]{1,0:T(1,128)S(1)} %copy-done.3, f32[1,2,3,512,512]{4,3,2,1,0:T(8,128)S(1)} %copy-done, f32[3,2,512,512]{3,2,1,0:T(8,128)} %b_ref.3, ...), custom_call_target="tpu_custom_call" | custom-call | bytes 1024 | tf_op jit(solution)/shard_map/own_store/pallas_call | solution.py:154
  13.7 1.9 %collective-permute-start.5 = (f32[1,512,512]{2,1,0:T(8,128)S(1)}, f32[1,512,512]{2,1,0:T(8,128)S(1)}, u32[]{:S(2)}, u32[]{:S(2)}) collective-permute-start(f32[1,512,512]{2,1,0:T(8,128)S(1)} %get-tuple-element.22), channel_id=1, source_target_pairs={{64,1},{65,2},{66,3},{67,4},{68,5},{69,6},{70,7},{71,8},{72,9},{73... | collective-permute-start | bytes 3145736 | tf_op jit(solution)/shard_map/ppermute | solution.py:422
  15.6 0.6 collective-permute-done.refs_0_
  16.2 1.4 %full_store.1 = (bf16[7,2,512,512]{3,2,1,0:T(8,128)(2,1)S(1)}, f32[1,512,512]{2,1,0:T(8,128)S(1)}) custom-call(s32[1]{0:T(128)} %bitcast.core_ref, f32[3,128,512]{2,1,0:T(8,128)S(1)} %collective-permute-done.refs_0_, f32[3,128,512]{2,1,0:T(8,128)S(1)} %collective-permute-done.1.refs_1_, ...), custom_call_target="tpu_custom_call", output_to_operand_aliasing={{0}: (5, {})} | custom-call | bytes 1024 | tf_op jit(solution)/shard_map/full_store/pallas_call | solution.py:196
  17.6 3.1 %collective-permute-start.8 = (f32[1,512,512]{2,1,0:T(8,128)S(1)}, f32[1,512,512]{2,1,0:T(8,128)S(1)}, u32[]{:S(2)}, u32[]{:S(2)}) collective-permute-start(f32[1,512,512]{2,1,0:T(8,128)S(1)} %get-tuple-element.23), channel_id=1, source_target_pairs={{64,1},{65,2},{66,3},{67,4},{68,5},{69,6},{70,7},{71,8},{72,9},{73... | collective-permute-start | bytes 3145736 | tf_op jit(solution)/shard_map/ppermute | solution.py:422
  20.7 7.3 %near_terms_0.2.p_ref = f32[2,512,512]{2,1,0:T(8,128)S(1)} custom-call(s32[1]{0:T(128)} %bitcast.core_ref, f32[3,2,512,512]{3,2,1,0:T(8,128)S(1)} %bitcast.3, f32[3,2,512,512]{3,2,1,0:T(8,128)S(1)} %bitcast.3, bf16[7,2,512,512]{3,2,1,0:T(8,128)(2,1)S(1)} %get-tuple-element.21.ta_ref.tb_ref.t_ref.refs_6_.refs_7_, ...), custom_call_target="tpu_custom_call" | custom-call | bytes 1024 | tf_op jit(solution)/shard_map/near_terms_0/pallas_call | solution.py:232
  28.0 1.9 %far_terms_0.2.d_ref = f32[1,512,512]{2,1,0:T(8,128)S(1)} custom-call(s32[1]{0:T(128)} %bitcast.core_ref, f32[2,512,512]{2,1,0:T(8,128)S(1)} %near_terms_0.2.p_ref, f32[1,512,512]{2,1,0:T(8,128)S(1)} %collective-permute-done.4.h_ref, bf16[7,2,512,512]{3,2,1,0:T(8,128)(2,1)S(1)} %get-tuple-element.21.ta_ref.tb_ref.t_ref.refs_6_.refs_7_), custom_call_target="tpu_custom_call" | custom-call | flops 18400000000 | bytes 1024 | tf_op jit(solution)/shard_map/far_terms_0/pallas_call | solution.py:256
  30.0 0.1 collective-permute-done.5.h_ref
  30.1 2.0 %far_pair.1.a_ref.refs_0_ = f32[2,512,512]{2,1,0:T(8,128)S(1)} custom-call(s32[1]{0:T(128)} %bitcast.core_ref, f32[2,512,512]{2,1,0:T(8,128)S(1)} %near_terms_0.2.p_ref, f32[1,512,512]{2,1,0:T(8,128)S(1)} %far_terms_0.2.d_ref, f32[1,512,512]{2,1,0:T(8,128)S(1)} %collective-permute-done.5.h_ref, ...), custom_call_target="tpu_custom_call" | custom-call | bytes 1024 | tf_op jit(solution)/shard_map/far_pair/pallas_call | solution.py:284
  32.1 4.6 %collective-permute-start.6 = (f32[2,512,512]{2,1,0:T(8,128)S(1)}, f32[2,512,512]{2,1,0:T(8,128)S(1)}, u32[]{:S(2)}, u32[]{:S(2)}) collective-permute-start(f32[2,512,512]{2,1,0:T(8,128)S(1)} %far_pair.1.a_ref.refs_0_), channel_id=1, source_target_pairs={{0,64},{1,65},{2,66},{3,67},{4,68},{5,69},{6,70},{7,71},{8,72},{9,... | collective-permute-start | bytes 6291464 | tf_op jit(solution)/shard_map/ppermute | solution.py:422
  36.7 2.1 %collective-permute-start.7 = (f32[2,512,512]{2,1,0:T(8,128)S(1)}, f32[2,512,512]{2,1,0:T(8,128)S(1)}, u32[]{:S(2)}, u32[]{:S(2)}) collective-permute-start(f32[2,512,512]{2,1,0:T(8,128)S(1)} %far_pair.1.a_ref.refs_0_), channel_id=1, source_target_pairs={{64,1},{65,2},{66,3},{67,4},{68,5},{69,6},{70,7},{71,8},{72,9},{73... | collective-permute-start | bytes 6291464 | tf_op jit(solution)/shard_map/ppermute | solution.py:422
  38.8 3.6 %near_terms_0.3.p_ref = f32[1,512,512]{2,1,0:T(8,128)S(1)} custom-call(s32[1]{0:T(128)} %bitcast.core_ref, f32[3,2,512,512]{3,2,1,0:T(8,128)S(1)} %bitcast.3, f32[3,2,512,512]{3,2,1,0:T(8,128)S(1)} %bitcast.3, bf16[7,2,512,512]{3,2,1,0:T(8,128)(2,1)S(1)} %get-tuple-element.21.ta_ref.tb_ref.t_ref.refs_6_.refs_7_, ...), custom_call_target="tpu_custom_call" | custom-call | bytes 1024 | tf_op jit(solution)/shard_map/near_terms_0/pallas_call | solution.py:232
  42.5 1.9 %far_terms_0.3.a_ref.refs_2_ = f32[1,512,512]{2,1,0:T(8,128)S(1)} custom-call(s32[1]{0:T(128)} %bitcast.core_ref, f32[1,512,512]{2,1,0:T(8,128)S(1)} %near_terms_0.3.p_ref, f32[1,512,512]{2,1,0:T(8,128)S(1)} %collective-permute-done.8.h_ref, bf16[7,2,512,512]{3,2,1,0:T(8,128)(2,1)S(1)} %get-tuple-element.21.ta_ref.tb_ref.t_ref.refs_6_.refs_7_, ...), custom_call_target="tpu_custom_call" | custom-call | bytes 1024 | tf_op jit(solution)/shard_map/far_terms_0/pallas_call | solution.py:256
  44.4 5.1 %collective-permute-start.9 = (f32[1,512,512]{2,1,0:T(8,128)S(1)}, f32[1,512,512]{2,1,0:T(8,128)S(1)}, u32[]{:S(2)}, u32[]{:S(2)}) collective-permute-start(f32[1,512,512]{2,1,0:T(8,128)S(1)} %far_terms_0.3.a_ref.refs_2_), channel_id=1, source_target_pairs={{0,64},{1,65},{2,66},{3,67},{4,68},{5,69},{6,70},{7,71},{8,72},{9,... | collective-permute-start | bytes 3145736 | tf_op jit(solution)/shard_map/ppermute | solution.py:422
  49.5 1.3 %collective-permute-start.14 = (f32[1,512,512]{2,1,0:T(8,128)S(1)}, f32[1,512,512]{2,1,0:T(8,128)S(1)}, u32[]{:S(2)}, u32[]{:S(2)}) collective-permute-start(f32[1,512,512]{2,1,0:T(8,128)S(1)} %far_terms_0.3.a_ref.refs_2_), channel_id=1, source_target_pairs={{1,64},{2,65},{3,66},{4,67},{5,68},{6,69},{7,70},{8,71},{9,72},{10... | collective-permute-start | bytes 3145736 | tf_op jit(solution)/shard_map/ppermute | solution.py:422
  50.8 1.9 %collective-permute-start.13 = (f32[1,512,512]{2,1,0:T(8,128)S(1)}, f32[1,512,512]{2,1,0:T(8,128)S(1)}, u32[]{:S(2)}, u32[]{:S(2)}) collective-permute-start(f32[1,512,512]{2,1,0:T(8,128)S(1)} %far_terms_0.3.a_ref.refs_2_), channel_id=1, source_target_pairs={{64,65},{65,66},{66,67},{67,68},{68,69},{69,70},{70,71},{71,72},{7... | collective-permute-start | bytes 3145736 | tf_op jit(solution)/shard_map/ppermute | solution.py:422
  52.7 7.3 %near_terms_1.2.refs_0_.p_ref = f32[2,512,512]{2,1,0:T(8,128)S(1)} custom-call(s32[1]{0:T(128)} %bitcast.core_ref, f32[2,512,512]{2,1,0:T(8,128)S(1)} %far_pair.1.a_ref.refs_0_, f32[2,512,512]{2,1,0:T(8,128)S(1)} %collective-permute-done.6.b_ref.refs_1_, bf16[7,2,512,512]{3,2,1,0:T(8,128)(2,1)S(1)} %get-tuple-element.21.ta_ref.tb_ref.t_ref.refs_6_.refs_7_, ...), custom_call_target="tpu_custom_call" | custom-call | bytes 1024 | tf_op jit(solution)/shard_map/near_terms_1/pallas_call | solution.py:232
  60.0 3.6 %near_terms_1.3.refs_0_.refs_3_ = f32[1,512,512]{2,1,0:T(8,128)S(1)} custom-call(s32[1]{0:T(128)} %bitcast.core_ref, f32[1,512,512]{2,1,0:T(8,128)S(1)} %far_terms_0.3.a_ref.refs_2_, f32[1,512,512]{2,1,0:T(8,128)S(1)} %collective-permute-done.9.b_ref.refs_3_, bf16[7,2,512,512]{3,2,1,0:T(8,128)(2,1)S(1)} %get-tuple-element.21.ta_ref.tb_ref.t_ref.refs_6_.refs_7_, ...), custom_call_target="tpu_custom_call" | custom-call | bytes 1024 | tf_op jit(solution)/shard_map/near_terms_1/pallas_call | solution.py:232
  63.6 0.7 collective-permute-done.7.h_ref
  64.4 3.9 %far_terms_1.1 = (f32[2,256,512]{2,1,0:T(8,128)S(1)}, f32[2,256,512]{2,1,0:T(8,128)S(1)}) custom-call(s32[1]{0:T(128)} %bitcast.core_ref, f32[2,512,512]{2,1,0:T(8,128)S(1)} %near_terms_1.2.refs_0_.p_ref, f32[2,512,512]{2,1,0:T(8,128)S(1)} %collective-permute-done.7.h_ref, bf16[7,2,512,512]{3,2,1,0:T(8,128)(2,1)S(1)} %get-tuple-element.21.ta_ref.tb_ref.t_ref.refs_6_.refs_7_, ...), custom_call_target="tpu_custom_call" | custom-call | bytes 1024 | tf_op jit(solution)/shard_map/far_terms_1/pallas_call | solution.py:256
  68.2 4.0 %collective-permute-start.10 = (f32[2,256,512]{2,1,0:T(8,128)S(1)}, f32[2,256,512]{2,1,0:T(8,128)S(1)}, u32[]{:S(2)}, u32[]{:S(2)}) collective-permute-start(f32[2,256,512]{2,1,0:T(8,128)S(1)} %get-tuple-element.24.refs_4_), channel_id=1, source_target_pairs={{0,64},{1,65},{2,66},{3,67},{4,68},{5,69},{6,70},{7,71},{8,72},{9,... | collective-permute-start | bytes 3145736 | tf_op jit(solution)/shard_map/ppermute | solution.py:422
  72.3 0.4 collective-permute-start.12
  72.8 2.0 %early_rows.1 = (f32[3,2,512,512]{3,2,1,0:T(8,128)}, f32[8,128]{1,0:T(8,128)}) custom-call(s32[1]{0:T(128)} %bitcast.core_ref, f32[2,512,512]{2,1,0:T(8,128)S(1)} %far_pair.1.a_ref.refs_0_, f32[2,512,512]{2,1,0:T(8,128)S(1)} %collective-permute-done.6.b_ref.refs_1_, f32[1,512,512]{2,1,0:T(8,128)S(1)} %far_terms_0.3.a_ref.refs_2_, ...), custom_call_target="tpu_custom_call" | custom-call | bytes 1024 | tf_op jit(solution)/shard_map/early_rows/pallas_call | solution.py:340
  74.8 0.5 collective-permute-done.14.refs_5_
  75.3 3.6 %collective-permute-done.13.refs_4_ = f32[1,512,512]{2,1,0:T(8,128)S(1)} collective-permute-done((f32[1,512,512]{2,1,0:T(8,128)S(1)}, f32[1,512,512]{2,1,0:T(8,128)S(1)}, u32[]{:S(2)}, u32[]{:S(2)}) %collective-permute-start.13) | collective-permute-done | bytes 1048608 | tf_op jit(solution)/shard_map/ppermute | solution.py:422
  78.9 4.7 %last_rows.1 = f32[3,2,512,512]{3,2,1,0:T(8,128)} custom-call(s32[1]{0:T(128)} %bitcast.core_ref, f32[2,256,512]{2,1,0:T(8,128)S(1)} %collective-permute-done.10.refs_0_, f32[2,256,512]{2,1,0:T(8,128)S(1)} %collective-permute-done.11.refs_1_, f32[1,512,512]{2,1,0:T(8,128)S(1)} %collective-permute-done.12.refs_2_, ...), custom_call_target="tpu_custom_call", output_to_operand_aliasing={{}: (9, {})} | custom-call | bytes 1024 | tf_op jit(solution)/shard_map/last_rows/pallas_call | solution.py:390
  (25 shorter events, 0.2 us)
Async XLA Ops:
  0.0 5.7 %copy-start.3 = (f32[1,4]{1,0:T(1,128)S(1)}, f32[1,4]{1,0:T(1,128)}, u32[]{:S(2)}) copy-start(f32[1,4]{1,0:T(1,128)} %coef_ref.3) | copy-start | bytes 52
  0.0 5.7 %copy-start.2 = (s32[1,2,3]{2,1,0:T(2,128)S(1)}, s32[1,2,3]{2,1,0:T(2,128)}, u32[]{:S(2)}) copy-start(s32[1,2,3]{2,1,0:T(2,128)} %index_ref.3) | copy-start | bytes 76
  0.0 5.7 %copy-start.1 = (s32[1,2,3]{2,1,0:T(2,128)S(1)}, s32[1,2,3]{2,1,0:T(2,128)}, u32[]{:S(2)}) copy-start(s32[1,2,3]{2,1,0:T(2,128)} %live_ref.3) | copy-start | bytes 76
  0.0 5.7 %copy-start = (f32[1,2,3,512,512]{4,3,2,1,0:T(8,128)S(1)}, f32[1,2,3,512,512]{4,3,2,1,0:T(8,128)}, u32[]{:S(2)}) copy-start(f32[1,2,3,512,512]{4,3,2,1,0:T(8,128)} %t_ref.3) | copy-start | bytes 18874372
  1.4 26.6 %collective-permute-start.4 = (f32[1,512,512]{2,1,0:T(8,128)S(1)}, f32[1,512,512]{2,1,0:T(8,128)S(1)}, u32[]{:S(2)}, u32[]{:S(2)}) collective-permute-start(f32[1,512,512]{2,1,0:T(8,128)S(1)} %edge.1.after_ref), channel_id=1, source_target_pairs={{64,1},{65,2},{66,3},{67,4},{68,5},{69,6},{70,7},{71,8},{72,9},{73... | collective-permute-start | bytes 3145736 | tf_op jit(solution)/shard_map/ppermute | solution.py:422
  6.5 7.2 %collective-permute-start.1 = (f32[3,128,512]{2,1,0:T(8,128)S(1)}, f32[3,128,512]{2,1,0:T(8,128)S(1)}, u32[]{:S(2)}, u32[]{:S(2)}) collective-permute-start(f32[3,128,512]{2,1,0:T(8,128)S(1)} %get-tuple-element.17), channel_id=1, source_target_pairs={{0,64},{1,65},{2,66},{3,67},{4,68},{5,69},{6,70},{7,71},{8,72},{9,... | collective-permute-start | bytes 2359304 | tf_op jit(solution)/shard_map/ppermute | solution.py:422
  10.9 4.7 %collective-permute-start.2 = (f32[3,128,512]{2,1,0:T(8,128)S(1)}, f32[3,128,512]{2,1,0:T(8,128)S(1)}, u32[]{:S(2)}, u32[]{:S(2)}) collective-permute-start(f32[3,128,512]{2,1,0:T(8,128)S(1)} %get-tuple-element.18), channel_id=1, source_target_pairs={{0,64},{1,65},{2,66},{3,67},{4,68},{5,69},{6,70},{7,71},{8,72},{9,... | collective-permute-start | bytes 2359304 | tf_op jit(solution)/shard_map/ppermute | solution.py:422
  11.0 4.6 %collective-permute-start.3 = (f32[3,128,512]{2,1,0:T(8,128)S(1)}, f32[3,128,512]{2,1,0:T(8,128)S(1)}, u32[]{:S(2)}, u32[]{:S(2)}) collective-permute-start(f32[3,128,512]{2,1,0:T(8,128)S(1)} %get-tuple-element.19), channel_id=1, source_target_pairs={{0,64},{1,65},{2,66},{3,67},{4,68},{5,69},{6,70},{7,71},{8,72},{9,... | collective-permute-start | bytes 2359304 | tf_op jit(solution)/shard_map/ppermute | solution.py:422
  11.4 4.8 %collective-permute-start = (f32[3,128,512]{2,1,0:T(8,128)S(1)}, f32[3,128,512]{2,1,0:T(8,128)S(1)}, u32[]{:S(2)}, u32[]{:S(2)}) collective-permute-start(f32[3,128,512]{2,1,0:T(8,128)S(1)} %get-tuple-element.16.after_ref), channel_id=1, source_target_pairs={{0,64},{1,65},{2,66},{3,67},{4,68},{5,69},{6,70},{7,71},{8,72},{9,... | collective-permute-start | bytes 2359304 | tf_op jit(solution)/shard_map/ppermute | solution.py:422
  11.5 9.2 %slice-start = ((s8[6291456]{0:T(1024)(128)(4,1)}), s8[4194304]{0:T(1024)(128)(4,1)S(1)}, s32[]{:S(2)}) async-start(s8[6291456]{0:T(1024)(128)(4,1)} %bitcast.2), calls=%async_computation | async-start | bytes 8388608
  13.7 16.4 %collective-permute-start.5 = (f32[1,512,512]{2,1,0:T(8,128)S(1)}, f32[1,512,512]{2,1,0:T(8,128)S(1)}, u32[]{:S(2)}, u32[]{:S(2)}) collective-permute-start(f32[1,512,512]{2,1,0:T(8,128)S(1)} %get-tuple-element.22), channel_id=1, source_target_pairs={{64,1},{65,2},{66,3},{67,4},{68,5},{69,6},{70,7},{71,8},{72,9},{73... | collective-permute-start | bytes 3145736 | tf_op jit(solution)/shard_map/ppermute | solution.py:422
  16.2 4.5 %slice-start.1 = ((s8[6291456]{0:T(1024)(128)(4,1)}), s8[2097152]{0:T(1024)(128)(4,1)S(1)}, s32[]{:S(2)}) async-start(s8[6291456]{0:T(1024)(128)(4,1)} %bitcast.2), calls=%async_computation.1 | async-start | bytes 4194304
  17.6 24.9 %collective-permute-start.8 = (f32[1,512,512]{2,1,0:T(8,128)S(1)}, f32[1,512,512]{2,1,0:T(8,128)S(1)}, u32[]{:S(2)}, u32[]{:S(2)}) collective-permute-start(f32[1,512,512]{2,1,0:T(8,128)S(1)} %get-tuple-element.23), channel_id=1, source_target_pairs={{64,1},{65,2},{66,3},{67,4},{68,5},{69,6},{70,7},{71,8},{72,9},{73... | collective-permute-start | bytes 3145736 | tf_op jit(solution)/shard_map/ppermute | solution.py:422
  32.1 20.6 %collective-permute-start.6 = (f32[2,512,512]{2,1,0:T(8,128)S(1)}, f32[2,512,512]{2,1,0:T(8,128)S(1)}, u32[]{:S(2)}, u32[]{:S(2)}) collective-permute-start(f32[2,512,512]{2,1,0:T(8,128)S(1)} %far_pair.1.a_ref.refs_0_), channel_id=1, source_target_pairs={{0,64},{1,65},{2,66},{3,67},{4,68},{5,69},{6,70},{7,71},{8,72},{9,... | collective-permute-start | bytes 6291464 | tf_op jit(solution)/shard_map/ppermute | solution.py:422
  36.7 27.6 %collective-permute-start.7 = (f32[2,512,512]{2,1,0:T(8,128)S(1)}, f32[2,512,512]{2,1,0:T(8,128)S(1)}, u32[]{:S(2)}, u32[]{:S(2)}) collective-permute-start(f32[2,512,512]{2,1,0:T(8,128)S(1)} %far_pair.1.a_ref.refs_0_), channel_id=1, source_target_pairs={{64,1},{65,2},{66,3},{67,4},{68,5},{69,6},{70,7},{71,8},{72,9},{73... | collective-permute-start | bytes 6291464 | tf_op jit(solution)/shard_map/ppermute | solution.py:422
  44.4 15.6 %collective-permute-start.9 = (f32[1,512,512]{2,1,0:T(8,128)S(1)}, f32[1,512,512]{2,1,0:T(8,128)S(1)}, u32[]{:S(2)}, u32[]{:S(2)}) collective-permute-start(f32[1,512,512]{2,1,0:T(8,128)S(1)} %far_terms_0.3.a_ref.refs_2_), channel_id=1, source_target_pairs={{0,64},{1,65},{2,66},{3,67},{4,68},{5,69},{6,70},{7,71},{8,72},{9,... | collective-permute-start | bytes 3145736 | tf_op jit(solution)/shard_map/ppermute | solution.py:422
  49.5 25.8 %collective-permute-start.14 = (f32[1,512,512]{2,1,0:T(8,128)S(1)}, f32[1,512,512]{2,1,0:T(8,128)S(1)}, u32[]{:S(2)}, u32[]{:S(2)}) collective-permute-start(f32[1,512,512]{2,1,0:T(8,128)S(1)} %far_terms_0.3.a_ref.refs_2_), channel_id=1, source_target_pairs={{1,64},{2,65},{3,66},{4,67},{5,68},{6,69},{7,70},{8,71},{9,72},{10... | collective-permute-start | bytes 3145736 | tf_op jit(solution)/shard_map/ppermute | solution.py:422
  50.8 28.1 %collective-permute-start.13 = (f32[1,512,512]{2,1,0:T(8,128)S(1)}, f32[1,512,512]{2,1,0:T(8,128)S(1)}, u32[]{:S(2)}, u32[]{:S(2)}) collective-permute-start(f32[1,512,512]{2,1,0:T(8,128)S(1)} %far_terms_0.3.a_ref.refs_2_), channel_id=1, source_target_pairs={{64,65},{65,66},{66,67},{67,68},{68,69},{69,70},{70,71},{71,72},{7... | collective-permute-start | bytes 3145736 | tf_op jit(solution)/shard_map/ppermute | solution.py:422
  68.2 10.6 %collective-permute-start.10 = (f32[2,256,512]{2,1,0:T(8,128)S(1)}, f32[2,256,512]{2,1,0:T(8,128)S(1)}, u32[]{:S(2)}, u32[]{:S(2)}) collective-permute-start(f32[2,256,512]{2,1,0:T(8,128)S(1)} %get-tuple-element.24.refs_4_), channel_id=1, source_target_pairs={{0,64},{1,65},{2,66},{3,67},{4,68},{5,69},{6,70},{7,71},{8,72},{9,... | collective-permute-start | bytes 3145736 | tf_op jit(solution)/shard_map/ppermute | solution.py:422
  72.2 6.6 %collective-permute-start.11 = (f32[2,256,512]{2,1,0:T(8,128)S(1)}, f32[2,256,512]{2,1,0:T(8,128)S(1)}, u32[]{:S(2)}, u32[]{:S(2)}) collective-permute-start(f32[2,256,512]{2,1,0:T(8,128)S(1)} %get-tuple-element.25.refs_5_), channel_id=1, source_target_pairs={{0,64},{1,65},{2,66},{3,67},{4,68},{5,69},{6,70},{7,71},{8,72},{9,... | collective-permute-start | bytes 3145736 | tf_op jit(solution)/shard_map/ppermute | solution.py:422
  72.3 6.5 %collective-permute-start.12 = (f32[1,512,512]{2,1,0:T(8,128)S(1)}, f32[1,512,512]{2,1,0:T(8,128)S(1)}, u32[]{:S(2)}, u32[]{:S(2)}) collective-permute-start(f32[1,512,512]{2,1,0:T(8,128)S(1)} %near_terms_1.3.refs_0_.refs_3_), channel_id=1, source_target_pairs={{0,64},{1,65},{2,66},{3,67},{4,68},{5,69},{6,70},{7,71},{8,72},{9,... | collective-permute-start | bytes 3145736 | tf_op jit(solution)/shard_map/ppermute | solution.py:422

commit v4 on v3

--- a/solution.py
+++ b/solution.py
@@ -354,16 +354,53 @@
     )(core, *sources, *old)
 
 
-def last_rows(core, out, moved, partials, sums, from_left, from_right, store):
-    width = from_left.shape[-1]
+RING = 4
+
+
+def sooner(j):
+    return (lax.rem(j, RING) == 0) * 1 if isinstance(j, jax.Array) else int(j % RING == 0)
+
+
+def sooner_term(core, halo, store, after):
+    width = halo.shape[-1]
+
+    def kernel(core_ref, h_ref, t_ref, after_ref, o_ref):
+        @pl.when(core_ref[0] == 1)
+        def _():
+            slot = 6 - 4 * sooner(lax.axis_index("blk"))
+            o_ref[...] = sandwich(h_ref[0], t_ref[slot, 0], t_ref[slot, 1])
+
+    return pl.pallas_call(
+        kernel,
+        grid_spec=pltpu.PrefetchScalarGridSpec(
+            num_scalar_prefetch=1,
+            grid=(1,),
+            in_specs=[
+                pl.BlockSpec((1, width, width), lambda n, c: (0, 0, 0)),
+                pl.BlockSpec(memory_space=pltpu.VMEM),
+                HBM_REF,
+            ],
+            out_specs=pl.BlockSpec((width, width), lambda n, c: (0, 0)),
+        ),
+        out_shape=jax.ShapeDtypeStruct((width, width), F32),
+        compiler_params=params(),
+        cost_estimate=cost(),
+        name="sooner_term",
+    )(core, halo, store, after)
+
+
+def last_rows(core, out, moved, partial, near, sooner_far, halo, store):
+    width = halo.shape[-1]
     rows = width // HALVES
-    first = out.shape[0] - from_left.shape[0]
-    given = [*moved, *partials, *sums]
+    first = out.shape[0] - halo.shape[0]
     early = moved[0].shape[1]
 
     def kernel(core_ref, *refs):
-        blocks, near = refs[: len(moved)], refs[len(moved) : len(given)]
-        left, right, t_left, t_right, _, o_ref, buf, sems, early_sems = refs[len(given) :]
+        blocks, (partial_ref, near_ref, s_ref, h_ref, t_ref, _, o_ref, buf, sems, early_sems) = refs[: len(moved)], refs[len(moved) :]
+        sector = sooner(lax.axis_index("blk"))
+
+        def near_sum(chosen, span):
+            return jnp.where(chosen == 0, partial_ref[0, span], near_ref[0, span])
 
         @pl.when(core_ref[0] == 1)
         def _():
@@ -372,41 +409,41 @@
                 for n in range(first):
                     copies.append(pltpu.make_async_copy(block.at[n], o_ref.at[n, 0, pl.ds(p * early, early)], early_sems.at[p, n]))
                     copies[-1].start()
-            for sector, (halo, t) in enumerate(((left, t_left), (right, t_right))):
-                high, low = t[0, 0], t[0, 1]
-                inner_high, inner_low = inner_halves(halo[0], high, low)
-                for h in range(HALVES):
-                    span = slice(h * rows, (h + 1) * rows)
-                    part, inside = h * PARTS // HALVES, h * rows % (width // PARTS)
-                    base = near[sector * PARTS + part][0, inside : inside + rows]
-                    buf[sector, span] = base + outer(high[span], low[span], inner_high, inner_low)
-                    copies.append(pltpu.make_async_copy(buf.at[sector, span], o_ref.at[first, sector, span], sems.at[sector, h]))
-                    copies[-1].start()
+            buf[0] = s_ref[...] + near_sum(sector, slice(0, width))
+            copies.append(pltpu.make_async_copy(buf.at[0], o_ref.at[first, sector], sems.at[HALVES]))
+            copies[-1].start()
+            slot = 2 + 4 * sector
+            high, low = t_ref[slot, 0], t_ref[slot, 1]
+            inner_high, inner_low = inner_halves(h_ref[0], high, low)
+            for h in range(HALVES):
+                span = slice(h * rows, (h + 1) * rows)
+                buf[1, span] = near_sum(1 - sector, span) + outer(high[span], low[span], inner_high, inner_low)
+                copies.append(pltpu.make_async_copy(buf.at[1, span], o_ref.at[first, 1 - sector, span], sems.at[h]))
+                copies[-1].start()
             for copy in copies:
                 copy.wait()
 
     whole = pl.BlockSpec(memory_space=pltpu.VMEM)
-    pair = (1, 2, width, width)
+    count = len(moved) + 4
     return pl.pallas_call(
         kernel,
         grid_spec=pltpu.PrefetchScalarGridSpec(
             num_scalar_prefetch=1,
             grid=(1,),
-            in_specs=[whole] * (len(given) + 2)
-            + [pl.BlockSpec(pair, lambda n, c: (6, 0, 0, 0)), pl.BlockSpec(pair, lambda n, c: (2, 0, 0, 0)), HBM_REF],
+            in_specs=[whole] * count + [whole, HBM_REF],
             out_specs=HBM_REF,
             scratch_shapes=[
                 pltpu.VMEM((2, width, width), F32),
-                pltpu.SemaphoreType.DMA((2, HALVES)),
+                pltpu.SemaphoreType.DMA((HALVES + 1,)),
                 pltpu.SemaphoreType.DMA((len(moved), first)),
             ],
         ),
         out_shape=jax.ShapeDtypeStruct(out.shape, F32),
-        input_output_aliases={len(given) + 5: 0},
+        input_output_aliases={count + 2: 0},
         compiler_params=params(),
         cost_estimate=cost(),
         name="last_rows",
-    )(core, *given, from_left, from_right, store, store, out)
+    )(core, *moved, partial, near, sooner_far, halo, store, out)
 
 
 def shards(chips, env_in, site_tensor, pair_live, coef_index, mpo_coef):
@@ -415,8 +452,11 @@
     swap = [(s * chips + j, (1 - s) * chips + j) for s in range(2) for j in range(chips)]
     meet = [(chips + j, j + 1) for j in range(chips - 1)] + [(j + 1, chips + j) for j in range(chips - 1)]
 
-    to_right = [(chips + j, chips + j + 1) for j in range(chips - 1)]
-    to_left = [(j + 1, chips + j) for j in range(chips - 1)]
+    from_left = {j: (chips + j - 1, chips + j) for j in range(1, chips)}
+    from_right = {j: (j + 1, chips + j) for j in range(chips - 1)}
+    sides = from_left, from_right
+    soon = [sides[sooner(j)][j] for j in range(chips) if j in sides[sooner(j)]]
+    later = [sides[1 - sooner(j)][j] for j in range(chips) if j in sides[1 - sooner(j)]]
 
     def send(value, pairs):
         return lax.ppermute(value, axes, pairs)
@@ -438,7 +478,7 @@
     second_halo_a, crossed_a = send(first_a, meet), send(first_a, swap)
     (near_2,) = near_terms(core, 0, env_in, env_in, True, store, 1, [first_a], CUTS, 3 - CUTS)
     (first_b,) = far_terms(core, 0, near_2, 0, halo_2, store, 1, 0, [first_a])
-    from_left, from_right, crossed_b = send(first_b, to_right), send(first_b, to_left), send(first_b, swap)
+    halo_soon, halo_later, crossed_b = send(first_b, soon), send(first_b, later), send(first_b, swap)
 
     (near_a,) = near_terms(core, 1, first_a, crossed_a, False, store, 1, [])
     sums = near_terms(core, 1, first_b, crossed_b, False, store, PARTS, [near_a])
@@ -446,8 +486,9 @@
     second_a = far_terms(core, 1, near_a, 0, second_halo_a, store, 2, 0, sums[:1])
     moved_a = [send(block, swap) for block in second_a]
     early = [([first_a], 0, 0), ([crossed_a], 0, 1), ([first_b], CUTS, 0), ([crossed_b], CUTS, 1)], [(second_a, 0, 1)]
-    out, _ = write_rows(core, None, env_in.shape, early, "early_rows")
-    out = last_rows(core, out, moved_a, partials, sums, from_left, from_right, store)
+    out, mark = write_rows(core, None, env_in.shape, early, "early_rows")
+    sooner_far = sooner_term(core, halo_soon, store, mark)
+    out = last_rows(core, out, moved_a, *partials, *sums, sooner_far, halo_later, store)
     return out[None]
 
 

time: 84 us -> 82.4 us (0.981)
  waiting for transfers between devices: 5.48 us -> 4.14 us
    pallas_call x0 -> x1, Pallas kernels: none -> 1.91 us  [sooner_term(): pl.pallas_call(kernel, grid_spec=pltpu.PrefetchScalarGridSpec(num_scalar_...]
    pallas_call x1, Pallas kernels: 4.74 us -> 3.19 us  [last_rows(): pl.pallas_call(kernel, grid_spec=pltpu.PrefetchScalarGridSpec(num_scalar_...]
    ppermute x15, waiting for transfers between devices: 5.48 us -> 4.14 us  [send(): return lax.ppermute(value, axes, pairs)]
  transfers between devices with their start and end apart: 15 -> 15, of which waited for: 5 -> 5; matrix products, arithmetic and copies ran while one was open for 0% -> 0% of each run, Pallas kernels for 45% -> 48%
where the time goes in v4:
time: 82.4 us; the launch traced here: 82.2 us
  Pallas kernels  43.8 us (53%)
  starting transfers between devices  33.8 us (41%)
  waiting for transfers between devices  4.14 us (5%)
    ppermute x15, starting transfers between devices, send(): return lax.ppermute(value, axes, pairs)  33.8 us
    pallas_call x4, Pallas kernels, near_terms(): pl.pallas_call(kernel, grid_spec=pltpu.PrefetchScalarGridSpec(num_scalar_...  21.8 us
    pallas_call x3, Pallas kernels, far_terms(): pl.pallas_call(kernel, grid_spec=pltpu.PrefetchScalarGridSpec(num_scalar_...  7.69 us
    ppermute x15, waiting for transfers between devices, send(): return lax.ppermute(value, axes, pairs)  4.14 us
    pallas_call x1, Pallas kernels, last_rows(): pl.pallas_call(kernel, grid_spec=pltpu.PrefetchScalarGridSpec(num_scalar_...  3.19 us
    pallas_call x1, Pallas kernels, own_store(): pl.pallas_call(kernel, grid_spec=pltpu.PrefetchScalarGridSpec(num_scalar_...  2.16 us
    pallas_call x1, Pallas kernels, far_pair(): pl.pallas_call(kernel, grid_spec=pltpu.PrefetchScalarGridSpec(num_scalar_...  2.01 us
    pallas_call x1, Pallas kernels, sooner_term(): pl.pallas_call(kernel, grid_spec=pltpu.PrefetchScalarGridSpec(num_scalar_...  1.91 us
  transfers between devices with their start and end apart: 15, of which 5 were waited for; matrix products, arithmetic and copies ran while one was open for 0% of the time, Pallas kernels for 48%

profile of v4, /device:TPU:25, one launch (start us, length us, event | category | flops | bytes accessed | tf_op | source)
XLA Modules:
  0.0 82.2 jit_solution(4438338832630679986)
XLA Ops:
  0.0 1.4 %edge.1.after_ref = f32[1,512,512]{2,1,0:T(8,128)S(1)} custom-call(s32[1]{0:T(128)} %bitcast.core_ref, f32[3,2,512,512]{3,2,1,0:T(8,128)} %b_ref.3), custom_call_target="tpu_custom_call" | custom-call | bytes 1024 | tf_op jit(solution)/shard_map/edge/pallas_call | solution.py:84
  1.4 4.2 %collective-permute-start.4 = (f32[1,512,512]{2,1,0:T(8,128)S(1)}, f32[1,512,512]{2,1,0:T(8,128)S(1)}, u32[]{:S(2)}, u32[]{:S(2)}) collective-permute-start(f32[1,512,512]{2,1,0:T(8,128)S(1)} %edge.1.after_ref), channel_id=1, source_target_pairs={{64,1},{65,2},{66,3},{67,4},{68,5},{69,6},{70,7},{71,8},{72,9},{73... | collective-permute-start | bytes 3145736 | tf_op jit(solution)/shard_map/ppermute | solution.py:462
  5.7 0.8 outgoing.1
  6.5 4.4 %collective-permute-start.1 = (f32[3,128,512]{2,1,0:T(8,128)S(1)}, f32[3,128,512]{2,1,0:T(8,128)S(1)}, u32[]{:S(2)}, u32[]{:S(2)}) collective-permute-start(f32[3,128,512]{2,1,0:T(8,128)S(1)} %get-tuple-element.18), channel_id=1, source_target_pairs={{0,64},{1,65},{2,66},{3,67},{4,68},{5,69},{6,70},{7,71},{8,72},{9,... | collective-permute-start | bytes 2359304 | tf_op jit(solution)/shard_map/ppermute | solution.py:462
  11.0 0.4 collective-permute-start.3
  11.5 2.2 %own_store.1 = (bf16[7,2,512,512]{3,2,1,0:T(8,128)(2,1)S(1)}, f32[1,512,512]{2,1,0:T(8,128)S(1)}) custom-call(s32[1]{0:T(128)} %bitcast.core_ref, s32[1,2,3]{2,1,0:T(2,128)S(1)} %copy-done.1, s32[1,2,3]{2,1,0:T(2,128)S(1)} %copy-done.2, f32[1,4]{1,0:T(1,128)S(1)} %copy-done.3, f32[1,2,3,512,512]{4,3,2,1,0:T(8,128)S(1)} %copy-done, f32[3,2,512,512]{3,2,1,0:T(8,128)} %b_ref.3, ...), custom_call_target="tpu_custom_call" | custom-call | bytes 1024 | tf_op jit(solution)/shard_map/own_store/pallas_call | solution.py:154
  13.7 1.9 %collective-permute-start.5 = (f32[1,512,512]{2,1,0:T(8,128)S(1)}, f32[1,512,512]{2,1,0:T(8,128)S(1)}, u32[]{:S(2)}, u32[]{:S(2)}) collective-permute-start(f32[1,512,512]{2,1,0:T(8,128)S(1)} %get-tuple-element.23), channel_id=1, source_target_pairs={{64,1},{65,2},{66,3},{67,4},{68,5},{69,6},{70,7},{71,8},{72,9},{73... | collective-permute-start | bytes 3145736 | tf_op jit(solution)/shard_map/ppermute | solution.py:462
  15.6 0.6 collective-permute-done.refs_0_
  16.2 1.4 %full_store.1 = (bf16[7,2,512,512]{3,2,1,0:T(8,128)(2,1)S(1)}, f32[1,512,512]{2,1,0:T(8,128)S(1)}) custom-call(s32[1]{0:T(128)} %bitcast.core_ref, f32[3,128,512]{2,1,0:T(8,128)S(1)} %collective-permute-done.refs_0_, f32[3,128,512]{2,1,0:T(8,128)S(1)} %collective-permute-done.1.refs_1_, ...), custom_call_target="tpu_custom_call", output_to_operand_aliasing={{0}: (5, {})} | custom-call | bytes 1024 | tf_op jit(solution)/shard_map/full_store/pallas_call | solution.py:196
  17.6 3.1 %collective-permute-start.8 = (f32[1,512,512]{2,1,0:T(8,128)S(1)}, f32[1,512,512]{2,1,0:T(8,128)S(1)}, u32[]{:S(2)}, u32[]{:S(2)}) collective-permute-start(f32[1,512,512]{2,1,0:T(8,128)S(1)} %get-tuple-element.24), channel_id=1, source_target_pairs={{64,1},{65,2},{66,3},{67,4},{68,5},{69,6},{70,7},{71,8},{72,9},{73... | collective-permute-start | bytes 3145736 | tf_op jit(solution)/shard_map/ppermute | solution.py:462
  20.7 7.3 %near_terms_0.2.p_ref = f32[2,512,512]{2,1,0:T(8,128)S(1)} custom-call(s32[1]{0:T(128)} %bitcast.core_ref, f32[3,2,512,512]{3,2,1,0:T(8,128)S(1)} %bitcast.3, f32[3,2,512,512]{3,2,1,0:T(8,128)S(1)} %bitcast.3, bf16[7,2,512,512]{3,2,1,0:T(8,128)(2,1)S(1)} %get-tuple-element.22.ta_ref.tb_ref.t_ref.refs_6_, ...), custom_call_target="tpu_custom_call" | custom-call | bytes 1024 | tf_op jit(solution)/shard_map/near_terms_0/pallas_call | solution.py:232
  28.0 1.9 %far_terms_0.2.d_ref = f32[1,512,512]{2,1,0:T(8,128)S(1)} custom-call(s32[1]{0:T(128)} %bitcast.core_ref, f32[2,512,512]{2,1,0:T(8,128)S(1)} %near_terms_0.2.p_ref, f32[1,512,512]{2,1,0:T(8,128)S(1)} %collective-permute-done.4.h_ref, bf16[7,2,512,512]{3,2,1,0:T(8,128)(2,1)S(1)} %get-tuple-element.22.ta_ref.tb_ref.t_ref.refs_6_), custom_call_target="tpu_custom_call" | custom-call | flops 18400000000 | bytes 1024 | tf_op jit(solution)/shard_map/far_terms_0/pallas_call | solution.py:256
  30.0 0.1 collective-permute-done.5.h_ref
  30.1 2.0 %far_pair.1.a_ref.refs_0_ = f32[2,512,512]{2,1,0:T(8,128)S(1)} custom-call(s32[1]{0:T(128)} %bitcast.core_ref, f32[2,512,512]{2,1,0:T(8,128)S(1)} %near_terms_0.2.p_ref, f32[1,512,512]{2,1,0:T(8,128)S(1)} %far_terms_0.2.d_ref, f32[1,512,512]{2,1,0:T(8,128)S(1)} %collective-permute-done.5.h_ref, ...), custom_call_target="tpu_custom_call" | custom-call | bytes 1024 | tf_op jit(solution)/shard_map/far_pair/pallas_call | solution.py:284
  32.1 4.6 %collective-permute-start.6 = (f32[2,512,512]{2,1,0:T(8,128)S(1)}, f32[2,512,512]{2,1,0:T(8,128)S(1)}, u32[]{:S(2)}, u32[]{:S(2)}) collective-permute-start(f32[2,512,512]{2,1,0:T(8,128)S(1)} %far_pair.1.a_ref.refs_0_), channel_id=1, source_target_pairs={{0,64},{1,65},{2,66},{3,67},{4,68},{5,69},{6,70},{7,71},{8,72},{9,... | collective-permute-start | bytes 6291464 | tf_op jit(solution)/shard_map/ppermute | solution.py:462
  36.7 2.1 %collective-permute-start.7 = (f32[2,512,512]{2,1,0:T(8,128)S(1)}, f32[2,512,512]{2,1,0:T(8,128)S(1)}, u32[]{:S(2)}, u32[]{:S(2)}) collective-permute-start(f32[2,512,512]{2,1,0:T(8,128)S(1)} %far_pair.1.a_ref.refs_0_), channel_id=1, source_target_pairs={{64,1},{65,2},{66,3},{67,4},{68,5},{69,6},{70,7},{71,8},{72,9},{73... | collective-permute-start | bytes 6291464 | tf_op jit(solution)/shard_map/ppermute | solution.py:462
  38.8 3.6 %near_terms_0.3.p_ref = f32[1,512,512]{2,1,0:T(8,128)S(1)} custom-call(s32[1]{0:T(128)} %bitcast.core_ref, f32[3,2,512,512]{3,2,1,0:T(8,128)S(1)} %bitcast.3, f32[3,2,512,512]{3,2,1,0:T(8,128)S(1)} %bitcast.3, bf16[7,2,512,512]{3,2,1,0:T(8,128)(2,1)S(1)} %get-tuple-element.22.ta_ref.tb_ref.t_ref.refs_6_, ...), custom_call_target="tpu_custom_call" | custom-call | bytes 1024 | tf_op jit(solution)/shard_map/near_terms_0/pallas_call | solution.py:232
  42.5 1.9 %far_terms_0.3.a_ref.refs_2_ = f32[1,512,512]{2,1,0:T(8,128)S(1)} custom-call(s32[1]{0:T(128)} %bitcast.core_ref, f32[1,512,512]{2,1,0:T(8,128)S(1)} %near_terms_0.3.p_ref, f32[1,512,512]{2,1,0:T(8,128)S(1)} %collective-permute-done.8.h_ref, bf16[7,2,512,512]{3,2,1,0:T(8,128)(2,1)S(1)} %get-tuple-element.22.ta_ref.tb_ref.t_ref.refs_6_, ...), custom_call_target="tpu_custom_call" | custom-call | bytes 1024 | tf_op jit(solution)/shard_map/far_terms_0/pallas_call | solution.py:256
  44.4 5.1 %collective-permute-start.9 = (f32[1,512,512]{2,1,0:T(8,128)S(1)}, f32[1,512,512]{2,1,0:T(8,128)S(1)}, u32[]{:S(2)}, u32[]{:S(2)}) collective-permute-start(f32[1,512,512]{2,1,0:T(8,128)S(1)} %far_terms_0.3.a_ref.refs_2_), channel_id=1, source_target_pairs={{0,64},{1,65},{2,66},{3,67},{4,68},{5,69},{6,70},{7,71},{8,72},{9,... | collective-permute-start | bytes 3145736 | tf_op jit(solution)/shard_map/ppermute | solution.py:462
  49.5 1.3 %collective-permute-start.14 = (f32[1,512,512]{2,1,0:T(8,128)S(1)}, f32[1,512,512]{2,1,0:T(8,128)S(1)}, u32[]{:S(2)}, u32[]{:S(2)}) collective-permute-start(f32[1,512,512]{2,1,0:T(8,128)S(1)} %far_terms_0.3.a_ref.refs_2_), channel_id=1, source_target_pairs={{2,65},{3,66},{4,67},{67,68},{6,69},{7,70},{8,71},{71,72},{10,73},... | collective-permute-start | bytes 3145736 | tf_op jit(solution)/shard_map/ppermute | solution.py:462
  50.8 1.9 %collective-permute-start.13 = (f32[1,512,512]{2,1,0:T(8,128)S(1)}, f32[1,512,512]{2,1,0:T(8,128)S(1)}, u32[]{:S(2)}, u32[]{:S(2)}) collective-permute-start(f32[1,512,512]{2,1,0:T(8,128)S(1)} %far_terms_0.3.a_ref.refs_2_), channel_id=1, source_target_pairs={{1,64},{64,65},{65,66},{66,67},{5,68},{68,69},{69,70},{70,71},{9,7... | collective-permute-start | bytes 3145736 | tf_op jit(solution)/shard_map/ppermute | solution.py:462
  52.7 7.3 %near_terms_1.2.refs_0_.p_ref = f32[2,512,512]{2,1,0:T(8,128)S(1)} custom-call(s32[1]{0:T(128)} %bitcast.core_ref, f32[2,512,512]{2,1,0:T(8,128)S(1)} %far_pair.1.a_ref.refs_0_, f32[2,512,512]{2,1,0:T(8,128)S(1)} %collective-permute-done.6.b_ref.refs_1_, bf16[7,2,512,512]{3,2,1,0:T(8,128)(2,1)S(1)} %get-tuple-element.22.ta_ref.tb_ref.t_ref.refs_6_, ...), custom_call_target="tpu_custom_call" | custom-call | bytes 1024 | tf_op jit(solution)/shard_map/near_terms_1/pallas_call | solution.py:232
  60.0 3.6 %near_terms_1.3.refs_0_.refs_3_ = f32[1,512,512]{2,1,0:T(8,128)S(1)} custom-call(s32[1]{0:T(128)} %bitcast.core_ref, f32[1,512,512]{2,1,0:T(8,128)S(1)} %far_terms_0.3.a_ref.refs_2_, f32[1,512,512]{2,1,0:T(8,128)S(1)} %collective-permute-done.9.b_ref.refs_3_, bf16[7,2,512,512]{3,2,1,0:T(8,128)(2,1)S(1)} %get-tuple-element.22.ta_ref.tb_ref.t_ref.refs_6_, ...), custom_call_target="tpu_custom_call" | custom-call | bytes 1024 | tf_op jit(solution)/shard_map/near_terms_1/pallas_call | solution.py:232
  63.6 0.7 collective-permute-done.7.h_ref
  64.4 3.9 %far_terms_1.1 = (f32[2,256,512]{2,1,0:T(8,128)S(1)}, f32[2,256,512]{2,1,0:T(8,128)S(1)}) custom-call(s32[1]{0:T(128)} %bitcast.core_ref, f32[2,512,512]{2,1,0:T(8,128)S(1)} %near_terms_1.2.refs_0_.p_ref, f32[2,512,512]{2,1,0:T(8,128)S(1)} %collective-permute-done.7.h_ref, bf16[7,2,512,512]{3,2,1,0:T(8,128)(2,1)S(1)} %get-tuple-element.22.ta_ref.tb_ref.t_ref.refs_6_, ...), custom_call_target="tpu_custom_call" | custom-call | bytes 1024 | tf_op jit(solution)/shard_map/far_terms_1/pallas_call | solution.py:256
  68.2 4.0 %collective-permute-start.10 = (f32[2,256,512]{2,1,0:T(8,128)S(1)}, f32[2,256,512]{2,1,0:T(8,128)S(1)}, u32[]{:S(2)}, u32[]{:S(2)}) collective-permute-start(f32[2,256,512]{2,1,0:T(8,128)S(1)} %get-tuple-element.25.refs_4_), channel_id=1, source_target_pairs={{0,64},{1,65},{2,66},{3,67},{4,68},{5,69},{6,70},{7,71},{8,72},{9,... | collective-permute-start | bytes 3145736 | tf_op jit(solution)/shard_map/ppermute | solution.py:462
  72.3 0.4 collective-permute-start.12
  72.8 1.5 %early_rows.1 = (f32[3,2,512,512]{3,2,1,0:T(8,128)}, f32[8,128]{1,0:T(8,128)S(1)}) custom-call(s32[1]{0:T(128)} %bitcast.core_ref, f32[2,512,512]{2,1,0:T(8,128)S(1)} %far_pair.1.a_ref.refs_0_, f32[2,512,512]{2,1,0:T(8,128)S(1)} %collective-permute-done.6.b_ref.refs_1_, f32[1,512,512]{2,1,0:T(8,128)S(1)} %far_terms_0.3.a_ref.refs_2_, ...), custom_call_target="tpu_custom_call" | custom-call | bytes 1024 | tf_op jit(solution)/shard_map/early_rows/pallas_call | solution.py:340
  74.2 1.1 %collective-permute-done.13.h_ref = f32[1,512,512]{2,1,0:T(8,128)S(1)} collective-permute-done((f32[1,512,512]{2,1,0:T(8,128)S(1)}, f32[1,512,512]{2,1,0:T(8,128)S(1)}, u32[]{:S(2)}, u32[]{:S(2)}) %collective-permute-start.13) | collective-permute-done | bytes 1048608 | tf_op jit(solution)/shard_map/ppermute | solution.py:462
  75.3 1.9 %sooner_term.1.refs_4_ = f32[512,512]{1,0:T(8,128)S(1)} custom-call(s32[1]{0:T(128)} %bitcast.core_ref, f32[1,512,512]{2,1,0:T(8,128)S(1)} %collective-permute-done.13.h_ref, bf16[7,2,512,512]{3,2,1,0:T(8,128)(2,1)S(1)} %get-tuple-element.22.ta_ref.tb_ref.t_ref.refs_6_, f32[8,128]{1,0:T(8,128)S(1)} %get-tuple-element.27.after_ref), custom_call_target="tpu_custom_call" | custom-call | bytes 1024 | tf_op jit(solution)/shard_map/sooner_term/pallas_call | solution.py:373
  77.2 1.6 %collective-permute-done.14.refs_5_ = f32[1,512,512]{2,1,0:T(8,128)S(1)} collective-permute-done((f32[1,512,512]{2,1,0:T(8,128)S(1)}, f32[1,512,512]{2,1,0:T(8,128)S(1)}, u32[]{:S(2)}, u32[]{:S(2)}) %collective-permute-start.14) | collective-permute-done | bytes 1048608 | tf_op jit(solution)/shard_map/ppermute | solution.py:462
  78.9 3.2 %last_rows.1 = f32[3,2,512,512]{3,2,1,0:T(8,128)} custom-call(s32[1]{0:T(128)} %bitcast.core_ref, f32[2,256,512]{2,1,0:T(8,128)S(1)} %collective-permute-done.10.refs_0_, f32[2,256,512]{2,1,0:T(8,128)S(1)} %collective-permute-done.11.refs_1_, f32[1,512,512]{2,1,0:T(8,128)S(1)} %collective-permute-done.12.refs_2_, ...), custom_call_target="tpu_custom_call", output_to_operand_aliasing={{}: (8, {})} | custom-call | bytes 1024 | tf_op jit(solution)/shard_map/last_rows/pallas_call | solution.py:428
  (26 shorter events, 0.3 us)
Async XLA Ops:
  0.0 5.7 %copy-start.3 = (f32[1,4]{1,0:T(1,128)S(1)}, f32[1,4]{1,0:T(1,128)}, u32[]{:S(2)}) copy-start(f32[1,4]{1,0:T(1,128)} %coef_ref.3) | copy-start | bytes 52
  0.0 5.7 %copy-start.2 = (s32[1,2,3]{2,1,0:T(2,128)S(1)}, s32[1,2,3]{2,1,0:T(2,128)}, u32[]{:S(2)}) copy-start(s32[1,2,3]{2,1,0:T(2,128)} %index_ref.3) | copy-start | bytes 76
  0.0 5.7 %copy-start.1 = (s32[1,2,3]{2,1,0:T(2,128)S(1)}, s32[1,2,3]{2,1,0:T(2,128)}, u32[]{:S(2)}) copy-start(s32[1,2,3]{2,1,0:T(2,128)} %live_ref.3) | copy-start | bytes 76
  0.0 5.7 %copy-start = (f32[1,2,3,512,512]{4,3,2,1,0:T(8,128)S(1)}, f32[1,2,3,512,512]{4,3,2,1,0:T(8,128)}, u32[]{:S(2)}) copy-start(f32[1,2,3,512,512]{4,3,2,1,0:T(8,128)} %t_ref.3) | copy-start | bytes 18874372
  1.4 26.6 %collective-permute-start.4 = (f32[1,512,512]{2,1,0:T(8,128)S(1)}, f32[1,512,512]{2,1,0:T(8,128)S(1)}, u32[]{:S(2)}, u32[]{:S(2)}) collective-permute-start(f32[1,512,512]{2,1,0:T(8,128)S(1)} %edge.1.after_ref), channel_id=1, source_target_pairs={{64,1},{65,2},{66,3},{67,4},{68,5},{69,6},{70,7},{71,8},{72,9},{73... | collective-permute-start | bytes 3145736 | tf_op jit(solution)/shard_map/ppermute | solution.py:462
  6.5 7.2 %collective-permute-start.1 = (f32[3,128,512]{2,1,0:T(8,128)S(1)}, f32[3,128,512]{2,1,0:T(8,128)S(1)}, u32[]{:S(2)}, u32[]{:S(2)}) collective-permute-start(f32[3,128,512]{2,1,0:T(8,128)S(1)} %get-tuple-element.18), channel_id=1, source_target_pairs={{0,64},{1,65},{2,66},{3,67},{4,68},{5,69},{6,70},{7,71},{8,72},{9,... | collective-permute-start | bytes 2359304 | tf_op jit(solution)/shard_map/ppermute | solution.py:462
  10.9 4.7 %collective-permute-start.2 = (f32[3,128,512]{2,1,0:T(8,128)S(1)}, f32[3,128,512]{2,1,0:T(8,128)S(1)}, u32[]{:S(2)}, u32[]{:S(2)}) collective-permute-start(f32[3,128,512]{2,1,0:T(8,128)S(1)} %get-tuple-element.19), channel_id=1, source_target_pairs={{0,64},{1,65},{2,66},{3,67},{4,68},{5,69},{6,70},{7,71},{8,72},{9,... | collective-permute-start | bytes 2359304 | tf_op jit(solution)/shard_map/ppermute | solution.py:462
  11.0 4.6 %collective-permute-start.3 = (f32[3,128,512]{2,1,0:T(8,128)S(1)}, f32[3,128,512]{2,1,0:T(8,128)S(1)}, u32[]{:S(2)}, u32[]{:S(2)}) collective-permute-start(f32[3,128,512]{2,1,0:T(8,128)S(1)} %get-tuple-element.20), channel_id=1, source_target_pairs={{0,64},{1,65},{2,66},{3,67},{4,68},{5,69},{6,70},{7,71},{8,72},{9,... | collective-permute-start | bytes 2359304 | tf_op jit(solution)/shard_map/ppermute | solution.py:462
  11.4 4.8 %collective-permute-start = (f32[3,128,512]{2,1,0:T(8,128)S(1)}, f32[3,128,512]{2,1,0:T(8,128)S(1)}, u32[]{:S(2)}, u32[]{:S(2)}) collective-permute-start(f32[3,128,512]{2,1,0:T(8,128)S(1)} %get-tuple-element.17.after_ref), channel_id=1, source_target_pairs={{0,64},{1,65},{2,66},{3,67},{4,68},{5,69},{6,70},{7,71},{8,72},{9,... | collective-permute-start | bytes 2359304 | tf_op jit(solution)/shard_map/ppermute | solution.py:462
  11.5 9.2 %slice-start = ((s8[6291456]{0:T(1024)(128)(4,1)}), s8[4194304]{0:T(1024)(128)(4,1)S(1)}, s32[]{:S(2)}) async-start(s8[6291456]{0:T(1024)(128)(4,1)} %bitcast.2), calls=%async_computation | async-start | bytes 8388608
  13.7 16.4 %collective-permute-start.5 = (f32[1,512,512]{2,1,0:T(8,128)S(1)}, f32[1,512,512]{2,1,0:T(8,128)S(1)}, u32[]{:S(2)}, u32[]{:S(2)}) collective-permute-start(f32[1,512,512]{2,1,0:T(8,128)S(1)} %get-tuple-element.23), channel_id=1, source_target_pairs={{64,1},{65,2},{66,3},{67,4},{68,5},{69,6},{70,7},{71,8},{72,9},{73... | collective-permute-start | bytes 3145736 | tf_op jit(solution)/shard_map/ppermute | solution.py:462
  16.2 4.5 %slice-start.1 = ((s8[6291456]{0:T(1024)(128)(4,1)}), s8[2097152]{0:T(1024)(128)(4,1)S(1)}, s32[]{:S(2)}) async-start(s8[6291456]{0:T(1024)(128)(4,1)} %bitcast.2), calls=%async_computation.1 | async-start | bytes 4194304
  17.6 24.9 %collective-permute-start.8 = (f32[1,512,512]{2,1,0:T(8,128)S(1)}, f32[1,512,512]{2,1,0:T(8,128)S(1)}, u32[]{:S(2)}, u32[]{:S(2)}) collective-permute-start(f32[1,512,512]{2,1,0:T(8,128)S(1)} %get-tuple-element.24), channel_id=1, source_target_pairs={{64,1},{65,2},{66,3},{67,4},{68,5},{69,6},{70,7},{71,8},{72,9},{73... | collective-permute-start | bytes 3145736 | tf_op jit(solution)/shard_map/ppermute | solution.py:462
  32.1 20.6 %collective-permute-start.6 = (f32[2,512,512]{2,1,0:T(8,128)S(1)}, f32[2,512,512]{2,1,0:T(8,128)S(1)}, u32[]{:S(2)}, u32[]{:S(2)}) collective-permute-start(f32[2,512,512]{2,1,0:T(8,128)S(1)} %far_pair.1.a_ref.refs_0_), channel_id=1, source_target_pairs={{0,64},{1,65},{2,66},{3,67},{4,68},{5,69},{6,70},{7,71},{8,72},{9,... | collective-permute-start | bytes 6291464 | tf_op jit(solution)/shard_map/ppermute | solution.py:462
  36.7 27.6 %collective-permute-start.7 = (f32[2,512,512]{2,1,0:T(8,128)S(1)}, f32[2,512,512]{2,1,0:T(8,128)S(1)}, u32[]{:S(2)}, u32[]{:S(2)}) collective-permute-start(f32[2,512,512]{2,1,0:T(8,128)S(1)} %far_pair.1.a_ref.refs_0_), channel_id=1, source_target_pairs={{64,1},{65,2},{66,3},{67,4},{68,5},{69,6},{70,7},{71,8},{72,9},{73... | collective-permute-start | bytes 6291464 | tf_op jit(solution)/shard_map/ppermute | solution.py:462
  44.4 15.6 %collective-permute-start.9 = (f32[1,512,512]{2,1,0:T(8,128)S(1)}, f32[1,512,512]{2,1,0:T(8,128)S(1)}, u32[]{:S(2)}, u32[]{:S(2)}) collective-permute-start(f32[1,512,512]{2,1,0:T(8,128)S(1)} %far_terms_0.3.a_ref.refs_2_), channel_id=1, source_target_pairs={{0,64},{1,65},{2,66},{3,67},{4,68},{5,69},{6,70},{7,71},{8,72},{9,... | collective-permute-start | bytes 3145736 | tf_op jit(solution)/shard_map/ppermute | solution.py:462
  49.5 29.3 %collective-permute-start.14 = (f32[1,512,512]{2,1,0:T(8,128)S(1)}, f32[1,512,512]{2,1,0:T(8,128)S(1)}, u32[]{:S(2)}, u32[]{:S(2)}) collective-permute-start(f32[1,512,512]{2,1,0:T(8,128)S(1)} %far_terms_0.3.a_ref.refs_2_), channel_id=1, source_target_pairs={{2,65},{3,66},{4,67},{67,68},{6,69},{7,70},{8,71},{71,72},{10,73},... | collective-permute-start | bytes 3145736 | tf_op jit(solution)/shard_map/ppermute | solution.py:462
  50.8 24.5 %collective-permute-start.13 = (f32[1,512,512]{2,1,0:T(8,128)S(1)}, f32[1,512,512]{2,1,0:T(8,128)S(1)}, u32[]{:S(2)}, u32[]{:S(2)}) collective-permute-start(f32[1,512,512]{2,1,0:T(8,128)S(1)} %far_terms_0.3.a_ref.refs_2_), channel_id=1, source_target_pairs={{1,64},{64,65},{65,66},{66,67},{5,68},{68,69},{69,70},{70,71},{9,7... | collective-permute-start | bytes 3145736 | tf_op jit(solution)/shard_map/ppermute | solution.py:462
  68.2 10.6 %collective-permute-start.10 = (f32[2,256,512]{2,1,0:T(8,128)S(1)}, f32[2,256,512]{2,1,0:T(8,128)S(1)}, u32[]{:S(2)}, u32[]{:S(2)}) collective-permute-start(f32[2,256,512]{2,1,0:T(8,128)S(1)} %get-tuple-element.25.refs_4_), channel_id=1, source_target_pairs={{0,64},{1,65},{2,66},{3,67},{4,68},{5,69},{6,70},{7,71},{8,72},{9,... | collective-permute-start | bytes 3145736 | tf_op jit(solution)/shard_map/ppermute | solution.py:462
  72.2 6.6 %collective-permute-start.11 = (f32[2,256,512]{2,1,0:T(8,128)S(1)}, f32[2,256,512]{2,1,0:T(8,128)S(1)}, u32[]{:S(2)}, u32[]{:S(2)}) collective-permute-start(f32[2,256,512]{2,1,0:T(8,128)S(1)} %get-tuple-element.26.refs_5_), channel_id=1, source_target_pairs={{0,64},{1,65},{2,66},{3,67},{4,68},{5,69},{6,70},{7,71},{8,72},{9,... | collective-permute-start | bytes 3145736 | tf_op jit(solution)/shard_map/ppermute | solution.py:462
  72.3 6.5 %collective-permute-start.12 = (f32[1,512,512]{2,1,0:T(8,128)S(1)}, f32[1,512,512]{2,1,0:T(8,128)S(1)}, u32[]{:S(2)}, u32[]{:S(2)}) collective-permute-start(f32[1,512,512]{2,1,0:T(8,128)S(1)} %near_terms_1.3.refs_0_.refs_3_), channel_id=1, source_target_pairs={{0,64},{1,65},{2,66},{3,67},{4,68},{5,69},{6,70},{7,71},{8,72},{9,... | collective-permute-start | bytes 3145736 | tf_op jit(solution)/shard_map/ppermute | solution.py:462

commit v5 on v4

--- a/solution.py
+++ b/solution.py
@@ -67,7 +67,7 @@
 
 def edge(core, env):
     width = env.shape[-1]
-    parts = 4
+    parts = 8
     rows = width // parts
 
     def kernel(core_ref, e_ref, o_ref, sems):
@@ -409,12 +409,12 @@
                 for n in range(first):
                     copies.append(pltpu.make_async_copy(block.at[n], o_ref.at[n, 0, pl.ds(p * early, early)], early_sems.at[p, n]))
                     copies[-1].start()
+            slot = 2 + 4 * sector
+            high, low = t_ref[slot, 0], t_ref[slot, 1]
+            inner_high, inner_low = inner_halves(h_ref[0], high, low)
             buf[0] = s_ref[...] + near_sum(sector, slice(0, width))
             copies.append(pltpu.make_async_copy(buf.at[0], o_ref.at[first, sector], sems.at[HALVES]))
             copies[-1].start()
-            slot = 2 + 4 * sector
-            high, low = t_ref[slot, 0], t_ref[slot, 1]
-            inner_high, inner_low = inner_halves(h_ref[0], high, low)
             for h in range(HALVES):
                 span = slice(h * rows, (h + 1) * rows)
                 buf[1, span] = near_sum(1 - sector, span) + outer(high[span], low[span], inner_high, inner_low)

time: 82.4 us -> 82.6 us (level)
  no operation moved by 1% of the time
where the time goes in v5:
time: 82.6 us; the launch traced here: 82.3 us
  Pallas kernels  43.9 us (53%)
  starting transfers between devices  33.8 us (41%)
  waiting for transfers between devices  4.12 us (5%)
    ppermute x15, starting transfers between devices, send(): return lax.ppermute(value, axes, pairs)  33.8 us
    pallas_call x4, Pallas kernels, near_terms(): pl.pallas_call(kernel, grid_spec=pltpu.PrefetchScalarGridSpec(num_scalar_...  21.8 us
    pallas_call x3, Pallas kernels, far_terms(): pl.pallas_call(kernel, grid_spec=pltpu.PrefetchScalarGridSpec(num_scalar_...  7.69 us
    ppermute x15, waiting for transfers between devices, send(): return lax.ppermute(value, axes, pairs)  4.12 us
    pallas_call x1, Pallas kernels, last_rows(): pl.pallas_call(kernel, grid_spec=pltpu.PrefetchScalarGridSpec(num_scalar_...  3.19 us
    pallas_call x1, Pallas kernels, own_store(): pl.pallas_call(kernel, grid_spec=pltpu.PrefetchScalarGridSpec(num_scalar_...  2.16 us
    pallas_call x1, Pallas kernels, far_pair(): pl.pallas_call(kernel, grid_spec=pltpu.PrefetchScalarGridSpec(num_scalar_...  2.02 us
    pallas_call x1, Pallas kernels, sooner_term(): pl.pallas_call(kernel, grid_spec=pltpu.PrefetchScalarGridSpec(num_scalar_...  1.91 us
  transfers between devices with their start and end apart: 15, of which 5 were waited for; matrix products, arithmetic and copies ran while one was open for 0% of the time, Pallas kernels for 48%

profile of v5, /device:TPU:25, one launch (start us, length us, event | category | flops | bytes accessed | tf_op | source)
XLA Modules:
  0.0 82.3 jit_solution(11866670526952793837)
XLA Ops:
  0.0 1.5 %edge.1.after_ref = f32[1,512,512]{2,1,0:T(8,128)S(1)} custom-call(s32[1]{0:T(128)} %bitcast.core_ref, f32[3,2,512,512]{3,2,1,0:T(8,128)} %b_ref.3), custom_call_target="tpu_custom_call" | custom-call | bytes 1024 | tf_op jit(solution)/shard_map/edge/pallas_call | solution.py:84
  1.5 4.2 %collective-permute-start.4 = (f32[1,512,512]{2,1,0:T(8,128)S(1)}, f32[1,512,512]{2,1,0:T(8,128)S(1)}, u32[]{:S(2)}, u32[]{:S(2)}) collective-permute-start(f32[1,512,512]{2,1,0:T(8,128)S(1)} %edge.1.after_ref), channel_id=1, source_target_pairs={{64,1},{65,2},{66,3},{67,4},{68,5},{69,6},{70,7},{71,8},{72,9},{73... | collective-permute-start | bytes 3145736 | tf_op jit(solution)/shard_map/ppermute | solution.py:462
  5.8 0.8 outgoing.1
  6.6 4.4 %collective-permute-start.1 = (f32[3,128,512]{2,1,0:T(8,128)S(1)}, f32[3,128,512]{2,1,0:T(8,128)S(1)}, u32[]{:S(2)}, u32[]{:S(2)}) collective-permute-start(f32[3,128,512]{2,1,0:T(8,128)S(1)} %get-tuple-element.18), channel_id=1, source_target_pairs={{0,64},{1,65},{2,66},{3,67},{4,68},{5,69},{6,70},{7,71},{8,72},{9,... | collective-permute-start | bytes 2359304 | tf_op jit(solution)/shard_map/ppermute | solution.py:462
  11.1 0.4 collective-permute-start.3
  11.6 2.2 %own_store.1 = (bf16[7,2,512,512]{3,2,1,0:T(8,128)(2,1)S(1)}, f32[1,512,512]{2,1,0:T(8,128)S(1)}) custom-call(s32[1]{0:T(128)} %bitcast.core_ref, s32[1,2,3]{2,1,0:T(2,128)S(1)} %copy-done.1, s32[1,2,3]{2,1,0:T(2,128)S(1)} %copy-done.2, f32[1,4]{1,0:T(1,128)S(1)} %copy-done.3, f32[1,2,3,512,512]{4,3,2,1,0:T(8,128)S(1)} %copy-done, f32[3,2,512,512]{3,2,1,0:T(8,128)} %b_ref.3, ...), custom_call_target="tpu_custom_call" | custom-call | bytes 1024 | tf_op jit(solution)/shard_map/own_store/pallas_call | solution.py:154
  13.8 1.9 %collective-permute-start.5 = (f32[1,512,512]{2,1,0:T(8,128)S(1)}, f32[1,512,512]{2,1,0:T(8,128)S(1)}, u32[]{:S(2)}, u32[]{:S(2)}) collective-permute-start(f32[1,512,512]{2,1,0:T(8,128)S(1)} %get-tuple-element.23), channel_id=1, source_target_pairs={{64,1},{65,2},{66,3},{67,4},{68,5},{69,6},{70,7},{71,8},{72,9},{73... | collective-permute-start | bytes 3145736 | tf_op jit(solution)/shard_map/ppermute | solution.py:462
  15.8 0.6 collective-permute-done.refs_0_
  16.3 1.4 %full_store.1 = (bf16[7,2,512,512]{3,2,1,0:T(8,128)(2,1)S(1)}, f32[1,512,512]{2,1,0:T(8,128)S(1)}) custom-call(s32[1]{0:T(128)} %bitcast.core_ref, f32[3,128,512]{2,1,0:T(8,128)S(1)} %collective-permute-done.refs_0_, f32[3,128,512]{2,1,0:T(8,128)S(1)} %collective-permute-done.1.refs_1_, ...), custom_call_target="tpu_custom_call", output_to_operand_aliasing={{0}: (5, {})} | custom-call | bytes 1024 | tf_op jit(solution)/shard_map/full_store/pallas_call | solution.py:196
  17.7 3.1 %collective-permute-start.8 = (f32[1,512,512]{2,1,0:T(8,128)S(1)}, f32[1,512,512]{2,1,0:T(8,128)S(1)}, u32[]{:S(2)}, u32[]{:S(2)}) collective-permute-start(f32[1,512,512]{2,1,0:T(8,128)S(1)} %get-tuple-element.24), channel_id=1, source_target_pairs={{64,1},{65,2},{66,3},{67,4},{68,5},{69,6},{70,7},{71,8},{72,9},{73... | collective-permute-start | bytes 3145736 | tf_op jit(solution)/shard_map/ppermute | solution.py:462
  20.9 7.3 %near_terms_0.2.p_ref = f32[2,512,512]{2,1,0:T(8,128)S(1)} custom-call(s32[1]{0:T(128)} %bitcast.core_ref, f32[3,2,512,512]{3,2,1,0:T(8,128)S(1)} %bitcast.3, f32[3,2,512,512]{3,2,1,0:T(8,128)S(1)} %bitcast.3, bf16[7,2,512,512]{3,2,1,0:T(8,128)(2,1)S(1)} %get-tuple-element.22.ta_ref.tb_ref.t_ref.refs_6_, ...), custom_call_target="tpu_custom_call" | custom-call | bytes 1024 | tf_op jit(solution)/shard_map/near_terms_0/pallas_call | solution.py:232
  28.2 1.9 %far_terms_0.2.d_ref = f32[1,512,512]{2,1,0:T(8,128)S(1)} custom-call(s32[1]{0:T(128)} %bitcast.core_ref, f32[2,512,512]{2,1,0:T(8,128)S(1)} %near_terms_0.2.p_ref, f32[1,512,512]{2,1,0:T(8,128)S(1)} %collective-permute-done.4.h_ref, bf16[7,2,512,512]{3,2,1,0:T(8,128)(2,1)S(1)} %get-tuple-element.22.ta_ref.tb_ref.t_ref.refs_6_), custom_call_target="tpu_custom_call" | custom-call | flops 18400000000 | bytes 1024 | tf_op jit(solution)/shard_map/far_terms_0/pallas_call | solution.py:256
  30.1 0.1 collective-permute-done.5.h_ref
  30.2 2.0 %far_pair.1.a_ref.refs_0_ = f32[2,512,512]{2,1,0:T(8,128)S(1)} custom-call(s32[1]{0:T(128)} %bitcast.core_ref, f32[2,512,512]{2,1,0:T(8,128)S(1)} %near_terms_0.2.p_ref, f32[1,512,512]{2,1,0:T(8,128)S(1)} %far_terms_0.2.d_ref, f32[1,512,512]{2,1,0:T(8,128)S(1)} %collective-permute-done.5.h_ref, ...), custom_call_target="tpu_custom_call" | custom-call | bytes 1024 | tf_op jit(solution)/shard_map/far_pair/pallas_call | solution.py:284
  32.2 4.6 %collective-permute-start.6 = (f32[2,512,512]{2,1,0:T(8,128)S(1)}, f32[2,512,512]{2,1,0:T(8,128)S(1)}, u32[]{:S(2)}, u32[]{:S(2)}) collective-permute-start(f32[2,512,512]{2,1,0:T(8,128)S(1)} %far_pair.1.a_ref.refs_0_), channel_id=1, source_target_pairs={{0,64},{1,65},{2,66},{3,67},{4,68},{5,69},{6,70},{7,71},{8,72},{9,... | collective-permute-start | bytes 6291464 | tf_op jit(solution)/shard_map/ppermute | solution.py:462
  36.8 2.1 %collective-permute-start.7 = (f32[2,512,512]{2,1,0:T(8,128)S(1)}, f32[2,512,512]{2,1,0:T(8,128)S(1)}, u32[]{:S(2)}, u32[]{:S(2)}) collective-permute-start(f32[2,512,512]{2,1,0:T(8,128)S(1)} %far_pair.1.a_ref.refs_0_), channel_id=1, source_target_pairs={{64,1},{65,2},{66,3},{67,4},{68,5},{69,6},{70,7},{71,8},{72,9},{73... | collective-permute-start | bytes 6291464 | tf_op jit(solution)/shard_map/ppermute | solution.py:462
  38.9 3.6 %near_terms_0.3.p_ref = f32[1,512,512]{2,1,0:T(8,128)S(1)} custom-call(s32[1]{0:T(128)} %bitcast.core_ref, f32[3,2,512,512]{3,2,1,0:T(8,128)S(1)} %bitcast.3, f32[3,2,512,512]{3,2,1,0:T(8,128)S(1)} %bitcast.3, bf16[7,2,512,512]{3,2,1,0:T(8,128)(2,1)S(1)} %get-tuple-element.22.ta_ref.tb_ref.t_ref.refs_6_, ...), custom_call_target="tpu_custom_call" | custom-call | bytes 1024 | tf_op jit(solution)/shard_map/near_terms_0/pallas_call | solution.py:232
  42.6 1.9 %far_terms_0.3.a_ref.refs_2_ = f32[1,512,512]{2,1,0:T(8,128)S(1)} custom-call(s32[1]{0:T(128)} %bitcast.core_ref, f32[1,512,512]{2,1,0:T(8,128)S(1)} %near_terms_0.3.p_ref, f32[1,512,512]{2,1,0:T(8,128)S(1)} %collective-permute-done.8.h_ref, bf16[7,2,512,512]{3,2,1,0:T(8,128)(2,1)S(1)} %get-tuple-element.22.ta_ref.tb_ref.t_ref.refs_6_, ...), custom_call_target="tpu_custom_call" | custom-call | bytes 1024 | tf_op jit(solution)/shard_map/far_terms_0/pallas_call | solution.py:256
  44.5 5.1 %collective-permute-start.9 = (f32[1,512,512]{2,1,0:T(8,128)S(1)}, f32[1,512,512]{2,1,0:T(8,128)S(1)}, u32[]{:S(2)}, u32[]{:S(2)}) collective-permute-start(f32[1,512,512]{2,1,0:T(8,128)S(1)} %far_terms_0.3.a_ref.refs_2_), channel_id=1, source_target_pairs={{0,64},{1,65},{2,66},{3,67},{4,68},{5,69},{6,70},{7,71},{8,72},{9,... | collective-permute-start | bytes 3145736 | tf_op jit(solution)/shard_map/ppermute | solution.py:462
  49.6 1.3 %collective-permute-start.14 = (f32[1,512,512]{2,1,0:T(8,128)S(1)}, f32[1,512,512]{2,1,0:T(8,128)S(1)}, u32[]{:S(2)}, u32[]{:S(2)}) collective-permute-start(f32[1,512,512]{2,1,0:T(8,128)S(1)} %far_terms_0.3.a_ref.refs_2_), channel_id=1, source_target_pairs={{2,65},{3,66},{4,67},{67,68},{6,69},{7,70},{8,71},{71,72},{10,73},... | collective-permute-start | bytes 3145736 | tf_op jit(solution)/shard_map/ppermute | solution.py:462
  50.9 1.9 %collective-permute-start.13 = (f32[1,512,512]{2,1,0:T(8,128)S(1)}, f32[1,512,512]{2,1,0:T(8,128)S(1)}, u32[]{:S(2)}, u32[]{:S(2)}) collective-permute-start(f32[1,512,512]{2,1,0:T(8,128)S(1)} %far_terms_0.3.a_ref.refs_2_), channel_id=1, source_target_pairs={{1,64},{64,65},{65,66},{66,67},{5,68},{68,69},{69,70},{70,71},{9,7... | collective-permute-start | bytes 3145736 | tf_op jit(solution)/shard_map/ppermute | solution.py:462
  52.8 7.3 %near_terms_1.2.refs_0_.p_ref = f32[2,512,512]{2,1,0:T(8,128)S(1)} custom-call(s32[1]{0:T(128)} %bitcast.core_ref, f32[2,512,512]{2,1,0:T(8,128)S(1)} %far_pair.1.a_ref.refs_0_, f32[2,512,512]{2,1,0:T(8,128)S(1)} %collective-permute-done.6.b_ref.refs_1_, bf16[7,2,512,512]{3,2,1,0:T(8,128)(2,1)S(1)} %get-tuple-element.22.ta_ref.tb_ref.t_ref.refs_6_, ...), custom_call_target="tpu_custom_call" | custom-call | bytes 1024 | tf_op jit(solution)/shard_map/near_terms_1/pallas_call | solution.py:232
  60.1 3.6 %near_terms_1.3.refs_0_.refs_3_ = f32[1,512,512]{2,1,0:T(8,128)S(1)} custom-call(s32[1]{0:T(128)} %bitcast.core_ref, f32[1,512,512]{2,1,0:T(8,128)S(1)} %far_terms_0.3.a_ref.refs_2_, f32[1,512,512]{2,1,0:T(8,128)S(1)} %collective-permute-done.9.b_ref.refs_3_, bf16[7,2,512,512]{3,2,1,0:T(8,128)(2,1)S(1)} %get-tuple-element.22.ta_ref.tb_ref.t_ref.refs_6_, ...), custom_call_target="tpu_custom_call" | custom-call | bytes 1024 | tf_op jit(solution)/shard_map/near_terms_1/pallas_call | solution.py:232
  63.8 0.7 collective-permute-done.7.h_ref
  64.5 3.9 %far_terms_1.1 = (f32[2,256,512]{2,1,0:T(8,128)S(1)}, f32[2,256,512]{2,1,0:T(8,128)S(1)}) custom-call(s32[1]{0:T(128)} %bitcast.core_ref, f32[2,512,512]{2,1,0:T(8,128)S(1)} %near_terms_1.2.refs_0_.p_ref, f32[2,512,512]{2,1,0:T(8,128)S(1)} %collective-permute-done.7.h_ref, bf16[7,2,512,512]{3,2,1,0:T(8,128)(2,1)S(1)} %get-tuple-element.22.ta_ref.tb_ref.t_ref.refs_6_, ...), custom_call_target="tpu_custom_call" | custom-call | bytes 1024 | tf_op jit(solution)/shard_map/far_terms_1/pallas_call | solution.py:256
  68.3 4.0 %collective-permute-start.10 = (f32[2,256,512]{2,1,0:T(8,128)S(1)}, f32[2,256,512]{2,1,0:T(8,128)S(1)}, u32[]{:S(2)}, u32[]{:S(2)}) collective-permute-start(f32[2,256,512]{2,1,0:T(8,128)S(1)} %get-tuple-element.25.refs_4_), channel_id=1, source_target_pairs={{0,64},{1,65},{2,66},{3,67},{4,68},{5,69},{6,70},{7,71},{8,72},{9,... | collective-permute-start | bytes 3145736 | tf_op jit(solution)/shard_map/ppermute | solution.py:462
  72.5 0.4 collective-permute-start.12
  72.9 1.5 %early_rows.1 = (f32[3,2,512,512]{3,2,1,0:T(8,128)}, f32[8,128]{1,0:T(8,128)S(1)}) custom-call(s32[1]{0:T(128)} %bitcast.core_ref, f32[2,512,512]{2,1,0:T(8,128)S(1)} %far_pair.1.a_ref.refs_0_, f32[2,512,512]{2,1,0:T(8,128)S(1)} %collective-permute-done.6.b_ref.refs_1_, f32[1,512,512]{2,1,0:T(8,128)S(1)} %far_terms_0.3.a_ref.refs_2_, ...), custom_call_target="tpu_custom_call" | custom-call | bytes 1024 | tf_op jit(solution)/shard_map/early_rows/pallas_call | solution.py:340
  74.3 1.1 %collective-permute-done.13.h_ref = f32[1,512,512]{2,1,0:T(8,128)S(1)} collective-permute-done((f32[1,512,512]{2,1,0:T(8,128)S(1)}, f32[1,512,512]{2,1,0:T(8,128)S(1)}, u32[]{:S(2)}, u32[]{:S(2)}) %collective-permute-start.13) | collective-permute-done | bytes 1048608 | tf_op jit(solution)/shard_map/ppermute | solution.py:462
  75.4 1.9 %sooner_term.1.refs_4_ = f32[512,512]{1,0:T(8,128)S(1)} custom-call(s32[1]{0:T(128)} %bitcast.core_ref, f32[1,512,512]{2,1,0:T(8,128)S(1)} %collective-permute-done.13.h_ref, bf16[7,2,512,512]{3,2,1,0:T(8,128)(2,1)S(1)} %get-tuple-element.22.ta_ref.tb_ref.t_ref.refs_6_, f32[8,128]{1,0:T(8,128)S(1)} %get-tuple-element.27.after_ref), custom_call_target="tpu_custom_call" | custom-call | bytes 1024 | tf_op jit(solution)/shard_map/sooner_term/pallas_call | solution.py:373
  77.3 1.6 %collective-permute-done.14.refs_5_ = f32[1,512,512]{2,1,0:T(8,128)S(1)} collective-permute-done((f32[1,512,512]{2,1,0:T(8,128)S(1)}, f32[1,512,512]{2,1,0:T(8,128)S(1)}, u32[]{:S(2)}, u32[]{:S(2)}) %collective-permute-start.14) | collective-permute-done | bytes 1048608 | tf_op jit(solution)/shard_map/ppermute | solution.py:462
  79.0 3.2 %last_rows.1 = f32[3,2,512,512]{3,2,1,0:T(8,128)} custom-call(s32[1]{0:T(128)} %bitcast.core_ref, f32[2,256,512]{2,1,0:T(8,128)S(1)} %collective-permute-done.10.refs_0_, f32[2,256,512]{2,1,0:T(8,128)S(1)} %collective-permute-done.11.refs_1_, f32[1,512,512]{2,1,0:T(8,128)S(1)} %collective-permute-done.12.refs_2_, ...), custom_call_target="tpu_custom_call", output_to_operand_aliasing={{}: (8, {})} | custom-call | bytes 1024 | tf_op jit(solution)/shard_map/last_rows/pallas_call | solution.py:428
  (26 shorter events, 0.3 us)
Async XLA Ops:
  0.0 5.8 %copy-start.3 = (f32[1,4]{1,0:T(1,128)S(1)}, f32[1,4]{1,0:T(1,128)}, u32[]{:S(2)}) copy-start(f32[1,4]{1,0:T(1,128)} %coef_ref.3) | copy-start | bytes 52
  0.0 5.8 %copy-start.2 = (s32[1,2,3]{2,1,0:T(2,128)S(1)}, s32[1,2,3]{2,1,0:T(2,128)}, u32[]{:S(2)}) copy-start(s32[1,2,3]{2,1,0:T(2,128)} %index_ref.3) | copy-start | bytes 76
  0.0 5.8 %copy-start.1 = (s32[1,2,3]{2,1,0:T(2,128)S(1)}, s32[1,2,3]{2,1,0:T(2,128)}, u32[]{:S(2)}) copy-start(s32[1,2,3]{2,1,0:T(2,128)} %live_ref.3) | copy-start | bytes 76
  0.0 5.8 %copy-start = (f32[1,2,3,512,512]{4,3,2,1,0:T(8,128)S(1)}, f32[1,2,3,512,512]{4,3,2,1,0:T(8,128)}, u32[]{:S(2)}) copy-start(f32[1,2,3,512,512]{4,3,2,1,0:T(8,128)} %t_ref.3) | copy-start | bytes 18874372
  1.5 26.6 %collective-permute-start.4 = (f32[1,512,512]{2,1,0:T(8,128)S(1)}, f32[1,512,512]{2,1,0:T(8,128)S(1)}, u32[]{:S(2)}, u32[]{:S(2)}) collective-permute-start(f32[1,512,512]{2,1,0:T(8,128)S(1)} %edge.1.after_ref), channel_id=1, source_target_pairs={{64,1},{65,2},{66,3},{67,4},{68,5},{69,6},{70,7},{71,8},{72,9},{73... | collective-permute-start | bytes 3145736 | tf_op jit(solution)/shard_map/ppermute | solution.py:462
  6.6 7.2 %collective-permute-start.1 = (f32[3,128,512]{2,1,0:T(8,128)S(1)}, f32[3,128,512]{2,1,0:T(8,128)S(1)}, u32[]{:S(2)}, u32[]{:S(2)}) collective-permute-start(f32[3,128,512]{2,1,0:T(8,128)S(1)} %get-tuple-element.18), channel_id=1, source_target_pairs={{0,64},{1,65},{2,66},{3,67},{4,68},{5,69},{6,70},{7,71},{8,72},{9,... | collective-permute-start | bytes 2359304 | tf_op jit(solution)/shard_map/ppermute | solution.py:462
  11.0 4.7 %collective-permute-start.2 = (f32[3,128,512]{2,1,0:T(8,128)S(1)}, f32[3,128,512]{2,1,0:T(8,128)S(1)}, u32[]{:S(2)}, u32[]{:S(2)}) collective-permute-start(f32[3,128,512]{2,1,0:T(8,128)S(1)} %get-tuple-element.19), channel_id=1, source_target_pairs={{0,64},{1,65},{2,66},{3,67},{4,68},{5,69},{6,70},{7,71},{8,72},{9,... | collective-permute-start | bytes 2359304 | tf_op jit(solution)/shard_map/ppermute | solution.py:462
  11.1 4.6 %collective-permute-start.3 = (f32[3,128,512]{2,1,0:T(8,128)S(1)}, f32[3,128,512]{2,1,0:T(8,128)S(1)}, u32[]{:S(2)}, u32[]{:S(2)}) collective-permute-start(f32[3,128,512]{2,1,0:T(8,128)S(1)} %get-tuple-element.20), channel_id=1, source_target_pairs={{0,64},{1,65},{2,66},{3,67},{4,68},{5,69},{6,70},{7,71},{8,72},{9,... | collective-permute-start | bytes 2359304 | tf_op jit(solution)/shard_map/ppermute | solution.py:462
  11.5 4.8 %collective-permute-start = (f32[3,128,512]{2,1,0:T(8,128)S(1)}, f32[3,128,512]{2,1,0:T(8,128)S(1)}, u32[]{:S(2)}, u32[]{:S(2)}) collective-permute-start(f32[3,128,512]{2,1,0:T(8,128)S(1)} %get-tuple-element.17.after_ref), channel_id=1, source_target_pairs={{0,64},{1,65},{2,66},{3,67},{4,68},{5,69},{6,70},{7,71},{8,72},{9,... | collective-permute-start | bytes 2359304 | tf_op jit(solution)/shard_map/ppermute | solution.py:462
  11.6 9.2 %slice-start = ((s8[6291456]{0:T(1024)(128)(4,1)}), s8[4194304]{0:T(1024)(128)(4,1)S(1)}, s32[]{:S(2)}) async-start(s8[6291456]{0:T(1024)(128)(4,1)} %bitcast.2), calls=%async_computation | async-start | bytes 8388608
  13.8 16.4 %collective-permute-start.5 = (f32[1,512,512]{2,1,0:T(8,128)S(1)}, f32[1,512,512]{2,1,0:T(8,128)S(1)}, u32[]{:S(2)}, u32[]{:S(2)}) collective-permute-start(f32[1,512,512]{2,1,0:T(8,128)S(1)} %get-tuple-element.23), channel_id=1, source_target_pairs={{64,1},{65,2},{66,3},{67,4},{68,5},{69,6},{70,7},{71,8},{72,9},{73... | collective-permute-start | bytes 3145736 | tf_op jit(solution)/shard_map/ppermute | solution.py:462
  16.3 4.5 %slice-start.1 = ((s8[6291456]{0:T(1024)(128)(4,1)}), s8[2097152]{0:T(1024)(128)(4,1)S(1)}, s32[]{:S(2)}) async-start(s8[6291456]{0:T(1024)(128)(4,1)} %bitcast.2), calls=%async_computation.1 | async-start | bytes 4194304
  17.7 24.9 %collective-permute-start.8 = (f32[1,512,512]{2,1,0:T(8,128)S(1)}, f32[1,512,512]{2,1,0:T(8,128)S(1)}, u32[]{:S(2)}, u32[]{:S(2)}) collective-permute-start(f32[1,512,512]{2,1,0:T(8,128)S(1)} %get-tuple-element.24), channel_id=1, source_target_pairs={{64,1},{65,2},{66,3},{67,4},{68,5},{69,6},{70,7},{71,8},{72,9},{73... | collective-permute-start | bytes 3145736 | tf_op jit(solution)/shard_map/ppermute | solution.py:462
  32.2 20.6 %collective-permute-start.6 = (f32[2,512,512]{2,1,0:T(8,128)S(1)}, f32[2,512,512]{2,1,0:T(8,128)S(1)}, u32[]{:S(2)}, u32[]{:S(2)}) collective-permute-start(f32[2,512,512]{2,1,0:T(8,128)S(1)} %far_pair.1.a_ref.refs_0_), channel_id=1, source_target_pairs={{0,64},{1,65},{2,66},{3,67},{4,68},{5,69},{6,70},{7,71},{8,72},{9,... | collective-permute-start | bytes 6291464 | tf_op jit(solution)/shard_map/ppermute | solution.py:462
  36.8 27.6 %collective-permute-start.7 = (f32[2,512,512]{2,1,0:T(8,128)S(1)}, f32[2,512,512]{2,1,0:T(8,128)S(1)}, u32[]{:S(2)}, u32[]{:S(2)}) collective-permute-start(f32[2,512,512]{2,1,0:T(8,128)S(1)} %far_pair.1.a_ref.refs_0_), channel_id=1, source_target_pairs={{64,1},{65,2},{66,3},{67,4},{68,5},{69,6},{70,7},{71,8},{72,9},{73... | collective-permute-start | bytes 6291464 | tf_op jit(solution)/shard_map/ppermute | solution.py:462
  44.5 15.6 %collective-permute-start.9 = (f32[1,512,512]{2,1,0:T(8,128)S(1)}, f32[1,512,512]{2,1,0:T(8,128)S(1)}, u32[]{:S(2)}, u32[]{:S(2)}) collective-permute-start(f32[1,512,512]{2,1,0:T(8,128)S(1)} %far_terms_0.3.a_ref.refs_2_), channel_id=1, source_target_pairs={{0,64},{1,65},{2,66},{3,67},{4,68},{5,69},{6,70},{7,71},{8,72},{9,... | collective-permute-start | bytes 3145736 | tf_op jit(solution)/shard_map/ppermute | solution.py:462
  49.6 29.3 %collective-permute-start.14 = (f32[1,512,512]{2,1,0:T(8,128)S(1)}, f32[1,512,512]{2,1,0:T(8,128)S(1)}, u32[]{:S(2)}, u32[]{:S(2)}) collective-permute-start(f32[1,512,512]{2,1,0:T(8,128)S(1)} %far_terms_0.3.a_ref.refs_2_), channel_id=1, source_target_pairs={{2,65},{3,66},{4,67},{67,68},{6,69},{7,70},{8,71},{71,72},{10,73},... | collective-permute-start | bytes 3145736 | tf_op jit(solution)/shard_map/ppermute | solution.py:462
  50.9 24.5 %collective-permute-start.13 = (f32[1,512,512]{2,1,0:T(8,128)S(1)}, f32[1,512,512]{2,1,0:T(8,128)S(1)}, u32[]{:S(2)}, u32[]{:S(2)}) collective-permute-start(f32[1,512,512]{2,1,0:T(8,128)S(1)} %far_terms_0.3.a_ref.refs_2_), channel_id=1, source_target_pairs={{1,64},{64,65},{65,66},{66,67},{5,68},{68,69},{69,70},{70,71},{9,7... | collective-permute-start | bytes 3145736 | tf_op jit(solution)/shard_map/ppermute | solution.py:462
  68.3 10.6 %collective-permute-start.10 = (f32[2,256,512]{2,1,0:T(8,128)S(1)}, f32[2,256,512]{2,1,0:T(8,128)S(1)}, u32[]{:S(2)}, u32[]{:S(2)}) collective-permute-start(f32[2,256,512]{2,1,0:T(8,128)S(1)} %get-tuple-element.25.refs_4_), channel_id=1, source_target_pairs={{0,64},{1,65},{2,66},{3,67},{4,68},{5,69},{6,70},{7,71},{8,72},{9,... | collective-permute-start | bytes 3145736 | tf_op jit(solution)/shard_map/ppermute | solution.py:462
  72.4 6.6 %collective-permute-start.11 = (f32[2,256,512]{2,1,0:T(8,128)S(1)}, f32[2,256,512]{2,1,0:T(8,128)S(1)}, u32[]{:S(2)}, u32[]{:S(2)}) collective-permute-start(f32[2,256,512]{2,1,0:T(8,128)S(1)} %get-tuple-element.26.refs_5_), channel_id=1, source_target_pairs={{0,64},{1,65},{2,66},{3,67},{4,68},{5,69},{6,70},{7,71},{8,72},{9,... | collective-permute-start | bytes 3145736 | tf_op jit(solution)/shard_map/ppermute | solution.py:462
  72.5 6.5 %collective-permute-start.12 = (f32[1,512,512]{2,1,0:T(8,128)S(1)}, f32[1,512,512]{2,1,0:T(8,128)S(1)}, u32[]{:S(2)}, u32[]{:S(2)}) collective-permute-start(f32[1,512,512]{2,1,0:T(8,128)S(1)} %near_terms_1.3.refs_0_.refs_3_), channel_id=1, source_target_pairs={{0,64},{1,65},{2,66},{3,67},{4,68},{5,69},{6,70},{7,71},{8,72},{9,... | collective-permute-start | bytes 3145736 | tf_op jit(solution)/shard_map/ppermute | solution.py:462

commit v6 on v4

--- a/solution.py
+++ b/solution.py
@@ -67,7 +67,7 @@
 
 def edge(core, env):
     width = env.shape[-1]
-    parts = 4
+    parts = 2
     rows = width // parts
 
     def kernel(core_ref, e_ref, o_ref, sems):

time: 82.4 us -> 82.4 us (level)
  no operation moved by 1% of the time
where the time goes in v6:
time: 82.4 us; the launch traced here: 82.2 us
  Pallas kernels  43.8 us (53%)
  starting transfers between devices  33.8 us (41%)
  waiting for transfers between devices  4.12 us (5%)
    ppermute x15, starting transfers between devices, send(): return lax.ppermute(value, axes, pairs)  33.8 us
    pallas_call x4, Pallas kernels, near_terms(): pl.pallas_call(kernel, grid_spec=pltpu.PrefetchScalarGridSpec(num_scalar_...  21.8 us
    pallas_call x3, Pallas kernels, far_terms(): pl.pallas_call(kernel, grid_spec=pltpu.PrefetchScalarGridSpec(num_scalar_...  7.69 us
    ppermute x15, waiting for transfers between devices, send(): return lax.ppermute(value, axes, pairs)  4.12 us
    pallas_call x1, Pallas kernels, last_rows(): pl.pallas_call(kernel, grid_spec=pltpu.PrefetchScalarGridSpec(num_scalar_...  3.19 us
    pallas_call x1, Pallas kernels, own_store(): pl.pallas_call(kernel, grid_spec=pltpu.PrefetchScalarGridSpec(num_scalar_...  2.16 us
    pallas_call x1, Pallas kernels, far_pair(): pl.pallas_call(kernel, grid_spec=pltpu.PrefetchScalarGridSpec(num_scalar_...  2.02 us
    pallas_call x1, Pallas kernels, sooner_term(): pl.pallas_call(kernel, grid_spec=pltpu.PrefetchScalarGridSpec(num_scalar_...  1.91 us
  transfers between devices with their start and end apart: 15, of which 5 were waited for; matrix products, arithmetic and copies ran while one was open for 0% of the time, Pallas kernels for 48%

profile of v6, /device:TPU:25, one launch (start us, length us, event | category | flops | bytes accessed | tf_op | source)
XLA Modules:
  0.0 82.2 jit_solution(262958986249078954)
XLA Ops:
  0.0 1.4 %edge.1.after_ref = f32[1,512,512]{2,1,0:T(8,128)S(1)} custom-call(s32[1]{0:T(128)} %bitcast.core_ref, f32[3,2,512,512]{3,2,1,0:T(8,128)} %b_ref.3), custom_call_target="tpu_custom_call" | custom-call | bytes 1024 | tf_op jit(solution)/shard_map/edge/pallas_call | solution.py:84
  1.4 4.2 %collective-permute-start.4 = (f32[1,512,512]{2,1,0:T(8,128)S(1)}, f32[1,512,512]{2,1,0:T(8,128)S(1)}, u32[]{:S(2)}, u32[]{:S(2)}) collective-permute-start(f32[1,512,512]{2,1,0:T(8,128)S(1)} %edge.1.after_ref), channel_id=1, source_target_pairs={{64,1},{65,2},{66,3},{67,4},{68,5},{69,6},{70,7},{71,8},{72,9},{73... | collective-permute-start | bytes 3145736 | tf_op jit(solution)/shard_map/ppermute | solution.py:462
  5.7 0.8 outgoing.1
  6.5 4.4 %collective-permute-start.1 = (f32[3,128,512]{2,1,0:T(8,128)S(1)}, f32[3,128,512]{2,1,0:T(8,128)S(1)}, u32[]{:S(2)}, u32[]{:S(2)}) collective-permute-start(f32[3,128,512]{2,1,0:T(8,128)S(1)} %get-tuple-element.18), channel_id=1, source_target_pairs={{0,64},{1,65},{2,66},{3,67},{4,68},{5,69},{6,70},{7,71},{8,72},{9,... | collective-permute-start | bytes 2359304 | tf_op jit(solution)/shard_map/ppermute | solution.py:462
  11.0 0.4 collective-permute-start.3
  11.5 2.2 %own_store.1 = (bf16[7,2,512,512]{3,2,1,0:T(8,128)(2,1)S(1)}, f32[1,512,512]{2,1,0:T(8,128)S(1)}) custom-call(s32[1]{0:T(128)} %bitcast.core_ref, s32[1,2,3]{2,1,0:T(2,128)S(1)} %copy-done.1, s32[1,2,3]{2,1,0:T(2,128)S(1)} %copy-done.2, f32[1,4]{1,0:T(1,128)S(1)} %copy-done.3, f32[1,2,3,512,512]{4,3,2,1,0:T(8,128)S(1)} %copy-done, f32[3,2,512,512]{3,2,1,0:T(8,128)} %b_ref.3, ...), custom_call_target="tpu_custom_call" | custom-call | bytes 1024 | tf_op jit(solution)/shard_map/own_store/pallas_call | solution.py:154
  13.7 1.9 %collective-permute-start.5 = (f32[1,512,512]{2,1,0:T(8,128)S(1)}, f32[1,512,512]{2,1,0:T(8,128)S(1)}, u32[]{:S(2)}, u32[]{:S(2)}) collective-permute-start(f32[1,512,512]{2,1,0:T(8,128)S(1)} %get-tuple-element.23), channel_id=1, source_target_pairs={{64,1},{65,2},{66,3},{67,4},{68,5},{69,6},{70,7},{71,8},{72,9},{73... | collective-permute-start | bytes 3145736 | tf_op jit(solution)/shard_map/ppermute | solution.py:462
  15.6 0.6 collective-permute-done.refs_0_
  16.2 1.4 %full_store.1 = (bf16[7,2,512,512]{3,2,1,0:T(8,128)(2,1)S(1)}, f32[1,512,512]{2,1,0:T(8,128)S(1)}) custom-call(s32[1]{0:T(128)} %bitcast.core_ref, f32[3,128,512]{2,1,0:T(8,128)S(1)} %collective-permute-done.refs_0_, f32[3,128,512]{2,1,0:T(8,128)S(1)} %collective-permute-done.1.refs_1_, ...), custom_call_target="tpu_custom_call", output_to_operand_aliasing={{0}: (5, {})} | custom-call | bytes 1024 | tf_op jit(solution)/shard_map/full_store/pallas_call | solution.py:196
  17.6 3.1 %collective-permute-start.8 = (f32[1,512,512]{2,1,0:T(8,128)S(1)}, f32[1,512,512]{2,1,0:T(8,128)S(1)}, u32[]{:S(2)}, u32[]{:S(2)}) collective-permute-start(f32[1,512,512]{2,1,0:T(8,128)S(1)} %get-tuple-element.24), channel_id=1, source_target_pairs={{64,1},{65,2},{66,3},{67,4},{68,5},{69,6},{70,7},{71,8},{72,9},{73... | collective-permute-start | bytes 3145736 | tf_op jit(solution)/shard_map/ppermute | solution.py:462
  20.7 7.3 %near_terms_0.2.p_ref = f32[2,512,512]{2,1,0:T(8,128)S(1)} custom-call(s32[1]{0:T(128)} %bitcast.core_ref, f32[3,2,512,512]{3,2,1,0:T(8,128)S(1)} %bitcast.3, f32[3,2,512,512]{3,2,1,0:T(8,128)S(1)} %bitcast.3, bf16[7,2,512,512]{3,2,1,0:T(8,128)(2,1)S(1)} %get-tuple-element.22.ta_ref.tb_ref.t_ref.refs_6_, ...), custom_call_target="tpu_custom_call" | custom-call | bytes 1024 | tf_op jit(solution)/shard_map/near_terms_0/pallas_call | solution.py:232
  28.0 1.9 %far_terms_0.2.d_ref = f32[1,512,512]{2,1,0:T(8,128)S(1)} custom-call(s32[1]{0:T(128)} %bitcast.core_ref, f32[2,512,512]{2,1,0:T(8,128)S(1)} %near_terms_0.2.p_ref, f32[1,512,512]{2,1,0:T(8,128)S(1)} %collective-permute-done.4.h_ref, bf16[7,2,512,512]{3,2,1,0:T(8,128)(2,1)S(1)} %get-tuple-element.22.ta_ref.tb_ref.t_ref.refs_6_), custom_call_target="tpu_custom_call" | custom-call | flops 18400000000 | bytes 1024 | tf_op jit(solution)/shard_map/far_terms_0/pallas_call | solution.py:256
  30.0 0.1 collective-permute-done.5.h_ref
  30.1 2.0 %far_pair.1.a_ref.refs_0_ = f32[2,512,512]{2,1,0:T(8,128)S(1)} custom-call(s32[1]{0:T(128)} %bitcast.core_ref, f32[2,512,512]{2,1,0:T(8,128)S(1)} %near_terms_0.2.p_ref, f32[1,512,512]{2,1,0:T(8,128)S(1)} %far_terms_0.2.d_ref, f32[1,512,512]{2,1,0:T(8,128)S(1)} %collective-permute-done.5.h_ref, ...), custom_call_target="tpu_custom_call" | custom-call | bytes 1024 | tf_op jit(solution)/shard_map/far_pair/pallas_call | solution.py:284
  32.1 4.6 %collective-permute-start.6 = (f32[2,512,512]{2,1,0:T(8,128)S(1)}, f32[2,512,512]{2,1,0:T(8,128)S(1)}, u32[]{:S(2)}, u32[]{:S(2)}) collective-permute-start(f32[2,512,512]{2,1,0:T(8,128)S(1)} %far_pair.1.a_ref.refs_0_), channel_id=1, source_target_pairs={{0,64},{1,65},{2,66},{3,67},{4,68},{5,69},{6,70},{7,71},{8,72},{9,... | collective-permute-start | bytes 6291464 | tf_op jit(solution)/shard_map/ppermute | solution.py:462
  36.7 2.1 %collective-permute-start.7 = (f32[2,512,512]{2,1,0:T(8,128)S(1)}, f32[2,512,512]{2,1,0:T(8,128)S(1)}, u32[]{:S(2)}, u32[]{:S(2)}) collective-permute-start(f32[2,512,512]{2,1,0:T(8,128)S(1)} %far_pair.1.a_ref.refs_0_), channel_id=1, source_target_pairs={{64,1},{65,2},{66,3},{67,4},{68,5},{69,6},{70,7},{71,8},{72,9},{73... | collective-permute-start | bytes 6291464 | tf_op jit(solution)/shard_map/ppermute | solution.py:462
  38.8 3.6 %near_terms_0.3.p_ref = f32[1,512,512]{2,1,0:T(8,128)S(1)} custom-call(s32[1]{0:T(128)} %bitcast.core_ref, f32[3,2,512,512]{3,2,1,0:T(8,128)S(1)} %bitcast.3, f32[3,2,512,512]{3,2,1,0:T(8,128)S(1)} %bitcast.3, bf16[7,2,512,512]{3,2,1,0:T(8,128)(2,1)S(1)} %get-tuple-element.22.ta_ref.tb_ref.t_ref.refs_6_, ...), custom_call_target="tpu_custom_call" | custom-call | bytes 1024 | tf_op jit(solution)/shard_map/near_terms_0/pallas_call | solution.py:232
  42.4 1.9 %far_terms_0.3.a_ref.refs_2_ = f32[1,512,512]{2,1,0:T(8,128)S(1)} custom-call(s32[1]{0:T(128)} %bitcast.core_ref, f32[1,512,512]{2,1,0:T(8,128)S(1)} %near_terms_0.3.p_ref, f32[1,512,512]{2,1,0:T(8,128)S(1)} %collective-permute-done.8.h_ref, bf16[7,2,512,512]{3,2,1,0:T(8,128)(2,1)S(1)} %get-tuple-element.22.ta_ref.tb_ref.t_ref.refs_6_, ...), custom_call_target="tpu_custom_call" | custom-call | bytes 1024 | tf_op jit(solution)/shard_map/far_terms_0/pallas_call | solution.py:256
  44.4 5.1 %collective-permute-start.9 = (f32[1,512,512]{2,1,0:T(8,128)S(1)}, f32[1,512,512]{2,1,0:T(8,128)S(1)}, u32[]{:S(2)}, u32[]{:S(2)}) collective-permute-start(f32[1,512,512]{2,1,0:T(8,128)S(1)} %far_terms_0.3.a_ref.refs_2_), channel_id=1, source_target_pairs={{0,64},{1,65},{2,66},{3,67},{4,68},{5,69},{6,70},{7,71},{8,72},{9,... | collective-permute-start | bytes 3145736 | tf_op jit(solution)/shard_map/ppermute | solution.py:462
  49.5 1.3 %collective-permute-start.14 = (f32[1,512,512]{2,1,0:T(8,128)S(1)}, f32[1,512,512]{2,1,0:T(8,128)S(1)}, u32[]{:S(2)}, u32[]{:S(2)}) collective-permute-start(f32[1,512,512]{2,1,0:T(8,128)S(1)} %far_terms_0.3.a_ref.refs_2_), channel_id=1, source_target_pairs={{2,65},{3,66},{4,67},{67,68},{6,69},{7,70},{8,71},{71,72},{10,73},... | collective-permute-start | bytes 3145736 | tf_op jit(solution)/shard_map/ppermute | solution.py:462
  50.8 1.9 %collective-permute-start.13 = (f32[1,512,512]{2,1,0:T(8,128)S(1)}, f32[1,512,512]{2,1,0:T(8,128)S(1)}, u32[]{:S(2)}, u32[]{:S(2)}) collective-permute-start(f32[1,512,512]{2,1,0:T(8,128)S(1)} %far_terms_0.3.a_ref.refs_2_), channel_id=1, source_target_pairs={{1,64},{64,65},{65,66},{66,67},{5,68},{68,69},{69,70},{70,71},{9,7... | collective-permute-start | bytes 3145736 | tf_op jit(solution)/shard_map/ppermute | solution.py:462
  52.7 7.3 %near_terms_1.2.refs_0_.p_ref = f32[2,512,512]{2,1,0:T(8,128)S(1)} custom-call(s32[1]{0:T(128)} %bitcast.core_ref, f32[2,512,512]{2,1,0:T(8,128)S(1)} %far_pair.1.a_ref.refs_0_, f32[2,512,512]{2,1,0:T(8,128)S(1)} %collective-permute-done.6.b_ref.refs_1_, bf16[7,2,512,512]{3,2,1,0:T(8,128)(2,1)S(1)} %get-tuple-element.22.ta_ref.tb_ref.t_ref.refs_6_, ...), custom_call_target="tpu_custom_call" | custom-call | bytes 1024 | tf_op jit(solution)/shard_map/near_terms_1/pallas_call | solution.py:232
  60.0 3.6 %near_terms_1.3.refs_0_.refs_3_ = f32[1,512,512]{2,1,0:T(8,128)S(1)} custom-call(s32[1]{0:T(128)} %bitcast.core_ref, f32[1,512,512]{2,1,0:T(8,128)S(1)} %far_terms_0.3.a_ref.refs_2_, f32[1,512,512]{2,1,0:T(8,128)S(1)} %collective-permute-done.9.b_ref.refs_3_, bf16[7,2,512,512]{3,2,1,0:T(8,128)(2,1)S(1)} %get-tuple-element.22.ta_ref.tb_ref.t_ref.refs_6_, ...), custom_call_target="tpu_custom_call" | custom-call | bytes 1024 | tf_op jit(solution)/shard_map/near_terms_1/pallas_call | solution.py:232
  63.6 0.7 collective-permute-done.7.h_ref
  64.3 3.9 %far_terms_1.1 = (f32[2,256,512]{2,1,0:T(8,128)S(1)}, f32[2,256,512]{2,1,0:T(8,128)S(1)}) custom-call(s32[1]{0:T(128)} %bitcast.core_ref, f32[2,512,512]{2,1,0:T(8,128)S(1)} %near_terms_1.2.refs_0_.p_ref, f32[2,512,512]{2,1,0:T(8,128)S(1)} %collective-permute-done.7.h_ref, bf16[7,2,512,512]{3,2,1,0:T(8,128)(2,1)S(1)} %get-tuple-element.22.ta_ref.tb_ref.t_ref.refs_6_, ...), custom_call_target="tpu_custom_call" | custom-call | bytes 1024 | tf_op jit(solution)/shard_map/far_terms_1/pallas_call | solution.py:256
  68.2 4.0 %collective-permute-start.10 = (f32[2,256,512]{2,1,0:T(8,128)S(1)}, f32[2,256,512]{2,1,0:T(8,128)S(1)}, u32[]{:S(2)}, u32[]{:S(2)}) collective-permute-start(f32[2,256,512]{2,1,0:T(8,128)S(1)} %get-tuple-element.25.refs_4_), channel_id=1, source_target_pairs={{0,64},{1,65},{2,66},{3,67},{4,68},{5,69},{6,70},{7,71},{8,72},{9,... | collective-permute-start | bytes 3145736 | tf_op jit(solution)/shard_map/ppermute | solution.py:462
  72.3 0.4 collective-permute-start.12
  72.7 1.5 %early_rows.1 = (f32[3,2,512,512]{3,2,1,0:T(8,128)}, f32[8,128]{1,0:T(8,128)S(1)}) custom-call(s32[1]{0:T(128)} %bitcast.core_ref, f32[2,512,512]{2,1,0:T(8,128)S(1)} %far_pair.1.a_ref.refs_0_, f32[2,512,512]{2,1,0:T(8,128)S(1)} %collective-permute-done.6.b_ref.refs_1_, f32[1,512,512]{2,1,0:T(8,128)S(1)} %far_terms_0.3.a_ref.refs_2_, ...), custom_call_target="tpu_custom_call" | custom-call | bytes 1024 | tf_op jit(solution)/shard_map/early_rows/pallas_call | solution.py:340
  74.2 1.1 %collective-permute-done.13.h_ref = f32[1,512,512]{2,1,0:T(8,128)S(1)} collective-permute-done((f32[1,512,512]{2,1,0:T(8,128)S(1)}, f32[1,512,512]{2,1,0:T(8,128)S(1)}, u32[]{:S(2)}, u32[]{:S(2)}) %collective-permute-start.13) | collective-permute-done | bytes 1048608 | tf_op jit(solution)/shard_map/ppermute | solution.py:462
  75.3 1.9 %sooner_term.1.refs_4_ = f32[512,512]{1,0:T(8,128)S(1)} custom-call(s32[1]{0:T(128)} %bitcast.core_ref, f32[1,512,512]{2,1,0:T(8,128)S(1)} %collective-permute-done.13.h_ref, bf16[7,2,512,512]{3,2,1,0:T(8,128)(2,1)S(1)} %get-tuple-element.22.ta_ref.tb_ref.t_ref.refs_6_, f32[8,128]{1,0:T(8,128)S(1)} %get-tuple-element.27.after_ref), custom_call_target="tpu_custom_call" | custom-call | bytes 1024 | tf_op jit(solution)/shard_map/sooner_term/pallas_call | solution.py:373
  77.2 1.6 %collective-permute-done.14.refs_5_ = f32[1,512,512]{2,1,0:T(8,128)S(1)} collective-permute-done((f32[1,512,512]{2,1,0:T(8,128)S(1)}, f32[1,512,512]{2,1,0:T(8,128)S(1)}, u32[]{:S(2)}, u32[]{:S(2)}) %collective-permute-start.14) | collective-permute-done | bytes 1048608 | tf_op jit(solution)/shard_map/ppermute | solution.py:462
  78.9 3.2 %last_rows.1 = f32[3,2,512,512]{3,2,1,0:T(8,128)} custom-call(s32[1]{0:T(128)} %bitcast.core_ref, f32[2,256,512]{2,1,0:T(8,128)S(1)} %collective-permute-done.10.refs_0_, f32[2,256,512]{2,1,0:T(8,128)S(1)} %collective-permute-done.11.refs_1_, f32[1,512,512]{2,1,0:T(8,128)S(1)} %collective-permute-done.12.refs_2_, ...), custom_call_target="tpu_custom_call", output_to_operand_aliasing={{}: (8, {})} | custom-call | bytes 1024 | tf_op jit(solution)/shard_map/last_rows/pallas_call | solution.py:428
  (26 shorter events, 0.3 us)
Async XLA Ops:
  0.0 5.6 %copy-start.3 = (f32[1,4]{1,0:T(1,128)S(1)}, f32[1,4]{1,0:T(1,128)}, u32[]{:S(2)}) copy-start(f32[1,4]{1,0:T(1,128)} %coef_ref.3) | copy-start | bytes 52
  0.0 5.7 %copy-start.2 = (s32[1,2,3]{2,1,0:T(2,128)S(1)}, s32[1,2,3]{2,1,0:T(2,128)}, u32[]{:S(2)}) copy-start(s32[1,2,3]{2,1,0:T(2,128)} %index_ref.3) | copy-start | bytes 76
  0.0 5.7 %copy-start.1 = (s32[1,2,3]{2,1,0:T(2,128)S(1)}, s32[1,2,3]{2,1,0:T(2,128)}, u32[]{:S(2)}) copy-start(s32[1,2,3]{2,1,0:T(2,128)} %live_ref.3) | copy-start | bytes 76
  0.0 5.7 %copy-start = (f32[1,2,3,512,512]{4,3,2,1,0:T(8,128)S(1)}, f32[1,2,3,512,512]{4,3,2,1,0:T(8,128)}, u32[]{:S(2)}) copy-start(f32[1,2,3,512,512]{4,3,2,1,0:T(8,128)} %t_ref.3) | copy-start | bytes 18874372
  1.4 26.6 %collective-permute-start.4 = (f32[1,512,512]{2,1,0:T(8,128)S(1)}, f32[1,512,512]{2,1,0:T(8,128)S(1)}, u32[]{:S(2)}, u32[]{:S(2)}) collective-permute-start(f32[1,512,512]{2,1,0:T(8,128)S(1)} %edge.1.after_ref), channel_id=1, source_target_pairs={{64,1},{65,2},{66,3},{67,4},{68,5},{69,6},{70,7},{71,8},{72,9},{73... | collective-permute-start | bytes 3145736 | tf_op jit(solution)/shard_map/ppermute | solution.py:462
  6.5 7.2 %collective-permute-start.1 = (f32[3,128,512]{2,1,0:T(8,128)S(1)}, f32[3,128,512]{2,1,0:T(8,128)S(1)}, u32[]{:S(2)}, u32[]{:S(2)}) collective-permute-start(f32[3,128,512]{2,1,0:T(8,128)S(1)} %get-tuple-element.18), channel_id=1, source_target_pairs={{0,64},{1,65},{2,66},{3,67},{4,68},{5,69},{6,70},{7,71},{8,72},{9,... | collective-permute-start | bytes 2359304 | tf_op jit(solution)/shard_map/ppermute | solution.py:462
  10.9 4.7 %collective-permute-start.2 = (f32[3,128,512]{2,1,0:T(8,128)S(1)}, f32[3,128,512]{2,1,0:T(8,128)S(1)}, u32[]{:S(2)}, u32[]{:S(2)}) collective-permute-start(f32[3,128,512]{2,1,0:T(8,128)S(1)} %get-tuple-element.19), channel_id=1, source_target_pairs={{0,64},{1,65},{2,66},{3,67},{4,68},{5,69},{6,70},{7,71},{8,72},{9,... | collective-permute-start | bytes 2359304 | tf_op jit(solution)/shard_map/ppermute | solution.py:462
  11.0 4.6 %collective-permute-start.3 = (f32[3,128,512]{2,1,0:T(8,128)S(1)}, f32[3,128,512]{2,1,0:T(8,128)S(1)}, u32[]{:S(2)}, u32[]{:S(2)}) collective-permute-start(f32[3,128,512]{2,1,0:T(8,128)S(1)} %get-tuple-element.20), channel_id=1, source_target_pairs={{0,64},{1,65},{2,66},{3,67},{4,68},{5,69},{6,70},{7,71},{8,72},{9,... | collective-permute-start | bytes 2359304 | tf_op jit(solution)/shard_map/ppermute | solution.py:462
  11.4 4.8 %collective-permute-start = (f32[3,128,512]{2,1,0:T(8,128)S(1)}, f32[3,128,512]{2,1,0:T(8,128)S(1)}, u32[]{:S(2)}, u32[]{:S(2)}) collective-permute-start(f32[3,128,512]{2,1,0:T(8,128)S(1)} %get-tuple-element.17.after_ref), channel_id=1, source_target_pairs={{0,64},{1,65},{2,66},{3,67},{4,68},{5,69},{6,70},{7,71},{8,72},{9,... | collective-permute-start | bytes 2359304 | tf_op jit(solution)/shard_map/ppermute | solution.py:462
  11.5 9.2 %slice-start = ((s8[6291456]{0:T(1024)(128)(4,1)}), s8[4194304]{0:T(1024)(128)(4,1)S(1)}, s32[]{:S(2)}) async-start(s8[6291456]{0:T(1024)(128)(4,1)} %bitcast.2), calls=%async_computation | async-start | bytes 8388608
  13.7 16.4 %collective-permute-start.5 = (f32[1,512,512]{2,1,0:T(8,128)S(1)}, f32[1,512,512]{2,1,0:T(8,128)S(1)}, u32[]{:S(2)}, u32[]{:S(2)}) collective-permute-start(f32[1,512,512]{2,1,0:T(8,128)S(1)} %get-tuple-element.23), channel_id=1, source_target_pairs={{64,1},{65,2},{66,3},{67,4},{68,5},{69,6},{70,7},{71,8},{72,9},{73... | collective-permute-start | bytes 3145736 | tf_op jit(solution)/shard_map/ppermute | solution.py:462
  16.2 4.5 %slice-start.1 = ((s8[6291456]{0:T(1024)(128)(4,1)}), s8[2097152]{0:T(1024)(128)(4,1)S(1)}, s32[]{:S(2)}) async-start(s8[6291456]{0:T(1024)(128)(4,1)} %bitcast.2), calls=%async_computation.1 | async-start | bytes 4194304
  17.6 24.9 %collective-permute-start.8 = (f32[1,512,512]{2,1,0:T(8,128)S(1)}, f32[1,512,512]{2,1,0:T(8,128)S(1)}, u32[]{:S(2)}, u32[]{:S(2)}) collective-permute-start(f32[1,512,512]{2,1,0:T(8,128)S(1)} %get-tuple-element.24), channel_id=1, source_target_pairs={{64,1},{65,2},{66,3},{67,4},{68,5},{69,6},{70,7},{71,8},{72,9},{73... | collective-permute-start | bytes 3145736 | tf_op jit(solution)/shard_map/ppermute | solution.py:462
  32.1 20.6 %collective-permute-start.6 = (f32[2,512,512]{2,1,0:T(8,128)S(1)}, f32[2,512,512]{2,1,0:T(8,128)S(1)}, u32[]{:S(2)}, u32[]{:S(2)}) collective-permute-start(f32[2,512,512]{2,1,0:T(8,128)S(1)} %far_pair.1.a_ref.refs_0_), channel_id=1, source_target_pairs={{0,64},{1,65},{2,66},{3,67},{4,68},{5,69},{6,70},{7,71},{8,72},{9,... | collective-permute-start | bytes 6291464 | tf_op jit(solution)/shard_map/ppermute | solution.py:462
  36.7 27.6 %collective-permute-start.7 = (f32[2,512,512]{2,1,0:T(8,128)S(1)}, f32[2,512,512]{2,1,0:T(8,128)S(1)}, u32[]{:S(2)}, u32[]{:S(2)}) collective-permute-start(f32[2,512,512]{2,1,0:T(8,128)S(1)} %far_pair.1.a_ref.refs_0_), channel_id=1, source_target_pairs={{64,1},{65,2},{66,3},{67,4},{68,5},{69,6},{70,7},{71,8},{72,9},{73... | collective-permute-start | bytes 6291464 | tf_op jit(solution)/shard_map/ppermute | solution.py:462
  44.4 15.6 %collective-permute-start.9 = (f32[1,512,512]{2,1,0:T(8,128)S(1)}, f32[1,512,512]{2,1,0:T(8,128)S(1)}, u32[]{:S(2)}, u32[]{:S(2)}) collective-permute-start(f32[1,512,512]{2,1,0:T(8,128)S(1)} %far_terms_0.3.a_ref.refs_2_), channel_id=1, source_target_pairs={{0,64},{1,65},{2,66},{3,67},{4,68},{5,69},{6,70},{7,71},{8,72},{9,... | collective-permute-start | bytes 3145736 | tf_op jit(solution)/shard_map/ppermute | solution.py:462
  49.5 29.3 %collective-permute-start.14 = (f32[1,512,512]{2,1,0:T(8,128)S(1)}, f32[1,512,512]{2,1,0:T(8,128)S(1)}, u32[]{:S(2)}, u32[]{:S(2)}) collective-permute-start(f32[1,512,512]{2,1,0:T(8,128)S(1)} %far_terms_0.3.a_ref.refs_2_), channel_id=1, source_target_pairs={{2,65},{3,66},{4,67},{67,68},{6,69},{7,70},{8,71},{71,72},{10,73},... | collective-permute-start | bytes 3145736 | tf_op jit(solution)/shard_map/ppermute | solution.py:462
  50.8 24.5 %collective-permute-start.13 = (f32[1,512,512]{2,1,0:T(8,128)S(1)}, f32[1,512,512]{2,1,0:T(8,128)S(1)}, u32[]{:S(2)}, u32[]{:S(2)}) collective-permute-start(f32[1,512,512]{2,1,0:T(8,128)S(1)} %far_terms_0.3.a_ref.refs_2_), channel_id=1, source_target_pairs={{1,64},{64,65},{65,66},{66,67},{5,68},{68,69},{69,70},{70,71},{9,7... | collective-permute-start | bytes 3145736 | tf_op jit(solution)/shard_map/ppermute | solution.py:462
  68.2 10.6 %collective-permute-start.10 = (f32[2,256,512]{2,1,0:T(8,128)S(1)}, f32[2,256,512]{2,1,0:T(8,128)S(1)}, u32[]{:S(2)}, u32[]{:S(2)}) collective-permute-start(f32[2,256,512]{2,1,0:T(8,128)S(1)} %get-tuple-element.25.refs_4_), channel_id=1, source_target_pairs={{0,64},{1,65},{2,66},{3,67},{4,68},{5,69},{6,70},{7,71},{8,72},{9,... | collective-permute-start | bytes 3145736 | tf_op jit(solution)/shard_map/ppermute | solution.py:462
  72.2 6.6 %collective-permute-start.11 = (f32[2,256,512]{2,1,0:T(8,128)S(1)}, f32[2,256,512]{2,1,0:T(8,128)S(1)}, u32[]{:S(2)}, u32[]{:S(2)}) collective-permute-start(f32[2,256,512]{2,1,0:T(8,128)S(1)} %get-tuple-element.26.refs_5_), channel_id=1, source_target_pairs={{0,64},{1,65},{2,66},{3,67},{4,68},{5,69},{6,70},{7,71},{8,72},{9,... | collective-permute-start | bytes 3145736 | tf_op jit(solution)/shard_map/ppermute | solution.py:462
  72.3 6.5 %collective-permute-start.12 = (f32[1,512,512]{2,1,0:T(8,128)S(1)}, f32[1,512,512]{2,1,0:T(8,128)S(1)}, u32[]{:S(2)}, u32[]{:S(2)}) collective-permute-start(f32[1,512,512]{2,1,0:T(8,128)S(1)} %near_terms_1.3.refs_0_.refs_3_), channel_id=1, source_target_pairs={{0,64},{1,65},{2,66},{3,67},{4,68},{5,69},{6,70},{7,71},{8,72},{9,... | collective-permute-start | bytes 3145736 | tf_op jit(solution)/shard_map/ppermute | solution.py:462
